TPU v7x, 128 devices: a whole 4x4x4 slice. The times are simulated.
128 devices in a mesh: sky: 16 (over y, x), tm: 8 (over z, core).
Axes of the slice: x: 4, y: 4, z: 4, core: 2. Of those that a mesh axis runs over, the one named last changes fastest.
Arguments:
- obs_source: int32 [524288], P(('sky', 'tm')), may hold values from 0 to 1023
- obs_knot: int32 [524288], P(('sky', 'tm')), may hold values from 0 to 4095, as said below
- obs_count: int32 [128], P(('sky', 'tm')), may hold values from 256 to 4096, as said below
- src_design: float32 [5, 524288], P(None, ('sky', 'tm')), may hold values from -3 to 3
- att_design: float32 [4, 524288], P(None, ('sky', 'tm')), may hold values from -6 to 6
- obs_phase: float32 [524288], P(('sky', 'tm')), may hold values from 0 to 1
- obs_value: float32 [524288], P(('sky', 'tm')), may hold values from -6 to 6
- src_prior: float32 [5, 16384], P(None, 'sky'), may hold values from 1 to 16
Outputs:
- att_solution: float32 [4, 8, 4096], P(None, 'tm', 'sky')
- att_residual: float32 [4, 8, 4096], P(None, 'tm', 'sky')
- source_solution: float32 [5, 16384], P(None, 'sky')
Inputs may be any that keep to these rules, and one draw needn't show every extreme that they name: Block b holds the 4096 observation slots o with o // 4096 = b; with i = b // 8 its sources are the sources i * 1024 + obs_source. With j = b % 8 for the observation's block b, its four spline knots are j * 4096 + obs_knot and the next three. In every block, each range of 256 values r * 256 to r * 256 + 255 of obs_knot holds exactly 256 of the block's slots. `obs_count`: each count is 4096 divided by 1, 2, 4, 8 or 16; the live slots of a block are its first ones; some block is full.
All inputs are finite; a program needn't handle non-finite values.
Results may differ from a plain program's by a relative error of at most 0.0001.
Values sent between devices are 32-bit elements; how exact they have to be, the bound alone decides.
No kernel may reach another device: no remote copies, remote signals or barrier semaphores. Data moves between devices by JAX's collectives and lax.ppermute only.
A program may use at most 64 MiB of HBM per device.

v0:
```python
import functools

import jax
import jax.numpy as jnp
from jax import lax
from jax.sharding import Mesh
from jax.sharding import PartitionSpec as P

ITERS = 2
SRC_DEV = 1024
KN_DEV = 256
SKY = ("sky_0", "sky_1")
TM = ("tm_0", "tm_1")
SKY_TM = ("sky_0", "sky_1", "tm_0", "tm_1")


damping = 0.5
entry_pairs = [(row_at, col_at) for row_at in range(5) for col_at in range(row_at + 1)]


def from_everyone(shard, axis):
    copies = jnp.broadcast_to(shard, (lax.axis_size(axis), *shard.shape))
    return lax.all_to_all(copies, axis, split_axis=0, concat_axis=0, tiled=True)


def taken_together(shard, axis):
    everything = from_everyone(shard, axis)
    return jnp.sum(everything, axis=0)


def in_order(tiles, dim):
    lengths = list(tiles.shape[1:])
    lengths[dim] *= tiles.shape[0]
    return jnp.moveaxis(tiles, 0, dim).reshape(lengths)


def gathered_copies(shard, axis, dim):
    tiles = from_everyone(shard, axis)
    return in_order(tiles, dim)


def shifted(value, axis, steps):
    count = lax.axis_size(axis)
    first, last = (max(0, -steps), min(count, count - steps))
    return lax.ppermute(value, axis, [(source, source + steps) for source in range(first, last)])


def cut_along(shard, dim, count):
    lengths = shard.shape
    tiles = shard.reshape(*lengths[:dim], count, lengths[dim] // count, *lengths[dim + 1 :])
    return jnp.moveaxis(tiles, dim, 0)


def sum_at_owner(shard, axis, dim):
    count = lax.axis_size(axis)
    tiles = lax.all_to_all(cut_along(shard, dim, count), axis, 0, 0, tiled=True)
    return jnp.sum(tiles, axis=0)


def over_axes(shard, axes):
    return functools.reduce(lax.psum, axes, shard)


def spline_taps(phase):
    squared = phase * phase
    cubed = squared * phase
    rest = 1.0 - phase
    return (
        rest * rest * rest / 6.0,
        (3.0 * cubed - 6.0 * squared + 4.0) / 6.0,
        (-3.0 * cubed + 3.0 * squared + 3.0 * phase + 1.0) / 6.0,
        cubed / 6.0,
    )


def factorize(normal):
    factor = {}
    for row_at in range(5):
        for col_at in range(row_at + 1):
            running = normal[row_at, col_at]
            for inner_at in range(col_at):
                running = running - factor[row_at, inner_at] * factor[col_at, inner_at]
            if row_at == col_at:
                factor[row_at, row_at] = jnp.sqrt(running)
            else:
                factor[row_at, col_at] = running / factor[col_at, col_at]
    return factor


def chol_solve(factor, target):
    forward = []
    for row_at in range(5):
        running = target[row_at]
        for inner_at in range(row_at):
            running = running - factor[row_at, inner_at] * forward[inner_at]
        forward.append(running / factor[row_at, row_at])
    result = [None] * 5
    for row_at in reversed(range(5)):
        running = forward[row_at]
        for inner_at in range(row_at + 1, 5):
            running = running - factor[inner_at, row_at] * result[inner_at]
        result[row_at] = running / factor[row_at, row_at]
    return jnp.stack(result)


def source_total(source, rows, count):
    return jnp.zeros((rows.shape[0], count), jnp.float32).at[:, source].add(rows)


def knot_values(padded, knot, design, tap_weights):
    summed = jnp.zeros(knot.shape, jnp.float32)
    for tap_at in range(4):
        picked = jnp.take(padded, knot + tap_at, axis=1)
        summed = summed + tap_weights[tap_at] * jnp.sum(design * picked, axis=0)
    return summed


def knot_total(knot, design, tap_weights, weight_vec, extent):
    summed = jnp.zeros((design.shape[0], extent + 3), jnp.float32)
    for tap_at in range(4):
        summed = summed.at[:, knot + tap_at].add(design * (tap_weights[tap_at] * weight_vec))
    return summed


def eliminate(factor, source, design, values_obs, source_sums):
    solved = chol_solve(factor, [source_sums[row_at] for row_at in range(5)])
    fitted = jnp.sum(design * jnp.take(solved, source, axis=1), axis=0)
    return values_obs - fitted


def shards(
    obs_source, obs_knot, obs_count, src_design, att_design, obs_phase, obs_value, src_prior
):
    sky_count = lax.axis_size(SKY)
    seg_knots = KN_DEV * sky_count
    slot_count = obs_source.shape[0]
    live_mask = (jnp.arange(slot_count, dtype=jnp.int32) < obs_count[0]).astype(jnp.float32)
    src_rows = src_design * live_mask
    att_rows = att_design * live_mask
    observed = obs_value * live_mask
    tap_weights = spline_taps(obs_phase)
    products = jnp.stack(
        [src_rows[row_at] * src_rows[col_at] for row_at, col_at in entry_pairs]
        + [src_rows[row_at] * observed for row_at in range(5)]
    )
    sums = taken_together(source_total(obs_source, products, SRC_DEV), TM)
    normal = {}
    for entry_at, pair in enumerate(entry_pairs):
        normal[pair] = sums[entry_at] + (src_prior[pair[0]] if pair[0] == pair[1] else 0.0)
    factor = factorize(normal)

    def source_part(values_obs):
        return taken_together(source_total(obs_source, src_rows * values_obs, SRC_DEV), TM)

    def along_knots(field):
        segment = gathered_copies(field, SKY, 1)
        next_edge = shifted(segment[:, :3], TM, -1)
        padded = jnp.concatenate([segment, next_edge], axis=1)
        return knot_values(padded, obs_knot, att_rows, tap_weights)

    def back_to_knots(cleaned):
        summed = knot_total(obs_knot, att_rows, tap_weights, cleaned, seg_knots)
        overflow = shifted(summed[:, seg_knots:], TM, 1)
        partial_value = summed[:, :seg_knots].at[:, :3].add(overflow)
        return sum_at_owner(partial_value, SKY, 1)

    def norm_sum(partial_value):
        return over_axes(partial_value, SKY_TM)

    cleaned = eliminate(factor, obs_source, src_rows, observed, sums[15:])
    residual = back_to_knots(cleaned)
    solution = jnp.zeros_like(residual)
    direction = residual
    norm_now = norm_sum(jnp.sum(residual * residual))
    for repeat in range(ITERS):
        image_obs = along_knots(direction)
        cleaned = eliminate(factor, obs_source, src_rows, image_obs, source_part(image_obs))
        mapped = back_to_knots(cleaned) + damping * direction
        alpha_step = norm_now / over_axes(jnp.sum(direction * mapped), SKY_TM)
        solution = solution + alpha_step * direction
        residual = residual - alpha_step * mapped
        norm_next = norm_sum(jnp.sum(residual * residual))
        direction = residual + norm_next / norm_now * direction
        norm_now = norm_next
    fitted = observed - along_knots(solution)
    source_solution = chol_solve(factor, [row for row in source_part(fitted)])
    return (solution[:, None, :], residual[:, None, :], source_solution)


def solution(mesh):
    torus = Mesh(mesh.devices.reshape(4, 4, 4, 2), ("sky_0", "sky_1", "tm_0", "tm_1"))
    placed = (
        P(SKY_TM),
        P(SKY_TM),
        P(SKY_TM),
        P(None, SKY_TM),
        P(None, SKY_TM),
        P(SKY_TM),
        P(SKY_TM),
        P(None, SKY),
    )
    return jax.shard_map(
        shards,
        mesh=torus,
        in_specs=placed,
        out_specs=(P(None, TM, SKY), P(None, TM, SKY), P(None, SKY)),
        check_vma=False,
    )
```

profile of v0, /device:TPU:0, one launch (start us, length us, event | category | flops | bytes accessed | tf_op | source)
XLA Modules:
  0.0 978.2 jit_solution(17283222722693372817)
XLA Ops:
  5.1 22.5 %scatter_custom_fusion = f32[20,1024]{0,1:T(8,128)S(1)} fusion(s32[4096]{0:T(1024)S(1)} %get-tuple-element.177, f32[4096,20]{1,0:T(8,128)S(1)} %copy.249, f32[]{:T(128)} %constant.111.clone.1), kind=kCustom, calls=%fused_computation.113 | custom fusion | flops 81920 | bytes 81924 | tf_op jit(solution)/shard_map/scatter-add | solution.py:107
  48.1 14.1 %gather_fusion = f32[4096,5]{1,0:T(8,128)} fusion(f32[5,1024]{0,1:T(8,128)S(1)} %copy.252, s32[4096]{0:T(1024)S(1)} %get-tuple-element.176), kind=kCustom, calls=%fused_computation.clone | custom fusion | bytes 180224 | tf_op jit(solution)/shard_map/jit(_take)/gather | solution.py:127
  64.5 26.4 %scatter_custom_fusion.1 = f32[4,4099]{0,1:T(8,128)} fusion(s32[4096]{0:T(1024)S(1)} %get-tuple-element.172, f32[]{:T(128)} %constant.111.clone.1, f32[4096]{0:T(1024)S(1)} %get-tuple-element.163, f32[4,4096]{0,1:T(8,128)S(1)} %copy.248, f32[4096]{0:T(1024)S(1)} %fusion.83), kind=kCustom, calls=%fused_computation.77 | custom fusion | flops 49152 | bytes 2195508 | tf_op jit(solution)/shard_map/scatter-add | solution.py:121
  90.9 27.8 %scatter_custom_fusion.2 = f32[4,4099]{0,1:T(8,128)} fusion(f32[4,4099]{0,1:T(8,128)} %scatter_custom_fusion.1, s32[4096]{0:T(1024)S(1)} %get-tuple-element.170, f32[4096]{0:T(1024)S(1)} %get-tuple-element.162, f32[4,4096]{0,1:T(8,128)S(1)} %copy.248, f32[4096]{0:T(1024)S(1)} %fusion.83), kind=kCustom, calls=%fused_computation.75 | custom fusion | flops 49152 | bytes 2195504 | tf_op jit(solution)/shard_map/scatter-add | solution.py:121
  118.7 28.0 %scatter_custom_fusion.3 = f32[4,4099]{0,1:T(8,128)} fusion(f32[4,4099]{0,1:T(8,128)} %scatter_custom_fusion.2, s32[4096]{0:T(1024)S(1)} %get-tuple-element.171, f32[4096]{0:T(1024)S(1)} %get-tuple-element.161, f32[4,4096]{0,1:T(8,128)S(1)} %copy.248, f32[4096]{0:T(1024)S(1)} %fusion.83), kind=kCustom, calls=%fused_computation.73 | custom fusion | flops 49152 | bytes 2195504 | tf_op jit(solution)/shard_map/scatter-add | solution.py:121
  146.6 27.8 %scatter_custom_fusion.4 = f32[4,4099]{0,1:T(8,128)} fusion(f32[4,4099]{0,1:T(8,128)} %scatter_custom_fusion.3, s32[4096]{0:T(1024)S(1)} %get-tuple-element.175, f32[4096]{0:T(1024)S(1)} %get-tuple-element.110, f32[4,4096]{0,1:T(8,128)S(1)} %copy.248, f32[4096]{0:T(1024)S(1)} %fusion.83), kind=kCustom, calls=%fused_computation.71 | custom fusion | flops 49152 | bytes 2195504 | tf_op jit(solution)/shard_map/scatter-add | solution.py:121
  185.3 14.5 %all_to_all.50 = f32[16,4,256]{2,1,0:T(4,128)S(1)} all-to-all(f32[16,4,256]{2,1,0:T(4,128)S(1)} %bitcast.178), channel_id=1, replica_groups=mesh['sky_0'=4,'sky_1'=4,'tm_0'=4,'tm_1'=2] {'sky_0','sky_1'}, dimensions={0} | all-to-all | bytes 131072 | tf_op jit(solution)/shard_map/all_to_all | solution.py:56
  216.7 15.8 %gather_fusion.4 = f32[4096,4]{1,0:T(8,128)} fusion(f32[4,4099]{0,1:T(8,128)} %copy.257, s32[4096]{0:T(1024)S(1)} %get-tuple-element.168), kind=kCustom, calls=%fused_computation.6.clone | custom fusion | bytes 147456 | tf_op jit(solution)/shard_map/jit(_take)/gather | solution.py:113
  232.5 15.8 %gather_fusion.3 = f32[4096,4]{1,0:T(8,128)} fusion(f32[4,4099]{0,1:T(8,128)} %copy.257, s32[4096]{0:T(1024)S(1)} %get-tuple-element.173), kind=kCustom, calls=%fused_computation.5.clone | custom fusion | bytes 147456 | tf_op jit(solution)/shard_map/jit(_take)/gather | solution.py:113
  248.2 15.8 %gather_fusion.2 = f32[4096,4]{1,0:T(8,128)} fusion(f32[4,4099]{0,1:T(8,128)} %copy.257, s32[4096]{0:T(1024)S(1)} %get-tuple-element.174), kind=kCustom, calls=%fused_computation.4.clone | custom fusion | bytes 147456 | tf_op jit(solution)/shard_map/jit(_take)/gather | solution.py:113
  264.0 15.8 %gather_fusion.1 = f32[4096,4]{1,0:T(8,128)} fusion(f32[4,4099]{0,1:T(8,128)} %copy.257, s32[4096]{0:T(1024)S(1)} %get-tuple-element.169), kind=kCustom, calls=%fused_computation.1.clone | custom fusion | bytes 147456 | tf_op jit(solution)/shard_map/jit(_take)/gather | solution.py:113
  290.8 22.8 %scatter_custom_fusion.5 = f32[5,1024]{0,1:T(8,128)S(1)} fusion(s32[4096]{0:T(1024)S(1)} %get-tuple-element.177, f32[4096,5]{1,0:T(8,128)} %copy.261, f32[]{:T(128)} %constant.111.clone.1), kind=kCustom, calls=%fused_computation.111 | custom fusion | flops 20480 | bytes 20992 | tf_op jit(solution)/shard_map/scatter-add | solution.py:107
  328.7 14.1 %gather_fusion.5 = f32[4096,5]{1,0:T(8,128)} fusion(f32[5,1024]{0,1:T(8,128)S(1)} %copy.264, s32[4096]{0:T(1024)S(1)} %get-tuple-element.176), kind=kCustom, calls=%fused_computation.2.clone | custom fusion | bytes 180224 | tf_op jit(solution)/shard_map/jit(_take)/gather | solution.py:127
  345.2 26.5 %scatter_custom_fusion.6 = f32[4,4099]{0,1:T(8,128)} fusion(s32[4096]{0:T(1024)S(1)} %get-tuple-element.172, f32[]{:T(128)} %constant.111.clone.1, f32[4096]{0:T(1024)S(1)} %get-tuple-element.160, f32[4,4096]{0,1:T(8,128)S(1)} %copy.248, f32[4096]{0:T(1024)S(1)} %fusion.83), kind=kCustom, calls=%fused_computation.61 | custom fusion | flops 49152 | bytes 2195508 | tf_op jit(solution)/shard_map/scatter-add | solution.py:121
  371.7 27.8 %scatter_custom_fusion.7 = f32[4,4099]{0,1:T(8,128)} fusion(f32[4,4099]{0,1:T(8,128)} %scatter_custom_fusion.6, s32[4096]{0:T(1024)S(1)} %get-tuple-element.170, f32[4096]{0:T(1024)S(1)} %get-tuple-element.159, f32[4,4096]{0,1:T(8,128)S(1)} %copy.248, f32[4096]{0:T(1024)S(1)} %fusion.83), kind=kCustom, calls=%fused_computation.59 | custom fusion | flops 49152 | bytes 2195504 | tf_op jit(solution)/shard_map/scatter-add | solution.py:121
  399.5 27.8 %scatter_custom_fusion.8 = f32[4,4099]{0,1:T(8,128)} fusion(f32[4,4099]{0,1:T(8,128)} %scatter_custom_fusion.7, s32[4096]{0:T(1024)S(1)} %get-tuple-element.171, f32[4096]{0:T(1024)S(1)} %get-tuple-element.158, f32[4,4096]{0,1:T(8,128)S(1)} %copy.248, f32[4096]{0:T(1024)S(1)} %fusion.83), kind=kCustom, calls=%fused_computation.57 | custom fusion | flops 49152 | bytes 2195504 | tf_op jit(solution)/shard_map/scatter-add | solution.py:121
  427.3 27.8 %scatter_custom_fusion.9 = f32[4,4099]{0,1:T(8,128)} fusion(f32[4,4099]{0,1:T(8,128)} %scatter_custom_fusion.8, s32[4096]{0:T(1024)S(1)} %get-tuple-element.175, f32[4096]{0:T(1024)S(1)} %get-tuple-element.99, f32[4,4096]{0,1:T(8,128)S(1)} %copy.248, f32[4096]{0:T(1024)S(1)} %fusion.83), kind=kCustom, calls=%fused_computation.55 | custom fusion | flops 49152 | bytes 2195504 | tf_op jit(solution)/shard_map/scatter-add | solution.py:121
  561.3 15.8 %gather_fusion.9 = f32[4096,4]{1,0:T(8,128)} fusion(f32[4,4099]{0,1:T(8,128)} %copy.274, s32[4096]{0:T(1024)S(1)} %get-tuple-element.168), kind=kCustom, calls=%fused_computation.10.clone | custom fusion | bytes 147456 | tf_op jit(solution)/shard_map/jit(_take)/gather | solution.py:113
  577.1 15.8 %gather_fusion.8 = f32[4096,4]{1,0:T(8,128)} fusion(f32[4,4099]{0,1:T(8,128)} %copy.274, s32[4096]{0:T(1024)S(1)} %get-tuple-element.173), kind=kCustom, calls=%fused_computation.9.clone | custom fusion | bytes 147456 | tf_op jit(solution)/shard_map/jit(_take)/gather | solution.py:113
  592.8 15.8 %gather_fusion.7 = f32[4096,4]{1,0:T(8,128)} fusion(f32[4,4099]{0,1:T(8,128)} %copy.274, s32[4096]{0:T(1024)S(1)} %get-tuple-element.174), kind=kCustom, calls=%fused_computation.8.clone | custom fusion | bytes 147456 | tf_op jit(solution)/shard_map/jit(_take)/gather | solution.py:113
  608.6 15.8 %gather_fusion.6 = f32[4096,4]{1,0:T(8,128)} fusion(f32[4,4099]{0,1:T(8,128)} %copy.274, s32[4096]{0:T(1024)S(1)} %get-tuple-element.169), kind=kCustom, calls=%fused_computation.7.clone | custom fusion | bytes 147456 | tf_op jit(solution)/shard_map/jit(_take)/gather | solution.py:113
  635.4 22.8 %scatter_custom_fusion.10 = f32[5,1024]{0,1:T(8,128)S(1)} fusion(s32[4096]{0:T(1024)S(1)} %get-tuple-element.177, f32[4096,5]{1,0:T(8,128)} %copy.278, f32[]{:T(128)} %constant.111.clone.1), kind=kCustom, calls=%fused_computation.109 | custom fusion | flops 20480 | bytes 20992 | tf_op jit(solution)/shard_map/scatter-add | solution.py:107
  670.8 14.1 %gather_fusion.10 = f32[4096,5]{1,0:T(8,128)} fusion(f32[5,1024]{0,1:T(8,128)S(1)} %copy.281, s32[4096]{0:T(1024)S(1)} %get-tuple-element.176), kind=kCustom, calls=%fused_computation.3.clone | custom fusion | bytes 180224 | tf_op jit(solution)/shard_map/jit(_take)/gather | solution.py:127
  687.2 26.4 %scatter_custom_fusion.11 = f32[4,4099]{0,1:T(8,128)} fusion(s32[4096]{0:T(1024)S(1)} %get-tuple-element.172, f32[]{:T(128)} %constant.111.clone.1, f32[4096]{0:T(1024)S(1)} %get-tuple-element.157, f32[4,4096]{0,1:T(8,128)S(1)} %copy.248, f32[4096]{0:T(1024)S(1)} %fusion.83), kind=kCustom, calls=%fused_computation.45 | custom fusion | flops 49152 | bytes 2195508 | tf_op jit(solution)/shard_map/scatter-add | solution.py:121
  713.5 27.8 %scatter_custom_fusion.12 = f32[4,4099]{0,1:T(8,128)} fusion(f32[4,4099]{0,1:T(8,128)} %scatter_custom_fusion.11, s32[4096]{0:T(1024)S(1)} %get-tuple-element.170, f32[4096]{0:T(1024)S(1)} %get-tuple-element.156, f32[4,4096]{0,1:T(8,128)S(1)} %copy.248, f32[4096]{0:T(1024)S(1)} %fusion.83), kind=kCustom, calls=%fused_computation.43 | custom fusion | flops 49152 | bytes 2195504 | tf_op jit(solution)/shard_map/scatter-add | solution.py:121
  741.3 28.0 %scatter_custom_fusion.13 = f32[4,4099]{0,1:T(8,128)} fusion(f32[4,4099]{0,1:T(8,128)} %scatter_custom_fusion.12, s32[4096]{0:T(1024)S(1)} %get-tuple-element.171, f32[4096]{0:T(1024)S(1)} %get-tuple-element.155, f32[4,4096]{0,1:T(8,128)S(1)} %copy.248, f32[4096]{0:T(1024)S(1)} %fusion.83), kind=kCustom, calls=%fused_computation.41 | custom fusion | flops 49152 | bytes 2195504 | tf_op jit(solution)/shard_map/scatter-add | solution.py:121
  769.3 27.8 %scatter_custom_fusion.14 = f32[4,4099]{0,1:T(8,128)} fusion(f32[4,4099]{0,1:T(8,128)} %scatter_custom_fusion.13, s32[4096]{0:T(1024)S(1)} %get-tuple-element.175, f32[4096]{0:T(1024)S(1)} %get-tuple-element.88, f32[4,4096]{0,1:T(8,128)S(1)} %copy.248, f32[4096]{0:T(1024)S(1)} %fusion.83), kind=kCustom, calls=%fused_computation.39 | custom fusion | flops 49152 | bytes 2195504 | tf_op jit(solution)/shard_map/scatter-add | solution.py:121
  870.1 15.8 %gather_fusion.14 = f32[4096,4]{1,0:T(8,128)} fusion(f32[4,4099]{0,1:T(8,128)} %copy.289, s32[4096]{0:T(1024)S(1)} %get-tuple-element.168), kind=kCustom, calls=%fused_computation.14.clone | custom fusion | bytes 147456 | tf_op jit(solution)/shard_map/jit(_take)/gather | solution.py:113
  885.9 15.8 %gather_fusion.13 = f32[4096,4]{1,0:T(8,128)} fusion(f32[4,4099]{0,1:T(8,128)} %copy.289, s32[4096]{0:T(1024)S(1)} %get-tuple-element.173), kind=kCustom, calls=%fused_computation.13.clone | custom fusion | bytes 147456 | tf_op jit(solution)/shard_map/jit(_take)/gather | solution.py:113
  901.7 15.8 %gather_fusion.12 = f32[4096,4]{1,0:T(8,128)} fusion(f32[4,4099]{0,1:T(8,128)} %copy.289, s32[4096]{0:T(1024)S(1)} %get-tuple-element.174), kind=kCustom, calls=%fused_computation.12.clone | custom fusion | bytes 147456 | tf_op jit(solution)/shard_map/jit(_take)/gather | solution.py:113
  917.5 15.8 %gather_fusion.11 = f32[4096,4]{1,0:T(8,128)} fusion(f32[4,4099]{0,1:T(8,128)} %copy.289, s32[4096]{0:T(1024)S(1)} %get-tuple-element.169), kind=kCustom, calls=%fused_computation.11.clone | custom fusion | bytes 147456 | tf_op jit(solution)/shard_map/jit(_take)/gather | solution.py:113
  942.9 22.5 %scatter_custom_fusion.15 = f32[5,1024]{0,1:T(8,128)S(1)} fusion(s32[4096]{0:T(1024)S(1)} %get-tuple-element.177, f32[4096,5]{1,0:T(8,128)S(1)} %copy.293, f32[]{:T(128)} %constant.111.clone.1), kind=kCustom, calls=%fused_computation.107 | custom fusion | flops 20480 | bytes 20484 | tf_op jit(solution)/shard_map/scatter-add | solution.py:107
  (156 shorter events, 305.9 us)
Async XLA Ops:
  5.0 29.2 %copy-start.3 = (f32[4,4096]{1,0:T(4,128)S(1)}, f32[4,4096]{1,0:T(4,128)}, u32[]{:S(2)}) copy-start(f32[4,4096]{1,0:T(4,128)} %param.22) | copy-start | bytes 196612
  27.7 7.8 copy-start.4
  28.7 6.8 copy-start.5
  28.7 18.7 %copy-start.6 = (f32[5,1024]{1,0:T(8,128)S(1)}, f32[5,1024]{1,0:T(8,128)}, u32[]{:S(2)}) copy-start(f32[5,1024]{1,0:T(8,128)} %param.25) | copy-start | bytes 61444
  28.7 18.7 %all-to-all-start = ((f32[8,20,1024]{2,1,0:T(8,128)}), f32[8,20,1024]{2,1,0:T(8,128)S(1)}, u32[]{:S(2)}, u32[]{:S(2)}) async-start(f32[8,20,1024]{2,1,0:T(8,128)} %broadcast_in_dim.47), calls=%async_computation | async-start | bytes 1572864 | tf_op jit(solution)/shard_map/all_to_all | solution.py:23
  47.6 16.7 %copy-start = (f32[5,4096]{1,0:T(8,128)S(1)}, f32[5,4096]{1,0:T(8,128)}, u32[]{:S(2)}) copy-start(f32[5,4096]{1,0:T(8,128)} %param.21) | copy-start | bytes 245764
  47.8 16.6 %copy-start.1 = (f32[4096]{0:T(1024)S(1)}, f32[4096]{0:T(1024)}, u32[]{:S(2)}) copy-start(f32[4096]{0:T(1024)} %param.23) | copy-start | bytes 49156
  47.8 16.6 %copy-start.2 = (f32[4096]{0:T(1024)S(1)}, f32[4096]{0:T(1024)}, u32[]{:S(2)}) copy-start(f32[4096]{0:T(1024)} %param.24) | copy-start | bytes 49156
  178.2 2.3 collective-permute-start
  200.5 11.1 %all-to-all-start.2 = ((f32[16,4,256]{2,1,0:T(4,128)}), f32[16,4,256]{2,1,0:T(4,128)S(1)}, u32[]{:S(2)}, u32[]{:S(2)}) async-start(f32[16,4,256]{2,1,0:T(4,128)} %broadcast_in_dim.51), calls=%async_computation.2 | async-start | bytes 131072 | tf_op jit(solution)/shard_map/all_to_all | solution.py:23
  211.6 3.0 collective-permute-start.1
  314.5 13.8 %all-to-all-start.3 = ((f32[8,5,1024]{2,1,0:T(8,128)}), f32[8,5,1024]{2,1,0:T(8,128)S(1)}, u32[]{:S(2)}, u32[]{:S(2)}) async-start(f32[8,5,1024]{2,1,0:T(8,128)} %broadcast_in_dim.52), calls=%async_computation.3 | async-start | bytes 524288 | tf_op jit(solution)/shard_map/all_to_all | solution.py:23
  458.9 2.2 collective-permute-start.2
  466.5 11.3 %all-to-all-start.4 = ((f32[16,4,256]{2,1,0:T(4,128)}), f32[16,4,256]{2,1,0:T(4,128)S(1)}, u32[]{:S(2)}, u32[]{:S(2)}) async-start(f32[16,4,256]{2,1,0:T(4,128)} %bitcast.33), calls=%async_computation.4 | async-start | bytes 131072 | tf_op jit(solution)/shard_map/all_to_all | solution.py:56
  556.2 3.0 collective-permute-start.3
  800.8 2.2 collective-permute-start.4
  865.1 3.0 collective-permute-start.5
  966.3 10.9 %all-to-all-start.9 = ((f32[8,5,1024]{2,1,0:T(8,128)}), f32[8,5,1024]{2,1,0:T(8,128)S(1)}, u32[]{:S(2)}, u32[]{:S(2)}) async-start(f32[8,5,1024]{2,1,0:T(8,128)} %broadcast_in_dim.99), calls=%async_computation.9 | async-start | bytes 524288 | tf_op jit(solution)/shard_map/all_to_all | solution.py:23
where the time goes:
time: 990 us; the launch traced here: 978 us
  other arithmetic  458 us (46%)
  local copies, waits for them, and re-layouts  279 us (28%)
  blocking collectives  156 us (16%)
  waiting for transfers between devices  47.4 us (5%)
  starting transfers between devices  30.7 us (3%)
    scatter-add x12, other arithmetic, knot_total(): summed.at[:, knot + tap_at].add(design * (tap_weights[tap_at] * weight_vec))  330 us
    gather x12, local copies, waits for them, and re-layouts, knot_values(): picked = jnp.take(padded, knot + tap_at, axis=1)  189 us
    psum x12, blocking collectives, over_axes(): return functools.reduce(lax.psum, axes, shard)  98.1 us
    scatter-add x4, other arithmetic, source_total(): jnp.zeros((rows.shape[0], count), jnp.float32).at[:, source].add(rows)  90.5 us
    gather x6, local copies, waits for them, and re-layouts, eliminate(): fitted = jnp.sum(design * jnp.take(solved, source, axis=1), axis=0)  48.9 us
    all_to_all x4, waiting for transfers between devices, from_everyone(): return lax.all_to_all(copies, axis, split_axis=0, concat_axis=0, tiled=True)  33 us
    all_to_all x3, blocking collectives, from_everyone(): return lax.all_to_all(copies, axis, split_axis=0, concat_axis=0, tiled=True)  32.7 us
    reduce_sum x3, other arithmetic, knot_values(): summed = summed + tap_weights[tap_at] * jnp.sum(design * picked, axis=0)  26.8 us
  transfers between devices with their start and end apart: 11, of which 11 were waited for; matrix products, arithmetic and copies ran while one was open for 0% of the time, Pallas kernels for 0%

commit v1 on v0

v1 whole, which is shorter than its diff:
```python
import functools

import jax
import jax.numpy as jnp
from jax import lax
from jax.experimental import pallas as pl
from jax.experimental.pallas import tpu as pltpu
from jax.sharding import Mesh
from jax.sharding import PartitionSpec as P

SKY = ("sky_0", "sky_1")
TM = ("tm_0", "tm_1")
SKY_TM = ("sky_0", "sky_1", "tm_0", "tm_1")

OBS_DEV = 4096
CHUNK = 1024
damping = 0.5
entry_pairs = [(row_at, col_at) for row_at in range(5) for col_at in range(row_at + 1)]


f32 = jnp.float32
bf16 = jnp.bfloat16


def split_rows(value):
    first = value.astype(bf16)
    rest = value - first.astype(f32)
    second = rest.astype(bf16)
    third = (rest - second.astype(f32)).astype(bf16)
    return jnp.concatenate([first, second, third], axis=0)


def join_rows(stacked):
    rows = stacked.shape[0] // 3
    return stacked[:rows] + (stacked[rows : 2 * rows] + stacked[2 * rows :])


def dot_nt(left, right):
    return lax.dot_general(left, right, (((1,), (1,)), ((), ())), preferred_element_type=f32)


def dot_nn(left, right):
    return lax.dot_general(left, right, (((1,), (0,)), ((), ())), preferred_element_type=f32)


def chunks():
    return [slice(start, start + CHUNK) for start in range(0, OBS_DEV, CHUNK)]


def four(refs):
    own, one, two, three = (ref[...] for ref in refs)
    return (own + two) + (one + three)


def lanes_from(start, rows):
    return lax.broadcasted_iota(jnp.int32, (rows, CHUNK), 1) + start


def source_kernel(count_ref, source_ref, g_ref, y_ref, hot_ref, spread_ref, y_live_ref, sums_ref):
    total = jnp.zeros((480, 128), f32)
    for at in chunks():
        live = lanes_from(at.start, 1) < count_ref[0]
        source = source_ref[:, at]
        hot = jnp.where(lax.broadcasted_iota(jnp.int32, (128, CHUNK), 0) == (source & 127), 1.0, 0.0).astype(bf16)
        hot_ref[:, at] = hot
        mark = jnp.where(live, source >> 7, -1)
        chosen = jnp.where(lax.broadcasted_iota(jnp.int32, (8, CHUNK), 0) == mark, 1.0, 0.0)
        g = [g_ref[j : j + 1, at] for j in range(5)]
        y = y_ref[:, at]
        y_live_ref[:, at] = jnp.where(live, y, 0.0)
        spread = [chosen * g[j] for j in range(5)]
        for j in range(5):
            spread_ref[8 * j : 8 * j + 8, at] = spread[j]
        rows = [spread[r] * g[c] for r, c in entry_pairs] + [spread[j] * y for j in range(5)]
        total = total + dot_nt(split_rows(jnp.concatenate(rows, axis=0)), hot)
    sums_ref[...] = join_rows(total)


def knot_kernel(count_ref, last_ref, knot_ref, h_ref, phase_ref, hot_ref, spread_ref):
    upper = lax.broadcasted_iota(jnp.int32, (8, CHUNK), 0) >> 2
    for at in chunks():
        live = lanes_from(at.start, 1) < count_ref[0]
        knot = knot_ref[:, at]
        high = knot >> 4
        hot_ref[:, at] = jnp.where(lax.broadcasted_iota(jnp.int32, (256, CHUNK), 0) == high, 1.0, 0.0).astype(bf16)
        h = jnp.where(live, h_ref[:, at], 0.0)
        h = jnp.concatenate([h, h], axis=0)
        phase = phase_ref[:, at]
        squared = phase * phase
        cubed = squared * phase
        rest = 1.0 - phase
        taps = (
            rest * rest * rest / 6.0,
            (3.0 * cubed - 6.0 * squared + 4.0) / 6.0,
            (-3.0 * cubed + 3.0 * squared + 3.0 * phase + 1.0) / 6.0,
            cubed / 6.0,
        )
        taps = [jnp.broadcast_to(tap, (8, CHUNK)) for tap in taps]
        ahead = upper - (knot & 15)
        kept = jnp.where((high == 255) & (last_ref[0] == 1), 0.0, 1.0)
        for q in range(10):
            gap = ahead + 2 * q
            weight = jnp.where(gap == 0, taps[0], 0.0)
            for m in range(1, 4):
                weight = jnp.where(gap == m, taps[m], weight)
            if q >= 8:
                weight = weight * kept
            spread_ref[8 * q : 8 * q + 8, at] = weight * h


def tile(value, at):
    return value[8 * at : 8 * at + 8]


def factor_of(value):
    return {pair: tile(value, at) for at, pair in enumerate(entry_pairs)}


def factorize(normal):
    factor = {}
    for row_at in range(5):
        for col_at in range(row_at + 1):
            running = normal[row_at, col_at]
            for inner_at in range(col_at):
                running = running - factor[row_at, inner_at] * factor[col_at, inner_at]
            if row_at == col_at:
                factor[row_at, row_at] = jnp.sqrt(running)
            else:
                factor[row_at, col_at] = running / factor[col_at, col_at]
    return factor


def chol_solve(factor, target):
    forward = []
    for row_at in range(5):
        running = target[row_at]
        for inner_at in range(row_at):
            running = running - factor[row_at, inner_at] * forward[inner_at]
        forward.append(running / factor[row_at, row_at])
    result = [None] * 5
    for row_at in reversed(range(5)):
        running = forward[row_at]
        for inner_at in range(row_at + 1, 5):
            running = running - factor[inner_at, row_at] * result[inner_at]
        result[row_at] = running / factor[row_at, row_at]
    return result


def eliminate_and_spread(solved, values_ref, source_hot_ref, source_spread_ref, knot_hot_ref, knot_spread_ref):
    solved = split_rows(jnp.concatenate(solved, axis=0))
    total = jnp.zeros((240, 256), f32)
    for at in chunks():
        picked = join_rows(dot_nn(solved, source_hot_ref[:, at]))
        fitted = jnp.sum(picked * source_spread_ref[:, at], axis=0, keepdims=True)
        cleaned = values_ref[:, at] - fitted
        total = total + dot_nt(split_rows(knot_spread_ref[:, at] * cleaned), knot_hot_ref[:, at])
    return join_rows(total)


def put_knots(total, energy, knots_ref, edge_ref):
    knots_ref[0:72] = total[0:72]
    if energy is None:
        tail = total[76:80]
    else:
        tail = jnp.concatenate([energy[0:4], energy[4:8]], axis=1)
    knots_ref[72:80] = jnp.concatenate([total[72:76], tail], axis=0)
    lane = lax.broadcasted_iota(jnp.int32, (16, 128), 1)
    edge_ref[...] = jnp.where(lane == 127, total[64:80, 128:256], jnp.where(lane == 0, total[0:16, 0:128], 0.0))


def first_kernel(own, one, two, three, prior_ref, y_ref, source_hot, source_spread, knot_hot, knot_spread, knots_ref, edge_ref, factor_ref, rhs_ref):
    sums = four((own, one, two, three))
    normal = factor_of(sums)
    for j in range(5):
        prior = jnp.concatenate([prior_ref[j : j + 1, 128 * a : 128 * a + 128] for a in range(8)], axis=0)
        normal[j, j] = normal[j, j] + prior
    factor = factorize(normal)
    for at, pair in enumerate(entry_pairs):
        factor_ref[8 * at : 8 * at + 8] = factor[pair]
    rhs_ref[...] = sums[120:160]
    solved = chol_solve(factor, [tile(sums, 15 + j) for j in range(5)])
    total = eliminate_and_spread(solved, y_ref, source_hot, source_spread, knot_hot, knot_spread)
    put_knots(total, None, knots_ref, edge_ref)


def back_kernel(energy_at, own, one, two, three, factor_ref, values_ref, source_hot, source_spread, knot_hot, knot_spread, knots_ref, edge_ref, sums_ref):
    sums = four((own, one, two, three))
    sums_ref[...] = sums
    target = [tile(sums, j) for j in range(5)]
    solved = chol_solve(factor_of(factor_ref[...]), target)
    energy = tile(sums, energy_at)
    for j in range(5):
        energy = energy - target[j] * solved[j]
    total = eliminate_and_spread(solved, values_ref, source_hot, source_spread, knot_hot, knot_spread)
    put_knots(total, energy, knots_ref, edge_ref)


def assembled(knots):
    lane = lax.broadcasted_iota(jnp.int32, (16, 256), 1)
    row = lax.broadcasted_iota(jnp.int32, (16, 256), 0)
    beyond = jnp.where(row < 12, knots[64:80], 0.0)
    low = knots[0:16] + jnp.where(lane == 0, 0.0, jnp.concatenate([beyond[:, 255:256], beyond[:, 0:255]], axis=1))
    following = jnp.concatenate([low[:, 1:256], low[:, 0:1]], axis=1)
    high = jnp.where(row < 12, jnp.where(lane == 255, beyond, following), 0.0)
    return jnp.concatenate([low, knots[16:64], high], axis=0)


def energy_of(knots):
    return jnp.sum(knots[76:80])


def folded(left, right):
    product = left[0:64] * right[0:64]
    product = product[:, 0:128] + product[:, 128:256]
    return functools.reduce(jnp.add, [tile(product, at) for at in range(8)])


def gather_and_sum(field, source_hot_ref, source_spread_ref, knot_hot_ref, knot_spread_ref, image_ref):
    parts = split_rows(field)
    total = jnp.zeros((120, 128), f32)
    square = jnp.zeros((1, 128), f32)
    for at in chunks():
        picked = join_rows(dot_nn(parts, knot_hot_ref[:, at]))
        image = jnp.sum(picked * knot_spread_ref[:, at], axis=0, keepdims=True)
        image_ref[:, at] = image
        for start in range(0, CHUNK, 128):
            piece = image[:, start : start + 128]
            square = square + piece * piece
        total = total + dot_nt(split_rows(source_spread_ref[:, at] * image), source_hot_ref[:, at])
    return join_rows(total), jnp.concatenate([square, jnp.zeros((7, 128), f32)], axis=0)


def start_kernel(own, one, two, three, source_hot, source_spread, knot_hot, knot_spread, sums_ref, image_ref, field_ref):
    residual = assembled(four((own, one, two, three)))
    field_ref[...] = residual
    sums, square = gather_and_sum(residual, source_hot, source_spread, knot_hot, knot_spread, image_ref)
    sums_ref[...] = jnp.concatenate([sums, square, folded(residual, residual)], axis=0)


def next_kernel(own, one, two, three, residual_ref, before_ref, source_hot, source_spread, knot_hot, knot_spread, sums_ref, image_ref, mapped_ref, field_ref, scalar_ref):
    knots = four((own, one, two, three))
    direction = residual_ref[...]
    mapped = assembled(knots) + damping * direction
    norm_now = jnp.sum(before_ref[48:56])
    product = energy_of(knots) + damping * norm_now
    residual = direction - (norm_now / product) * mapped
    mapped_ref[...] = mapped
    field_ref[...] = residual
    scalar_ref[...] = jnp.zeros((8, 128), f32) + product
    sums, square = gather_and_sum(residual, source_hot, source_spread, knot_hot, knot_spread, image_ref)
    sums_ref[...] = jnp.concatenate([sums, square, folded(residual, residual), folded(residual, mapped)], axis=0)


def last_kernel(place_ref, own, one, two, three, start_ref, mapped_ref, residual_ref, scalar_ref, before_ref, after_ref, factor_ref, rhs_ref, solution_ref, left_ref, source_ref):
    knots = four((own, one, two, three))
    residual = residual_ref[0:64]
    image = assembled(knots)[0:64] + damping * residual
    norm_first = jnp.sum(before_ref[48:56])
    product_first = jnp.max(scalar_ref[...])
    alpha_first = norm_first / product_first
    norm_now = jnp.sum(after_ref[48:56])
    crossed = jnp.sum(after_ref[56:64])
    beta = norm_now / norm_first
    product = energy_of(knots) + damping * norm_now + beta * (2.0 * crossed + beta * product_first)
    alpha = norm_now / product
    from_start = alpha_first + alpha * beta
    solution = from_start * start_ref[0:64] + alpha * residual
    left = residual - alpha * (image + beta * mapped_ref[0:64])
    both = split_rows(jnp.concatenate([solution, left], axis=0))
    row = lax.broadcasted_iota(jnp.int32, (256, 256), 0)
    lane = lax.broadcasted_iota(jnp.int32, (256, 256), 1)
    chosen = jnp.where(row == place_ref[0] * 16 + (lane >> 4), 1.0, 0.0).astype(bf16)
    picked = join_rows(dot_nn(both, chosen))
    low = lax.broadcasted_iota(jnp.int32, (8, 256), 1) & 15
    upper = lax.broadcasted_iota(jnp.int32, (8, 256), 0) >> 2
    for at, ref in enumerate((solution_ref, left_ref)):
        own_rows = jnp.zeros((8, 256), f32)
        for q in range(8):
            own_rows = jnp.where(low == upper + 2 * q, tile(picked, 8 * at + q), own_rows)
        ref[...] = own_rows[0:4] + own_rows[4:8]
    target = [tile(rhs_ref, j) - from_start * tile(before_ref, j) - alpha * tile(after_ref, j) for j in range(5)]
    solved = chol_solve(factor_of(factor_ref[...]), target)
    for j in range(5):
        for a in range(8):
            source_ref[j : j + 1, 128 * a : 128 * a + 128] = solved[j][a : a + 1]


VMEM = pl.BlockSpec(memory_space=pltpu.VMEM)
SMEM = pl.BlockSpec(memory_space=pltpu.SMEM)


def call(kernel, name, outs, *operands, scalars=0):
    specs = [SMEM] * scalars + [VMEM] * (len(operands) - scalars)
    shapes = [jax.ShapeDtypeStruct(shape, dtype) for shape, dtype in outs]
    return pl.pallas_call(
        kernel,
        out_shape=shapes,
        in_specs=specs,
        out_specs=[VMEM] * len(outs),
        compiler_params=pltpu.CompilerParams(vmem_limit_bytes=32 * 1024 * 1024),
        name=name,
    )(*operands)


def ring_parts(value, axis):
    count = lax.axis_size(axis)
    return [value] + [
        lax.ppermute(value, axis, [(at, (at + step) % count) for at in range(count)]) for step in (1, 2, 3)
    ]


def tm_parts(value):
    value = value + lax.ppermute(value, "tm_1", [(0, 1), (1, 0)])
    return ring_parts(value, "tm_0")


def sky_parts(knots, edge):
    count = lax.axis_size(TM)
    at = lax.axis_index(TM)
    twin = lax.ppermute(edge, "tm_1", [(0, 1), (1, 0)])
    swaps = [(low, low + 1) for low in range(1, count - 1, 2)]
    other = lax.ppermute(edge, TM, swaps + [(high, low) for low, high in swaps])
    odd = at % 2 == 1
    earlier = jnp.where(odd, twin, other)[:, 127]
    later = jnp.where(odd, other, twin)[:, 0]
    row = lax.broadcasted_iota(jnp.int32, (80, 256), 0)
    lane = lax.broadcasted_iota(jnp.int32, (80, 256), 1)
    keep_low = jnp.arange(16) < 12
    keep_high = (jnp.arange(16) < 12) & (at < count - 1)
    low = jnp.concatenate([jnp.where(keep_low, earlier, 0.0), jnp.zeros((64,), f32)])
    high = jnp.concatenate([jnp.zeros((64,), f32), jnp.where(keep_high, later, 0.0)])
    knots = knots + jnp.where(lane == 0, low[:, None], 0.0) + jnp.where(lane == 255, high[:, None], 0.0)
    own, one, two, three = ring_parts(knots, "sky_1")
    return ring_parts((own + two) + (one + three), "sky_0")


def shards(obs_source, obs_knot, obs_count, src_design, att_design, obs_phase, obs_value, src_prior):
    last = (lax.axis_index(TM) == lax.axis_size(TM) - 1).astype(jnp.int32).reshape(1)
    place = lax.axis_index(SKY).astype(jnp.int32).reshape(1)
    line = lambda value: value.reshape(1, OBS_DEV)
    source_hot, source_spread, y_live, sums = call(
        source_kernel,
        "source_sums",
        [((128, OBS_DEV), bf16), ((40, OBS_DEV), f32), ((1, OBS_DEV), f32), ((160, 128), f32)],
        obs_count, line(obs_source), src_design, line(obs_value),
        scalars=1,
    )
    parts = tm_parts(sums)
    knot_hot, knot_spread = call(
        knot_kernel,
        "knot_spread",
        [((256, OBS_DEV), bf16), ((80, OBS_DEV), f32)],
        obs_count, last, line(obs_knot), att_design, line(obs_phase),
        scalars=2,
    )
    maps = (source_hot, source_spread, knot_hot, knot_spread)
    knots_out = [((80, 256), f32), ((16, 128), f32)]
    knots, edge, factor, rhs = call(
        first_kernel, "first", knots_out + [((120, 128), f32), ((40, 128), f32)], *parts, src_prior, y_live, *maps
    )
    parts = sky_parts(knots, edge)
    sums, image, start = call(
        start_kernel, "start", [((56, 128), f32), ((1, OBS_DEV), f32), ((80, 256), f32)], *parts, *maps
    )
    parts = tm_parts(sums)
    knots, edge, before = call(
        functools.partial(back_kernel, 5), "back", knots_out + [((56, 128), f32)], *parts, factor, image, *maps
    )
    parts = sky_parts(knots, edge)
    sums, image, mapped, residual, scalar = call(
        next_kernel,
        "next",
        [((64, 128), f32), ((1, OBS_DEV), f32), ((80, 256), f32), ((80, 256), f32), ((8, 128), f32)],
        *parts, start, before, *maps,
    )
    parts = tm_parts(sums)
    knots, edge, after = call(
        functools.partial(back_kernel, 5), "back_again", knots_out + [((64, 128), f32)], *parts, factor, image, *maps
    )
    parts = sky_parts(knots, edge)
    solution, left, source_solution = call(
        last_kernel,
        "last",
        [((4, 256), f32), ((4, 256), f32), ((5, 1024), f32)],
        place, *parts, start, mapped, residual, scalar, before, after, factor, rhs,
        scalars=1,
    )
    return (solution[:, None, :], left[:, None, :], source_solution)


def solution(mesh):
    torus = Mesh(mesh.devices.reshape(4, 4, 4, 2), SKY_TM)
    placed = (
        P(SKY_TM),
        P(SKY_TM),
        P(SKY_TM),
        P(None, SKY_TM),
        P(None, SKY_TM),
        P(SKY_TM),
        P(SKY_TM),
        P(None, SKY),
    )
    return jax.shard_map(
        shards,
        mesh=torus,
        in_specs=placed,
        out_specs=(P(None, TM, SKY), P(None, TM, SKY), P(None, SKY)),
        check_vma=False,
    )
```

time: 990 us -> 131 us (0.13); the launches traced: 978 us -> 130 us
  other arithmetic: 458 us -> 3.69 us
  local copies, waits for them, and re-layouts: 279 us -> 19.5 us
  blocking collectives: 156 us -> 0 us
  Pallas kernels: 0 us -> 12.3 us
  starting transfers between devices: 30.7 us -> 41.9 us
    scatter-add x16 -> x0, other arithmetic: 420 us -> none  [the longest x12 330 us: knot_total(): summed.at[:, knot + tap_at].add(design * (tap_weights[tap_at] * weight_vec))]
    gather x18 -> x0, local copies, waits for them, and re-layouts: 238 us -> none  [the longest x12 189 us: knot_values(): picked = jnp.take(padded, knot + tap_at, axis=1)]
    psum x12 -> x0, blocking collectives: 98.1 us -> none  [over_axes(): return functools.reduce(lax.psum, axes, shard)]
    all_to_all x5 -> x0, blocking collectives: 58.3 us -> none  [the longest x3 32.7 us: from_everyone(): return lax.all_to_all(copies, axis, split_axis=0, concat_axis=0, tiled=True)]
    ppermute x6 -> x36, waiting for transfers between devices: 7.25 us -> 50.7 us  [the longest x27 44.7 us: ring_parts(): lax.ppermute(value, axis, [(at, (at + step) % count) for at in range(coun...]
    all_to_all x5 -> x0, waiting for transfers between devices: 40.2 us -> none  [the longest x4 33 us: from_everyone(): return lax.all_to_all(copies, axis, split_axis=0, concat_axis=0, tiled=True)]
    ppermute x6 -> x36, starting transfers between devices: 8.5 us -> 41.9 us  [the longest x27 36.3 us: ring_parts(): lax.ppermute(value, axis, [(at, (at + step) % count) for at in range(coun...]
    reduce_sum x17 -> x0, other arithmetic: 29.6 us -> none  [the longest x3 26.8 us: knot_values(): summed = summed + tap_weights[tap_at] * jnp.sum(design * picked, axis=0)]
  transfers between devices with their start and end apart: 11 -> 36, of which waited for: 11 -> 31; matrix products, arithmetic and copies ran while one was open for 0% -> 0% of each run, Pallas kernels for 0% -> 1%
where the time goes in v1:
time: 131 us; the launch traced here: 130 us
  waiting for transfers between devices  50.7 us (39%)
  starting transfers between devices  41.9 us (32%)
  local copies, waits for them, and re-layouts  19.5 us (15%)
  Pallas kernels  12.3 us (9%)
  other arithmetic  3.69 us (3%)
  between operations  1.63 us (1%)
    ppermute x27, waiting for transfers between devices, ring_parts(): lax.ppermute(value, axis, [(at, (at + step) % count) for at in range(coun...  44.7 us
    ppermute x27, starting transfers between devices, ring_parts(): lax.ppermute(value, axis, [(at, (at + step) % count) for at in range(coun...  36.3 us
    unnamed x62, local copies, waits for them, and re-layouts  19.3 us
    pallas_call x8, Pallas kernels, call(): pl.pallas_call(kernel, out_shape=shapes, in_specs=specs, out_specs=[VMEM]...  12.3 us
    ppermute x3, waiting for transfers between devices, tm_parts(): value = value + lax.ppermute(value, 'tm_1', [(0, 1), (1, 0)])  3.66 us
    ppermute x3, starting transfers between devices, sky_parts(): twin = lax.ppermute(edge, 'tm_1', [(0, 1), (1, 0)])  2.91 us
  transfers between devices with their start and end apart: 36, of which 31 were waited for; matrix products, arithmetic and copies ran while one was open for 0% of the time, Pallas kernels for 1%

profile of v1, /device:TPU:0, one launch (start us, length us, event | category | flops | bytes accessed | tf_op | source)
XLA Modules:
  0.0 129.8 jit_solution(3670275912533478232)
XLA Ops:
  3.6 1.3 %source_sums.1 = (bf16[128,4096]{1,0:T(8,128)(2,1)S(1)}, f32[40,4096]{1,0:T(8,128)S(1)}, f32[1,4096]{1,0:T(1,128)S(1)}, f32[160,128]{1,0:T(8,128)S(1)}) custom-call(s32[1]{0:T(128)S(6)} %copy.15.count_ref, s32[1,4096]{1,0:T(1,128)S(1)} %bitcast.8, f32[5,4096]{1,0:T(8,128)S(1)} %copy-done.8, f32[1,4096]{1,0:T(1,128)S(1)} %bitcast.9), custom_call_target="tpu_custom_call" | custom-call | tf_op jit(solution)/shard_map/source_sums/pallas_call | solution.py:295
  8.1 4.2 %collective-permute-start.3 = (f32[160,128]{1,0:T(8,128)S(1)}, f32[160,128]{1,0:T(8,128)}, u32[]{:S(2)}, u32[]{:S(2)}) collective-permute-start(f32[160,128]{1,0:T(8,128)S(1)} %add.82.own), channel_id=1, source_target_pairs={{0,6},{2,0},{4,2},{6,4},{1,7},{3,1},{5,3},{7,5},{8,14},{10,8},{12,... | collective-permute-start | bytes 245768 | tf_op jit(solution)/shard_map/ppermute | solution.py:308
  16.8 2.2 %collective-permute-done.2.two = f32[160,128]{1,0:T(8,128)} collective-permute-done((f32[160,128]{1,0:T(8,128)S(1)}, f32[160,128]{1,0:T(8,128)}, u32[]{:S(2)}, u32[]{:S(2)}) %collective-permute-start.2) | collective-permute-done | bytes 81952 | tf_op jit(solution)/shard_map/ppermute | solution.py:308
  24.3 3.3 %first.1 = (f32[80,256]{1,0:T(8,128)S(1)}, f32[16,128]{1,0:T(8,128)}, f32[120,128]{1,0:T(8,128)S(1)}, f32[40,128]{1,0:T(8,128)S(1)}) custom-call(f32[160,128]{1,0:T(8,128)S(1)} %copy-done.7, f32[160,128]{1,0:T(8,128)} %collective-permute-done.1.one, f32[160,128]{1,0:T(8,128)} %collective-permute-done.2.two, f32[160,128]{1,0:T(8,128)} %collective-permute-done.3.three, ...), custom_call_target="tpu_custom_call" | custom-call | tf_op jit(solution)/shard_map/first/pallas_call | solution.py:295
  32.9 1.6 %collective-permute-start.7 = (f32[80,256]{1,0:T(8,128)S(1)}, f32[80,256]{1,0:T(8,128)S(1)}, u32[]{:S(2)}, u32[]{:S(2)}) collective-permute-start(f32[80,256]{1,0:T(8,128)S(1)} %select_add_fusion.2), channel_id=1, source_target_pairs={{0,8},{8,16},{16,24},{24,0},{1,9},{9,17},{17,25},{25,1},{2,10},{10... | collective-permute-start | bytes 245768 | tf_op jit(solution)/shard_map/ppermute | solution.py:308
  34.5 1.7 %collective-permute-start.8 = (f32[80,256]{1,0:T(8,128)S(1)}, f32[80,256]{1,0:T(8,128)S(1)}, u32[]{:S(2)}, u32[]{:S(2)}) collective-permute-start(f32[80,256]{1,0:T(8,128)S(1)} %select_add_fusion.2), channel_id=1, source_target_pairs={{0,24},{8,0},{16,8},{24,16},{1,25},{9,1},{17,9},{25,17},{2,26},{10... | collective-permute-start | bytes 245768 | tf_op jit(solution)/shard_map/ppermute | solution.py:308
  36.2 1.8 %collective-permute-start.6 = (f32[80,256]{1,0:T(8,128)S(1)}, f32[80,256]{1,0:T(8,128)S(1)}, u32[]{:S(2)}, u32[]{:S(2)}) collective-permute-start(f32[80,256]{1,0:T(8,128)S(1)} %select_add_fusion.2), channel_id=1, source_target_pairs={{0,16},{8,24},{16,0},{24,8},{1,17},{9,25},{17,1},{25,9},{2,18},{10... | collective-permute-start | bytes 245768 | tf_op jit(solution)/shard_map/ppermute | solution.py:308
  38.9 3.6 %collective-permute-done.6 = f32[80,256]{1,0:T(8,128)S(1)} collective-permute-done((f32[80,256]{1,0:T(8,128)S(1)}, f32[80,256]{1,0:T(8,128)S(1)}, u32[]{:S(2)}, u32[]{:S(2)}) %collective-permute-start.6) | collective-permute-done | bytes 81952 | tf_op jit(solution)/shard_map/ppermute | solution.py:308
  43.3 3.1 %collective-permute-start.11 = (f32[80,256]{1,0:T(8,128)S(1)}, f32[80,256]{1,0:T(8,128)S(1)}, u32[]{:S(2)}, u32[]{:S(2)}) collective-permute-start(f32[80,256]{1,0:T(8,128)S(1)} %add_add_fusion.2.own), channel_id=1, source_target_pairs={{0,96},{32,0},{64,32},{96,64},{1,97},{33,1},{65,33},{97,65},{2,98}... | collective-permute-start | bytes 245768 | tf_op jit(solution)/shard_map/ppermute | solution.py:308
  47.9 2.4 %collective-permute-done.11.three = f32[80,256]{1,0:T(8,128)S(1)} collective-permute-done((f32[80,256]{1,0:T(8,128)S(1)}, f32[80,256]{1,0:T(8,128)S(1)}, u32[]{:S(2)}, u32[]{:S(2)}) %collective-permute-start.11) | collective-permute-done | bytes 81952 | tf_op jit(solution)/shard_map/ppermute | solution.py:308
  50.3 2.8 %collective-permute-done.10.two = f32[80,256]{1,0:T(8,128)S(1)} collective-permute-done((f32[80,256]{1,0:T(8,128)S(1)}, f32[80,256]{1,0:T(8,128)S(1)}, u32[]{:S(2)}, u32[]{:S(2)}) %collective-permute-start.10) | collective-permute-done | bytes 81952 | tf_op jit(solution)/shard_map/ppermute | solution.py:308
  58.9 2.0 %collective-permute-start.15 = (f32[56,128]{1,0:T(8,128)S(1)}, f32[56,128]{1,0:T(8,128)S(1)}, u32[]{:S(2)}, u32[]{:S(2)}) collective-permute-start(f32[56,128]{1,0:T(8,128)S(1)} %add.90.own), channel_id=1, source_target_pairs={{0,6},{2,0},{4,2},{6,4},{1,7},{3,1},{5,3},{7,5},{8,14},{10,8},{12,... | collective-permute-start | bytes 86024 | tf_op jit(solution)/shard_map/ppermute | solution.py:308
  62.7 3.5 %collective-permute-done.14.two = f32[56,128]{1,0:T(8,128)S(1)} collective-permute-done((f32[56,128]{1,0:T(8,128)S(1)}, f32[56,128]{1,0:T(8,128)S(1)}, u32[]{:S(2)}, u32[]{:S(2)}) %collective-permute-start.14) | collective-permute-done | bytes 28704 | tf_op jit(solution)/shard_map/ppermute | solution.py:308
  66.8 1.7 %back.1 = (f32[80,256]{1,0:T(8,128)S(1)}, f32[16,128]{1,0:T(8,128)S(1)}, f32[56,128]{1,0:T(8,128)S(1)}) custom-call(f32[56,128]{1,0:T(8,128)S(1)} %add.90.own, f32[56,128]{1,0:T(8,128)S(1)} %collective-permute-done.13.one, f32[56,128]{1,0:T(8,128)S(1)} %collective-permute-done.14.two, f32[56,128]{1,0:T(8,128)S(1)} %collective-permute-done.15.three, ...), custom_call_target="tpu_custom_call" | custom-call | tf_op jit(solution)/shard_map/back/pallas_call | solution.py:295
  72.2 2.6 %collective-permute-start.20 = (f32[80,256]{1,0:T(8,128)S(1)}, f32[80,256]{1,0:T(8,128)S(1)}, u32[]{:S(2)}, u32[]{:S(2)}) collective-permute-start(f32[80,256]{1,0:T(8,128)S(1)} %select_add_fusion.1), channel_id=1, source_target_pairs={{0,24},{8,0},{16,8},{24,16},{1,25},{9,1},{17,9},{25,17},{2,26},{10... | collective-permute-start | bytes 245768 | tf_op jit(solution)/shard_map/ppermute | solution.py:308
  75.4 2.6 %collective-permute-done.19 = f32[80,256]{1,0:T(8,128)S(1)} collective-permute-done((f32[80,256]{1,0:T(8,128)S(1)}, f32[80,256]{1,0:T(8,128)S(1)}, u32[]{:S(2)}, u32[]{:S(2)}) %collective-permute-start.19) | collective-permute-done | bytes 81952 | tf_op jit(solution)/shard_map/ppermute | solution.py:308
  77.9 1.3 collective-permute-done.20
  79.2 1.9 %collective-permute-done.18 = f32[80,256]{1,0:T(8,128)S(1)} collective-permute-done((f32[80,256]{1,0:T(8,128)S(1)}, f32[80,256]{1,0:T(8,128)S(1)}, u32[]{:S(2)}, u32[]{:S(2)}) %collective-permute-start.18) | collective-permute-done | bytes 81952 | tf_op jit(solution)/shard_map/ppermute | solution.py:308
  82.6 1.3 %collective-permute-start.21 = (f32[80,256]{1,0:T(8,128)S(1)}, f32[80,256]{1,0:T(8,128)S(1)}, u32[]{:S(2)}, u32[]{:S(2)}) collective-permute-start(f32[80,256]{1,0:T(8,128)S(1)} %add_add_fusion.1.own), channel_id=1, source_target_pairs={{0,32},{32,64},{64,96},{96,0},{1,33},{33,65},{65,97},{97,1},{2,34}... | collective-permute-start | bytes 245768 | tf_op jit(solution)/shard_map/ppermute | solution.py:308
  83.9 2.4 %collective-permute-done.23.three = f32[80,256]{1,0:T(8,128)S(1)} collective-permute-done((f32[80,256]{1,0:T(8,128)S(1)}, f32[80,256]{1,0:T(8,128)S(1)}, u32[]{:S(2)}, u32[]{:S(2)}) %collective-permute-start.23) | collective-permute-done | bytes 81952 | tf_op jit(solution)/shard_map/ppermute | solution.py:308
  86.3 2.1 %collective-permute-done.22.two = f32[80,256]{1,0:T(8,128)S(1)} collective-permute-done((f32[80,256]{1,0:T(8,128)S(1)}, f32[80,256]{1,0:T(8,128)S(1)}, u32[]{:S(2)}, u32[]{:S(2)}) %collective-permute-start.22) | collective-permute-done | bytes 81952 | tf_op jit(solution)/shard_map/ppermute | solution.py:308
  91.6 2.5 %collective-permute-start.27 = (f32[64,128]{1,0:T(8,128)S(1)}, f32[64,128]{1,0:T(8,128)S(1)}, u32[]{:S(2)}, u32[]{:S(2)}) collective-permute-start(f32[64,128]{1,0:T(8,128)S(1)} %add.96.own), channel_id=1, source_target_pairs={{0,6},{2,0},{4,2},{6,4},{1,7},{3,1},{5,3},{7,5},{8,14},{10,8},{12,... | collective-permute-start | bytes 98312 | tf_op jit(solution)/shard_map/ppermute | solution.py:308
  95.1 1.3 %collective-permute-start.25 = (f32[64,128]{1,0:T(8,128)S(1)}, f32[64,128]{1,0:T(8,128)S(1)}, u32[]{:S(2)}, u32[]{:S(2)}) collective-permute-start(f32[64,128]{1,0:T(8,128)S(1)} %add.96.own), channel_id=1, source_target_pairs={{0,2},{2,4},{4,6},{6,0},{1,3},{3,5},{5,7},{7,1},{8,10},{10,12},{12... | collective-permute-start | bytes 98312 | tf_op jit(solution)/shard_map/ppermute | solution.py:308
  96.4 3.1 %collective-permute-done.26.two = f32[64,128]{1,0:T(8,128)S(1)} collective-permute-done((f32[64,128]{1,0:T(8,128)S(1)}, f32[64,128]{1,0:T(8,128)S(1)}, u32[]{:S(2)}, u32[]{:S(2)}) %collective-permute-start.26) | collective-permute-done | bytes 32800 | tf_op jit(solution)/shard_map/ppermute | solution.py:308
  100.2 1.7 %back_again.1 = (f32[80,256]{1,0:T(8,128)S(1)}, f32[16,128]{1,0:T(8,128)S(1)}, f32[64,128]{1,0:T(8,128)S(1)}) custom-call(f32[64,128]{1,0:T(8,128)S(1)} %add.96.own, f32[64,128]{1,0:T(8,128)S(1)} %collective-permute-done.25.one, f32[64,128]{1,0:T(8,128)S(1)} %collective-permute-done.26.two, f32[64,128]{1,0:T(8,128)S(1)} %collective-permute-done.27.three, ...), custom_call_target="tpu_custom_call" | custom-call | tf_op jit(solution)/shard_map/back_again/pallas_call | solution.py:295
  102.6 1.5 %collective-permute-start.28 = (f32[16,128]{1,0:T(8,128)S(1)}, f32[16,128]{1,0:T(8,128)S(1)}, u32[]{:S(2)}, u32[]{:S(2)}) collective-permute-start(f32[16,128]{1,0:T(8,128)S(1)} %get-tuple-element.48), channel_id=1, source_target_pairs={{0,1},{1,0},{2,3},{3,2},{4,5},{5,4},{6,7},{7,6},{8,9},{9,8},{10,11... | collective-permute-start | bytes 24584 | tf_op jit(solution)/shard_map/ppermute | solution.py:320
  105.4 3.2 %collective-permute-start.32 = (f32[80,256]{1,0:T(8,128)S(1)}, f32[80,256]{1,0:T(8,128)S(1)}, u32[]{:S(2)}, u32[]{:S(2)}) collective-permute-start(f32[80,256]{1,0:T(8,128)S(1)} %select_add_fusion), channel_id=1, source_target_pairs={{0,24},{8,0},{16,8},{24,16},{1,25},{9,1},{17,9},{25,17},{2,26},{10... | collective-permute-start | bytes 245768 | tf_op jit(solution)/shard_map/ppermute | solution.py:308
  108.7 3.3 %collective-permute-done.31 = f32[80,256]{1,0:T(8,128)S(1)} collective-permute-done((f32[80,256]{1,0:T(8,128)S(1)}, f32[80,256]{1,0:T(8,128)S(1)}, u32[]{:S(2)}, u32[]{:S(2)}) %collective-permute-start.31) | collective-permute-done | bytes 81952 | tf_op jit(solution)/shard_map/ppermute | solution.py:308
  112.9 1.9 %collective-permute-done.30 = f32[80,256]{1,0:T(8,128)S(1)} collective-permute-done((f32[80,256]{1,0:T(8,128)S(1)}, f32[80,256]{1,0:T(8,128)S(1)}, u32[]{:S(2)}, u32[]{:S(2)}) %collective-permute-start.30) | collective-permute-done | bytes 81952 | tf_op jit(solution)/shard_map/ppermute | solution.py:308
  115.0 1.8 %collective-permute-start.35 = (f32[80,256]{1,0:T(8,128)S(1)}, f32[80,256]{1,0:T(8,128)S(1)}, u32[]{:S(2)}, u32[]{:S(2)}) collective-permute-start(f32[80,256]{1,0:T(8,128)S(1)} %add_add_fusion.own), channel_id=1, source_target_pairs={{0,96},{32,0},{64,32},{96,64},{1,97},{33,1},{65,33},{97,65},{2,98}... | collective-permute-start | bytes 245768 | tf_op jit(solution)/shard_map/ppermute | solution.py:308
  117.8 2.3 %collective-permute-done.35.three = f32[80,256]{1,0:T(8,128)S(1)} collective-permute-done((f32[80,256]{1,0:T(8,128)S(1)}, f32[80,256]{1,0:T(8,128)S(1)}, u32[]{:S(2)}, u32[]{:S(2)}) %collective-permute-start.35) | collective-permute-done | bytes 81952 | tf_op jit(solution)/shard_map/ppermute | solution.py:308
  120.0 2.8 %collective-permute-done.34.two = f32[80,256]{1,0:T(8,128)S(1)} collective-permute-done((f32[80,256]{1,0:T(8,128)S(1)}, f32[80,256]{1,0:T(8,128)S(1)}, u32[]{:S(2)}, u32[]{:S(2)}) %collective-permute-start.34) | collective-permute-done | bytes 81952 | tf_op jit(solution)/shard_map/ppermute | solution.py:308
  (134 shorter events, 53.2 us)
Async XLA Ops:
  8.1 8.7 %collective-permute-start.3 = (f32[160,128]{1,0:T(8,128)S(1)}, f32[160,128]{1,0:T(8,128)}, u32[]{:S(2)}, u32[]{:S(2)}) collective-permute-start(f32[160,128]{1,0:T(8,128)S(1)} %add.82.own), channel_id=1, source_target_pairs={{0,6},{2,0},{4,2},{6,4},{1,7},{3,1},{5,3},{7,5},{8,14},{10,8},{12,... | collective-permute-start | bytes 245768 | tf_op jit(solution)/shard_map/ppermute | solution.py:308
  12.3 6.7 %collective-permute-start.2 = (f32[160,128]{1,0:T(8,128)S(1)}, f32[160,128]{1,0:T(8,128)}, u32[]{:S(2)}, u32[]{:S(2)}) collective-permute-start(f32[160,128]{1,0:T(8,128)S(1)} %add.82.own), channel_id=1, source_target_pairs={{0,4},{2,6},{4,0},{6,2},{1,5},{3,7},{5,1},{7,3},{8,12},{10,14},{12... | collective-permute-start | bytes 245768 | tf_op jit(solution)/shard_map/ppermute | solution.py:308
  12.3 7.3 %collective-permute-start.1 = (f32[160,128]{1,0:T(8,128)S(1)}, f32[160,128]{1,0:T(8,128)}, u32[]{:S(2)}, u32[]{:S(2)}) collective-permute-start(f32[160,128]{1,0:T(8,128)S(1)} %add.82.own), channel_id=1, source_target_pairs={{0,2},{2,4},{4,6},{6,0},{1,3},{3,5},{5,7},{7,1},{8,10},{10,12},{12... | collective-permute-start | bytes 245768 | tf_op jit(solution)/shard_map/ppermute | solution.py:308
  28.2 2.2 %collective-permute-start.5 = (f32[16,128]{1,0:T(8,128)}, f32[16,128]{1,0:T(8,128)}, u32[]{:S(2)}, u32[]{:S(2)}) collective-permute-start(f32[16,128]{1,0:T(8,128)} %get-tuple-element.37), channel_id=1, source_target_pairs={{1,2},{3,4},{5,6},{2,1},{4,3},{6,5},{9,10},{11,12},{13,14},{10,9},... | collective-permute-start | bytes 24584 | tf_op jit(solution)/shard_map/ppermute | solution.py:322
  29.5 1.6 %collective-permute-start.4 = (f32[16,128]{1,0:T(8,128)}, f32[16,128]{1,0:T(8,128)}, u32[]{:S(2)}, u32[]{:S(2)}) collective-permute-start(f32[16,128]{1,0:T(8,128)} %get-tuple-element.37), channel_id=1, source_target_pairs={{0,1},{1,0},{2,3},{3,2},{4,5},{5,4},{6,7},{7,6},{8,9},{9,8},{10,11... | collective-permute-start | bytes 24584 | tf_op jit(solution)/shard_map/ppermute | solution.py:320
  32.9 5.7 %collective-permute-start.7 = (f32[80,256]{1,0:T(8,128)S(1)}, f32[80,256]{1,0:T(8,128)S(1)}, u32[]{:S(2)}, u32[]{:S(2)}) collective-permute-start(f32[80,256]{1,0:T(8,128)S(1)} %select_add_fusion.2), channel_id=1, source_target_pairs={{0,8},{8,16},{16,24},{24,0},{1,9},{9,17},{17,25},{25,1},{2,10},{10... | collective-permute-start | bytes 245768 | tf_op jit(solution)/shard_map/ppermute | solution.py:308
  34.5 4.5 %collective-permute-start.8 = (f32[80,256]{1,0:T(8,128)S(1)}, f32[80,256]{1,0:T(8,128)S(1)}, u32[]{:S(2)}, u32[]{:S(2)}) collective-permute-start(f32[80,256]{1,0:T(8,128)S(1)} %select_add_fusion.2), channel_id=1, source_target_pairs={{0,24},{8,0},{16,8},{24,16},{1,25},{9,1},{17,9},{25,17},{2,26},{10... | collective-permute-start | bytes 245768 | tf_op jit(solution)/shard_map/ppermute | solution.py:308
  36.2 6.3 %collective-permute-start.6 = (f32[80,256]{1,0:T(8,128)S(1)}, f32[80,256]{1,0:T(8,128)S(1)}, u32[]{:S(2)}, u32[]{:S(2)}) collective-permute-start(f32[80,256]{1,0:T(8,128)S(1)} %select_add_fusion.2), channel_id=1, source_target_pairs={{0,16},{8,24},{16,0},{24,8},{1,17},{9,25},{17,1},{25,9},{2,18},{10... | collective-permute-start | bytes 245768 | tf_op jit(solution)/shard_map/ppermute | solution.py:308
  43.3 7.1 %collective-permute-start.11 = (f32[80,256]{1,0:T(8,128)S(1)}, f32[80,256]{1,0:T(8,128)S(1)}, u32[]{:S(2)}, u32[]{:S(2)}) collective-permute-start(f32[80,256]{1,0:T(8,128)S(1)} %add_add_fusion.2.own), channel_id=1, source_target_pairs={{0,96},{32,0},{64,32},{96,64},{1,97},{33,1},{65,33},{97,65},{2,98}... | collective-permute-start | bytes 245768 | tf_op jit(solution)/shard_map/ppermute | solution.py:308
  46.3 6.8 %collective-permute-start.10 = (f32[80,256]{1,0:T(8,128)S(1)}, f32[80,256]{1,0:T(8,128)S(1)}, u32[]{:S(2)}, u32[]{:S(2)}) collective-permute-start(f32[80,256]{1,0:T(8,128)S(1)} %add_add_fusion.2.own), channel_id=1, source_target_pairs={{0,64},{32,96},{64,0},{96,32},{1,65},{33,97},{65,1},{97,33},{2,66}... | collective-permute-start | bytes 245768 | tf_op jit(solution)/shard_map/ppermute | solution.py:308
  47.0 7.0 %collective-permute-start.9 = (f32[80,256]{1,0:T(8,128)S(1)}, f32[80,256]{1,0:T(8,128)S(1)}, u32[]{:S(2)}, u32[]{:S(2)}) collective-permute-start(f32[80,256]{1,0:T(8,128)S(1)} %add_add_fusion.2.own), channel_id=1, source_target_pairs={{0,32},{32,64},{64,96},{96,0},{1,33},{33,65},{65,97},{97,1},{2,34}... | collective-permute-start | bytes 245768 | tf_op jit(solution)/shard_map/ppermute | solution.py:308
  58.9 3.9 %collective-permute-start.15 = (f32[56,128]{1,0:T(8,128)S(1)}, f32[56,128]{1,0:T(8,128)S(1)}, u32[]{:S(2)}, u32[]{:S(2)}) collective-permute-start(f32[56,128]{1,0:T(8,128)S(1)} %add.90.own), channel_id=1, source_target_pairs={{0,6},{2,0},{4,2},{6,4},{1,7},{3,1},{5,3},{7,5},{8,14},{10,8},{12,... | collective-permute-start | bytes 86024 | tf_op jit(solution)/shard_map/ppermute | solution.py:308
  60.9 5.4 %collective-permute-start.14 = (f32[56,128]{1,0:T(8,128)S(1)}, f32[56,128]{1,0:T(8,128)S(1)}, u32[]{:S(2)}, u32[]{:S(2)}) collective-permute-start(f32[56,128]{1,0:T(8,128)S(1)} %add.90.own), channel_id=1, source_target_pairs={{0,4},{2,6},{4,0},{6,2},{1,5},{3,7},{5,1},{7,3},{8,12},{10,14},{12... | collective-permute-start | bytes 86024 | tf_op jit(solution)/shard_map/ppermute | solution.py:308
  61.7 5.1 %collective-permute-start.13 = (f32[56,128]{1,0:T(8,128)S(1)}, f32[56,128]{1,0:T(8,128)S(1)}, u32[]{:S(2)}, u32[]{:S(2)}) collective-permute-start(f32[56,128]{1,0:T(8,128)S(1)} %add.90.own), channel_id=1, source_target_pairs={{0,2},{2,4},{4,6},{6,0},{1,3},{3,5},{5,7},{7,1},{8,10},{10,12},{12... | collective-permute-start | bytes 86024 | tf_op jit(solution)/shard_map/ppermute | solution.py:308
  69.2 1.7 %collective-permute-start.16 = (f32[16,128]{1,0:T(8,128)S(1)}, f32[16,128]{1,0:T(8,128)S(1)}, u32[]{:S(2)}, u32[]{:S(2)}) collective-permute-start(f32[16,128]{1,0:T(8,128)S(1)} %get-tuple-element.42), channel_id=1, source_target_pairs={{0,1},{1,0},{2,3},{3,2},{4,5},{5,4},{6,7},{7,6},{8,9},{9,8},{10,11... | collective-permute-start | bytes 24584 | tf_op jit(solution)/shard_map/ppermute | solution.py:320
  71.3 6.7 %collective-permute-start.19 = (f32[80,256]{1,0:T(8,128)S(1)}, f32[80,256]{1,0:T(8,128)S(1)}, u32[]{:S(2)}, u32[]{:S(2)}) collective-permute-start(f32[80,256]{1,0:T(8,128)S(1)} %select_add_fusion.1), channel_id=1, source_target_pairs={{0,8},{8,16},{16,24},{24,0},{1,9},{9,17},{17,25},{25,1},{2,10},{10... | collective-permute-start | bytes 245768 | tf_op jit(solution)/shard_map/ppermute | solution.py:308
  72.2 7.1 %collective-permute-start.20 = (f32[80,256]{1,0:T(8,128)S(1)}, f32[80,256]{1,0:T(8,128)S(1)}, u32[]{:S(2)}, u32[]{:S(2)}) collective-permute-start(f32[80,256]{1,0:T(8,128)S(1)} %select_add_fusion.1), channel_id=1, source_target_pairs={{0,24},{8,0},{16,8},{24,16},{1,25},{9,1},{17,9},{25,17},{2,26},{10... | collective-permute-start | bytes 245768 | tf_op jit(solution)/shard_map/ppermute | solution.py:308
  74.8 6.4 %collective-permute-start.18 = (f32[80,256]{1,0:T(8,128)S(1)}, f32[80,256]{1,0:T(8,128)S(1)}, u32[]{:S(2)}, u32[]{:S(2)}) collective-permute-start(f32[80,256]{1,0:T(8,128)S(1)} %select_add_fusion.1), channel_id=1, source_target_pairs={{0,16},{8,24},{16,0},{24,8},{1,17},{9,25},{17,1},{25,9},{2,18},{10... | collective-permute-start | bytes 245768 | tf_op jit(solution)/shard_map/ppermute | solution.py:308
  81.2 5.0 %collective-permute-start.23 = (f32[80,256]{1,0:T(8,128)S(1)}, f32[80,256]{1,0:T(8,128)S(1)}, u32[]{:S(2)}, u32[]{:S(2)}) collective-permute-start(f32[80,256]{1,0:T(8,128)S(1)} %add_add_fusion.1.own), channel_id=1, source_target_pairs={{0,96},{32,0},{64,32},{96,64},{1,97},{33,1},{65,33},{97,65},{2,98}... | collective-permute-start | bytes 245768 | tf_op jit(solution)/shard_map/ppermute | solution.py:308
  81.9 6.5 %collective-permute-start.22 = (f32[80,256]{1,0:T(8,128)S(1)}, f32[80,256]{1,0:T(8,128)S(1)}, u32[]{:S(2)}, u32[]{:S(2)}) collective-permute-start(f32[80,256]{1,0:T(8,128)S(1)} %add_add_fusion.1.own), channel_id=1, source_target_pairs={{0,64},{32,96},{64,0},{96,32},{1,65},{33,97},{65,1},{97,33},{2,66}... | collective-permute-start | bytes 245768 | tf_op jit(solution)/shard_map/ppermute | solution.py:308
  82.6 6.4 %collective-permute-start.21 = (f32[80,256]{1,0:T(8,128)S(1)}, f32[80,256]{1,0:T(8,128)S(1)}, u32[]{:S(2)}, u32[]{:S(2)}) collective-permute-start(f32[80,256]{1,0:T(8,128)S(1)} %add_add_fusion.1.own), channel_id=1, source_target_pairs={{0,32},{32,64},{64,96},{96,0},{1,33},{33,65},{65,97},{97,1},{2,34}... | collective-permute-start | bytes 245768 | tf_op jit(solution)/shard_map/ppermute | solution.py:308
  91.6 4.8 %collective-permute-start.27 = (f32[64,128]{1,0:T(8,128)S(1)}, f32[64,128]{1,0:T(8,128)S(1)}, u32[]{:S(2)}, u32[]{:S(2)}) collective-permute-start(f32[64,128]{1,0:T(8,128)S(1)} %add.96.own), channel_id=1, source_target_pairs={{0,6},{2,0},{4,2},{6,4},{1,7},{3,1},{5,3},{7,5},{8,14},{10,8},{12,... | collective-permute-start | bytes 98312 | tf_op jit(solution)/shard_map/ppermute | solution.py:308
  94.1 5.4 %collective-permute-start.26 = (f32[64,128]{1,0:T(8,128)S(1)}, f32[64,128]{1,0:T(8,128)S(1)}, u32[]{:S(2)}, u32[]{:S(2)}) collective-permute-start(f32[64,128]{1,0:T(8,128)S(1)} %add.96.own), channel_id=1, source_target_pairs={{0,4},{2,6},{4,0},{6,2},{1,5},{3,7},{5,1},{7,3},{8,12},{10,14},{12... | collective-permute-start | bytes 98312 | tf_op jit(solution)/shard_map/ppermute | solution.py:308
  95.1 5.1 %collective-permute-start.25 = (f32[64,128]{1,0:T(8,128)S(1)}, f32[64,128]{1,0:T(8,128)S(1)}, u32[]{:S(2)}, u32[]{:S(2)}) collective-permute-start(f32[64,128]{1,0:T(8,128)S(1)} %add.96.own), channel_id=1, source_target_pairs={{0,2},{2,4},{4,6},{6,0},{1,3},{3,5},{5,7},{7,1},{8,10},{10,12},{12... | collective-permute-start | bytes 98312 | tf_op jit(solution)/shard_map/ppermute | solution.py:308
  101.9 2.2 %collective-permute-start.29 = (f32[16,128]{1,0:T(8,128)S(1)}, f32[16,128]{1,0:T(8,128)S(1)}, u32[]{:S(2)}, u32[]{:S(2)}) collective-permute-start(f32[16,128]{1,0:T(8,128)S(1)} %get-tuple-element.48), channel_id=1, source_target_pairs={{1,2},{3,4},{5,6},{2,1},{4,3},{6,5},{9,10},{11,12},{13,14},{10,9},... | collective-permute-start | bytes 24584 | tf_op jit(solution)/shard_map/ppermute | solution.py:322
  102.6 2.4 %collective-permute-start.28 = (f32[16,128]{1,0:T(8,128)S(1)}, f32[16,128]{1,0:T(8,128)S(1)}, u32[]{:S(2)}, u32[]{:S(2)}) collective-permute-start(f32[16,128]{1,0:T(8,128)S(1)} %get-tuple-element.48), channel_id=1, source_target_pairs={{0,1},{1,0},{2,3},{3,2},{4,5},{5,4},{6,7},{7,6},{8,9},{9,8},{10,11... | collective-permute-start | bytes 24584 | tf_op jit(solution)/shard_map/ppermute | solution.py:320
  105.3 6.6 %collective-permute-start.31 = (f32[80,256]{1,0:T(8,128)S(1)}, f32[80,256]{1,0:T(8,128)S(1)}, u32[]{:S(2)}, u32[]{:S(2)}) collective-permute-start(f32[80,256]{1,0:T(8,128)S(1)} %select_add_fusion), channel_id=1, source_target_pairs={{0,8},{8,16},{16,24},{24,0},{1,9},{9,17},{17,25},{25,1},{2,10},{10... | collective-permute-start | bytes 245768 | tf_op jit(solution)/shard_map/ppermute | solution.py:308
  105.4 7.5 %collective-permute-start.32 = (f32[80,256]{1,0:T(8,128)S(1)}, f32[80,256]{1,0:T(8,128)S(1)}, u32[]{:S(2)}, u32[]{:S(2)}) collective-permute-start(f32[80,256]{1,0:T(8,128)S(1)} %select_add_fusion), channel_id=1, source_target_pairs={{0,24},{8,0},{16,8},{24,16},{1,25},{9,1},{17,9},{25,17},{2,26},{10... | collective-permute-start | bytes 245768 | tf_op jit(solution)/shard_map/ppermute | solution.py:308
  108.7 6.2 %collective-permute-start.30 = (f32[80,256]{1,0:T(8,128)S(1)}, f32[80,256]{1,0:T(8,128)S(1)}, u32[]{:S(2)}, u32[]{:S(2)}) collective-permute-start(f32[80,256]{1,0:T(8,128)S(1)} %select_add_fusion), channel_id=1, source_target_pairs={{0,16},{8,24},{16,0},{24,8},{1,17},{9,25},{17,1},{25,9},{2,18},{10... | collective-permute-start | bytes 245768 | tf_op jit(solution)/shard_map/ppermute | solution.py:308
  115.0 5.0 %collective-permute-start.35 = (f32[80,256]{1,0:T(8,128)S(1)}, f32[80,256]{1,0:T(8,128)S(1)}, u32[]{:S(2)}, u32[]{:S(2)}) collective-permute-start(f32[80,256]{1,0:T(8,128)S(1)} %add_add_fusion.own), channel_id=1, source_target_pairs={{0,96},{32,0},{64,32},{96,64},{1,97},{33,1},{65,33},{97,65},{2,98}... | collective-permute-start | bytes 245768 | tf_op jit(solution)/shard_map/ppermute | solution.py:308
  116.8 6.0 %collective-permute-start.34 = (f32[80,256]{1,0:T(8,128)S(1)}, f32[80,256]{1,0:T(8,128)S(1)}, u32[]{:S(2)}, u32[]{:S(2)}) collective-permute-start(f32[80,256]{1,0:T(8,128)S(1)} %add_add_fusion.own), channel_id=1, source_target_pairs={{0,64},{32,96},{64,0},{96,32},{1,65},{33,97},{65,1},{97,33},{2,66}... | collective-permute-start | bytes 245768 | tf_op jit(solution)/shard_map/ppermute | solution.py:308
  117.7 6.0 %collective-permute-start.33 = (f32[80,256]{1,0:T(8,128)S(1)}, f32[80,256]{1,0:T(8,128)S(1)}, u32[]{:S(2)}, u32[]{:S(2)}) collective-permute-start(f32[80,256]{1,0:T(8,128)S(1)} %add_add_fusion.own), channel_id=1, source_target_pairs={{0,32},{32,64},{64,96},{96,0},{1,33},{33,65},{65,97},{97,1},{2,34}... | collective-permute-start | bytes 245768 | tf_op jit(solution)/shard_map/ppermute | solution.py:308
  (34 other events, 160.5 us)

commit v2 on v1

v2 whole, which is shorter than its diff:
```python
import functools

import jax
import jax.numpy as jnp
from jax import lax
from jax.experimental import pallas as pl
from jax.experimental.pallas import tpu as pltpu
from jax.sharding import Mesh
from jax.sharding import PartitionSpec as P

SKY = ("sky_0", "sky_1")
TM = ("tm_0", "tm_1")
SKY_TM = ("sky_0", "sky_1", "tm_0", "tm_1")

OBS_DEV = 4096
CHUNK = 1024
damping = 0.5
entry_pairs = [(row_at, col_at) for row_at in range(5) for col_at in range(row_at + 1)]


f32 = jnp.float32
bf16 = jnp.bfloat16


def split_rows(value):
    first = value.astype(bf16)
    rest = value - first.astype(f32)
    second = rest.astype(bf16)
    third = (rest - second.astype(f32)).astype(bf16)
    return jnp.concatenate([first, second, third], axis=0)


def join_rows(stacked):
    rows = stacked.shape[0] // 3
    return stacked[:rows] + (stacked[rows : 2 * rows] + stacked[2 * rows :])


def dot_nt(left, right):
    return lax.dot_general(left, right, (((1,), (1,)), ((), ())), preferred_element_type=f32)


def dot_nn(left, right):
    return lax.dot_general(left, right, (((1,), (0,)), ((), ())), preferred_element_type=f32)


def chunks():
    return [slice(start, start + CHUNK) for start in range(0, OBS_DEV, CHUNK)]


def four(refs):
    own, one, two, three = (ref[...] for ref in refs)
    return (own + two) + (one + three)


def lanes_from(start, rows):
    return lax.broadcasted_iota(jnp.int32, (rows, CHUNK), 1) + start


SOURCE_SPREAD = slice(0, 40)
KNOT_SPREAD = slice(40, 120)
IMAGE = slice(120, 121)
SOURCE_LANE = slice(121, 122)
KNOT_LANE = slice(122, 123)
START, MAPPED, RESIDUAL = (slice(at, at + 256) for at in (0, 256, 512))
FACTOR_A, FACTOR_B, BEFORE, AFTER, SCALAR = (slice(at, at + 128) for at in (768, 896, 1024, 1152, 1280))
WORK = ((128, OBS_DEV), f32)
STATE = ((80, 1408), f32)


def put(state, lanes, start, value):
    state[start : start + value.shape[0], lanes] = value


def get(state, lanes, start, rows):
    return state[start : start + rows, lanes]


def row_numbers(rows):
    return lax.broadcasted_iota(jnp.int32, (rows, CHUNK), 0).astype(f32).astype(bf16)


def hot_rows(numbers, lane_row):
    wanted = jnp.broadcast_to(lane_row, numbers.shape).astype(bf16)
    return jnp.where(numbers == wanted, jnp.ones_like(numbers), jnp.zeros_like(numbers))


def open_kernel(state):
    state[0:8, 0:128] = jnp.zeros((8, 128), f32)


def source_kernel(count_ref, first_ref, source_ref, g_ref, y_ref, prior_ref, _state, work, sums_ref, state):
    numbers = row_numbers(128)
    total = jnp.zeros((480, 128), f32)
    for at in chunks():
        live = lanes_from(at.start, 1) < count_ref[0]
        source = source_ref[:, at]
        lane = (source & 127).astype(f32)
        work[SOURCE_LANE, at] = lane
        mark = jnp.where(live, source >> 7, -1)
        chosen = jnp.where(lax.broadcasted_iota(jnp.int32, (8, CHUNK), 0) == mark, 1.0, 0.0)
        g = [g_ref[j : j + 1, at] for j in range(5)]
        y = y_ref[:, at]
        work[IMAGE, at] = y
        spread = [chosen * g[j] for j in range(5)]
        for j in range(5):
            work[8 * j : 8 * j + 8, at] = spread[j]
        rows = [spread[r] * g[c] for r, c in entry_pairs] + [spread[j] * y for j in range(5)]
        total = total + dot_nt(split_rows(jnp.concatenate(rows, axis=0)), hot_rows(numbers, lane))
    sums_ref[...] = join_rows(total)
    once = jnp.where(first_ref[0] == 1, 1.0, 0.0)
    for at, (row_at, col_at) in enumerate(entry_pairs):
        if row_at == col_at:
            prior = jnp.concatenate([prior_ref[row_at : row_at + 1, 128 * a : 128 * a + 128] for a in range(8)], axis=0)
            sums_ref[8 * at : 8 * at + 8] += prior * once


def knot_kernel(count_ref, last_ref, knot_ref, h_ref, phase_ref, _work, work):
    upper = lax.broadcasted_iota(jnp.int32, (8, CHUNK), 0) >> 2
    for at in chunks():
        live = lanes_from(at.start, 1) < count_ref[0]
        knot = knot_ref[:, at]
        high = knot >> 4
        work[KNOT_LANE, at] = high.astype(f32)
        h = jnp.where(live, h_ref[:, at], 0.0)
        h = jnp.concatenate([h, h], axis=0)
        phase = phase_ref[:, at]
        squared = phase * phase
        cubed = squared * phase
        rest = 1.0 - phase
        taps = (
            rest * rest * rest / 6.0,
            (3.0 * cubed - 6.0 * squared + 4.0) / 6.0,
            (-3.0 * cubed + 3.0 * squared + 3.0 * phase + 1.0) / 6.0,
            cubed / 6.0,
        )
        taps = [jnp.broadcast_to(tap, (8, CHUNK)) for tap in taps]
        ahead = upper - (knot & 15)
        kept = jnp.where((high == 255) & (last_ref[0] == 1), 0.0, 1.0)
        for q in range(10):
            gap = ahead + 2 * q
            weight = jnp.where(gap == 0, taps[0], 0.0)
            for m in range(1, 4):
                weight = jnp.where(gap == m, taps[m], weight)
            if q >= 8:
                weight = weight * kept
            row = KNOT_SPREAD.start + 8 * q
            work[row : row + 8, at] = weight * h


def tile(value, at):
    return value[8 * at : 8 * at + 8]


def factor_of(value):
    return {pair: tile(value, at) for at, pair in enumerate(entry_pairs)}


def factorize(normal):
    factor = {}
    for row_at in range(5):
        for col_at in range(row_at + 1):
            running = normal[row_at, col_at]
            for inner_at in range(col_at):
                running = running - factor[row_at, inner_at] * factor[col_at, inner_at]
            if row_at == col_at:
                factor[row_at, row_at] = 1.0 / jnp.sqrt(running)
            else:
                factor[row_at, col_at] = running * factor[col_at, col_at]
    return factor


def chol_solve(factor, target):
    forward = []
    for row_at in range(5):
        running = target[row_at]
        for inner_at in range(row_at):
            running = running - factor[row_at, inner_at] * forward[inner_at]
        forward.append(running * factor[row_at, row_at])
    result = [None] * 5
    for row_at in reversed(range(5)):
        running = forward[row_at]
        for inner_at in range(row_at + 1, 5):
            running = running - factor[inner_at, row_at] * result[inner_at]
        result[row_at] = running * factor[row_at, row_at]
    return result


def eliminate_and_spread(solved, work):
    solved = split_rows(jnp.concatenate(solved, axis=0))
    source_numbers, knot_numbers = row_numbers(128), row_numbers(256)
    total = jnp.zeros((240, 256), f32)
    for at in chunks():
        picked = join_rows(dot_nn(solved, hot_rows(source_numbers, work[SOURCE_LANE, at])))
        fitted = jnp.sum(picked * work[SOURCE_SPREAD, at], axis=0, keepdims=True)
        cleaned = work[IMAGE, at] - fitted
        total = total + dot_nt(split_rows(work[KNOT_SPREAD, at] * cleaned), hot_rows(knot_numbers, work[KNOT_LANE, at]))
    return join_rows(total)


def put_knots(total, energy, knots_ref, edge_ref):
    knots_ref[0:72] = total[0:72]
    if energy is None:
        tail = total[76:80]
    else:
        tail = jnp.concatenate([energy[0:4], energy[4:8]], axis=1)
    knots_ref[72:80] = jnp.concatenate([total[72:76], tail], axis=0)
    lane = lax.broadcasted_iota(jnp.int32, (16, 128), 1)
    edge_ref[...] = jnp.where(lane == 127, total[64:80, 128:256], jnp.where(lane == 0, total[0:16, 0:128], 0.0))


def first_kernel(own, one, two, three, _work, _state, knots_ref, edge_ref, work, state):
    sums = four((own, one, two, three))
    factor = factorize(factor_of(sums))
    stacked = jnp.concatenate([factor[pair] for pair in entry_pairs], axis=0)
    put(state, FACTOR_A, 0, stacked[0:80])
    put(state, FACTOR_B, 0, stacked[80:120])
    put(state, FACTOR_B, 40, sums[120:160])
    solved = chol_solve(factor, [tile(sums, 15 + j) for j in range(5)])
    put_knots(eliminate_and_spread(solved, work), None, knots_ref, edge_ref)


def kept_factor(state):
    return factor_of(jnp.concatenate([get(state, FACTOR_A, 0, 80), get(state, FACTOR_B, 0, 40)], axis=0))


def back_kernel(lanes, own, one, two, three, _work, _state, knots_ref, edge_ref, work, state):
    sums = four((own, one, two, three))
    put(state, lanes, 0, sums)
    target = [tile(sums, j) for j in range(5)]
    solved = chol_solve(kept_factor(state), target)
    energy = tile(sums, 5)
    for j in range(5):
        energy = energy - target[j] * solved[j]
    put_knots(eliminate_and_spread(solved, work), energy, knots_ref, edge_ref)


def edge_kernel(odd_ref, _knots, twin_ref, other_ref, knots_ref):
    odd = odd_ref[0] == 1
    twin, other = twin_ref[...], other_ref[...]
    earlier = pltpu.roll(jnp.where(odd, twin, other), 1, 1)
    later = pltpu.roll(jnp.where(odd, other, twin), 127, 1)
    lane = lax.broadcasted_iota(jnp.int32, (16, 128), 1)
    within = lax.broadcasted_iota(jnp.int32, (16, 128), 0) < 12
    knots_ref[0:16, 0:128] += jnp.where(within & (lane == 0), earlier, 0.0)
    knots_ref[64:80, 128:256] += jnp.where(within & (lane == 127), later, 0.0)


def assembled(knots):
    lane = lax.broadcasted_iota(jnp.int32, (16, 256), 1)
    row = lax.broadcasted_iota(jnp.int32, (16, 256), 0)
    beyond = jnp.where(row < 12, knots[64:80], 0.0)
    low = knots[0:16] + jnp.where(lane == 0, 0.0, pltpu.roll(beyond, 1, 1))
    high = jnp.where(row < 12, jnp.where(lane == 255, beyond, pltpu.roll(low, 255, 1)), 0.0)
    return jnp.concatenate([low, knots[16:64], high], axis=0)


def energy_of(knots):
    return jnp.sum(knots[76:80])


def folded(left, right):
    product = left[0:64] * right[0:64]
    product = product[:, 0:128] + product[:, 128:256]
    return functools.reduce(jnp.add, [tile(product, at) for at in range(8)])


def gather_and_sum(field, work):
    source_numbers, knot_numbers = row_numbers(128), row_numbers(256)
    parts = split_rows(field)
    total = jnp.zeros((120, 128), f32)
    square = jnp.zeros((1, 128), f32)
    for at in chunks():
        picked = join_rows(dot_nn(parts, hot_rows(knot_numbers, work[KNOT_LANE, at])))
        image = jnp.sum(picked * work[KNOT_SPREAD, at], axis=0, keepdims=True)
        work[IMAGE, at] = image
        for start in range(0, CHUNK, 128):
            piece = image[:, start : start + 128]
            square = square + piece * piece
        total = total + dot_nt(split_rows(work[SOURCE_SPREAD, at] * image), hot_rows(source_numbers, work[SOURCE_LANE, at]))
    return join_rows(total), jnp.concatenate([square, jnp.zeros((7, 128), f32)], axis=0)


def start_kernel(own, one, two, three, _work, _state, sums_ref, work, state):
    residual = assembled(four((own, one, two, three)))
    put(state, START, 0, residual)
    sums, square = gather_and_sum(residual, work)
    sums_ref[...] = jnp.concatenate([sums, square, folded(residual, residual)], axis=0)


def next_kernel(own, one, two, three, _work, _state, sums_ref, work, state):
    knots = four((own, one, two, three))
    direction = get(state, START, 0, 80)
    mapped = assembled(knots) + damping * direction
    norm_now = jnp.sum(get(state, BEFORE, 48, 8))
    product = energy_of(knots) + damping * norm_now
    residual = direction - (norm_now / product) * mapped
    put(state, MAPPED, 0, mapped)
    put(state, RESIDUAL, 0, residual)
    put(state, SCALAR, 0, jnp.zeros((8, 128), f32) + product)
    sums, square = gather_and_sum(residual, work)
    sums_ref[...] = jnp.concatenate([sums, square, folded(residual, residual), folded(residual, mapped)], axis=0)


def last_kernel(place_ref, own, one, two, three, state, solution_ref, left_ref, source_ref):
    knots = four((own, one, two, three))
    residual = get(state, RESIDUAL, 0, 64)
    image = assembled(knots)[0:64] + damping * residual
    before, after = get(state, BEFORE, 0, 56), get(state, AFTER, 0, 64)
    norm_first = jnp.sum(before[48:56])
    product_first = jnp.max(get(state, SCALAR, 0, 8))
    alpha_first = norm_first / product_first
    norm_now = jnp.sum(after[48:56])
    crossed = jnp.sum(after[56:64])
    beta = norm_now / norm_first
    product = energy_of(knots) + damping * norm_now + beta * (2.0 * crossed + beta * product_first)
    alpha = norm_now / product
    from_start = alpha_first + alpha * beta
    solution = from_start * get(state, START, 0, 64) + alpha * residual
    left = residual - alpha * (image + beta * get(state, MAPPED, 0, 64))
    both = split_rows(jnp.concatenate([solution, left], axis=0))
    row = lax.broadcasted_iota(jnp.int32, (256, 256), 0)
    lane = lax.broadcasted_iota(jnp.int32, (256, 256), 1)
    chosen = jnp.where(row == place_ref[0] * 16 + (lane >> 4), 1.0, 0.0).astype(bf16)
    picked = join_rows(dot_nn(both, chosen))
    low = lax.broadcasted_iota(jnp.int32, (8, 256), 1) & 15
    upper = lax.broadcasted_iota(jnp.int32, (8, 256), 0) >> 2
    for at, ref in enumerate((solution_ref, left_ref)):
        own_rows = jnp.zeros((8, 256), f32)
        for q in range(8):
            own_rows = jnp.where(low == upper + 2 * q, tile(picked, 8 * at + q), own_rows)
        own_rows = own_rows[0:4] + own_rows[4:8]
        for c in range(4):
            ref[c] = own_rows[c : c + 1]
    rhs = get(state, FACTOR_B, 40, 40)
    target = [tile(rhs, j) - from_start * tile(before, j) - alpha * tile(after, j) for j in range(5)]
    solved = chol_solve(kept_factor(state), target)
    for j in range(5):
        for a in range(8):
            source_ref[j : j + 1, 128 * a : 128 * a + 128] = solved[j][a : a + 1]


VMEM = pl.BlockSpec(memory_space=pltpu.VMEM)
SMEM = pl.BlockSpec(memory_space=pltpu.SMEM)


def call(kernel, name, outs, *operands, scalars=0, aliases=None, work_ahead=0):
    specs = [SMEM] * scalars + [VMEM] * (len(operands) - scalars)
    shapes = [jax.ShapeDtypeStruct(shape, dtype) for shape, dtype in outs]
    return pl.pallas_call(
        kernel,
        out_shape=shapes,
        in_specs=specs,
        out_specs=[VMEM] * len(outs),
        input_output_aliases=aliases or {},
        compiler_params=pltpu.CompilerParams(vmem_limit_bytes=8 * 1024 * 1024),
        cost_estimate=pl.CostEstimate(flops=work_ahead, bytes_accessed=0, transcendentals=0) if work_ahead else None,
        name=name,
    )(*operands)


def ring_parts(value, axis):
    count = lax.axis_size(axis)
    return [value] + [
        lax.ppermute(value, axis, [(at, (at + step) % count) for at in range(count)]) for step in (1, 2, 3)
    ]


def tm_parts(value):
    value = value + lax.ppermute(value, "tm_1", [(0, 1), (1, 0)])
    return ring_parts(value, "tm_0")


def sky_parts(knots, edge, odd):
    count = lax.axis_size(TM)
    twin = lax.ppermute(edge, "tm_1", [(0, 1), (1, 0)])
    swaps = [(low, low + 1) for low in range(1, count - 1, 2)]
    other = lax.ppermute(edge, TM, swaps + [(high, low) for low, high in swaps])
    (knots,) = call(edge_kernel, "edges", [KNOTS], odd, knots, twin, other, scalars=1, aliases={1: 0})
    own, one, two, three = ring_parts(knots, "sky_1")
    return ring_parts((own + two) + (one + three), "sky_0")


KNOTS = ((80, 256), f32)
EDGE = ((16, 128), f32)


def shards(obs_source, obs_knot, obs_count, src_design, att_design, obs_phase, obs_value, src_prior):
    at = lax.axis_index(TM)
    first = (at == 0).astype(jnp.int32).reshape(1)
    last = (at == lax.axis_size(TM) - 1).astype(jnp.int32).reshape(1)
    odd = (at % 2).astype(jnp.int32).reshape(1)
    place = lax.axis_index(SKY).astype(jnp.int32).reshape(1)
    line = lambda value: value.reshape(1, OBS_DEV)
    (state,) = call(open_kernel, "open", [STATE], work_ahead=1 << 32)
    work, sums, state = call(
        source_kernel,
        "source_sums",
        [WORK, ((160, 128), f32), STATE],
        obs_count, first, line(obs_source), src_design, line(obs_value), src_prior, state,
        aliases={6: 2},
        scalars=2,
    )
    parts = tm_parts(sums)
    (work,) = call(
        knot_kernel,
        "knot_spread",
        [WORK],
        obs_count, last, line(obs_knot), att_design, line(obs_phase), work,
        scalars=2,
        aliases={5: 0},
    )
    there = [KNOTS, EDGE, WORK, STATE]
    knots, edge, work, state = call(first_kernel, "first", there, *parts, work, state, aliases={4: 2, 5: 3})
    parts = sky_parts(knots, edge, odd)
    sums, work, state = call(
        start_kernel, "start", [((56, 128), f32), WORK, STATE], *parts, work, state, aliases={4: 1, 5: 2}
    )
    parts = tm_parts(sums)
    knots, edge, work, state = call(
        functools.partial(back_kernel, BEFORE), "back", there, *parts, work, state, aliases={4: 2, 5: 3}
    )
    parts = sky_parts(knots, edge, odd)
    sums, work, state = call(
        next_kernel, "next", [((64, 128), f32), WORK, STATE], *parts, work, state, aliases={4: 1, 5: 2}
    )
    parts = tm_parts(sums)
    knots, edge, work, state = call(
        functools.partial(back_kernel, AFTER), "back_again", there, *parts, work, state, aliases={4: 2, 5: 3}
    )
    parts = sky_parts(knots, edge, odd)
    return call(
        last_kernel,
        "last",
        [((4, 1, 256), f32), ((4, 1, 256), f32), ((5, 1024), f32)],
        place, *parts, state,
        scalars=1,
    )


def solution(mesh):
    torus = Mesh(mesh.devices.reshape(4, 4, 4, 2), SKY_TM)
    placed = (
        P(SKY_TM),
        P(SKY_TM),
        P(SKY_TM),
        P(None, SKY_TM),
        P(None, SKY_TM),
        P(SKY_TM),
        P(SKY_TM),
        P(None, SKY),
    )
    return jax.shard_map(
        shards,
        mesh=torus,
        in_specs=placed,
        out_specs=(P(None, TM, SKY), P(None, TM, SKY), P(None, SKY)),
        check_vma=False,
    )
```

time: 131 us -> 109 us (0.83); the launches traced: 130 us -> 109 us
  local copies, waits for them, and re-layouts: 19.5 us -> 0.11 us
  waiting for transfers between devices: 50.7 us -> 56.9 us
  other arithmetic: 3.69 us -> 0.1 us
  starting transfers between devices: 41.9 us -> 39.9 us
  Pallas kernels: 12.3 us -> 10.6 us
    unnamed x62 -> x14, local copies, waits for them, and re-layouts: 19.3 us -> 0.11 us
    ppermute x27, waiting for transfers between devices: 44.7 us -> 50.8 us  [ring_parts(): lax.ppermute(value, axis, [(at, (at + step) % count) for at in range(coun...]
    pallas_call x8 -> x12, Pallas kernels: 12.3 us -> 10.6 us  [call(): pl.pallas_call(kernel, out_shape=shapes, in_specs=specs, out_specs=[VMEM]...]
    ppermute x27, starting transfers between devices: 36.3 us -> 34.8 us  [ring_parts(): lax.ppermute(value, axis, [(at, (at + step) % count) for at in range(coun...]
  transfers between devices with their start and end apart: 36 -> 36, of which waited for: 31 -> 29; matrix products, arithmetic and copies ran while one was open for 0% -> 0% of each run, Pallas kernels for 1% -> 0%
where the time goes in v2:
time: 109 us
  waiting for transfers between devices  56.9 us (52%)
  starting transfers between devices  39.9 us (37%)
  Pallas kernels  10.6 us (10%)
  between operations  1.59 us (1%)
    ppermute x27, waiting for transfers between devices, ring_parts(): lax.ppermute(value, axis, [(at, (at + step) % count) for at in range(coun...  50.8 us
    ppermute x27, starting transfers between devices, ring_parts(): lax.ppermute(value, axis, [(at, (at + step) % count) for at in range(coun...  34.8 us
    pallas_call x12, Pallas kernels, call(): pl.pallas_call(kernel, out_shape=shapes, in_specs=specs, out_specs=[VMEM]...  10.6 us
    ppermute x3, waiting for transfers between devices, tm_parts(): value = value + lax.ppermute(value, 'tm_1', [(0, 1), (1, 0)])  3.65 us
    ppermute x3, starting transfers between devices, sky_parts(): twin = lax.ppermute(edge, 'tm_1', [(0, 1), (1, 0)])  2.83 us
    ppermute x3, waiting for transfers between devices, sky_parts(): twin = lax.ppermute(edge, 'tm_1', [(0, 1), (1, 0)])  2.48 us
  transfers between devices with their start and end apart: 36, of which 29 were waited for; matrix products, arithmetic and copies ran while one was open for 0% of the time, Pallas kernels for 0%

profile of v2, /device:TPU:0, one launch (start us, length us, event | category | flops | bytes accessed | tf_op | source)
XLA Modules:
  0.0 109.2 jit_solution(5268762021869915229)
XLA Ops:
  4.2 4.2 %collective-permute-start.3 = (f32[160,128]{1,0:T(8,128)S(1)}, f32[160,128]{1,0:T(8,128)S(1)}, u32[]{:S(2)}, u32[]{:S(2)}) collective-permute-start(f32[160,128]{1,0:T(8,128)S(1)} %add.49.own), channel_id=1, source_target_pairs={{0,6},{2,0},{4,2},{6,4},{1,7},{3,1},{5,3},{7,5},{8,14},{10,8},{12,... | collective-permute-start | bytes 245768 | tf_op jit(solution)/shard_map/ppermute | solution.py:364
  10.1 2.0 %collective-permute-done.3.three = f32[160,128]{1,0:T(8,128)S(1)} collective-permute-done((f32[160,128]{1,0:T(8,128)S(1)}, f32[160,128]{1,0:T(8,128)S(1)}, u32[]{:S(2)}, u32[]{:S(2)}) %collective-permute-start.3) | collective-permute-done | bytes 81952 | tf_op jit(solution)/shard_map/ppermute | solution.py:364
  12.2 2.8 %collective-permute-done.2.two = f32[160,128]{1,0:T(8,128)S(1)} collective-permute-done((f32[160,128]{1,0:T(8,128)S(1)}, f32[160,128]{1,0:T(8,128)S(1)}, u32[]{:S(2)}, u32[]{:S(2)}) %collective-permute-start.2) | collective-permute-done | bytes 81952 | tf_op jit(solution)/shard_map/ppermute | solution.py:364
  15.6 1.7 %first.1 = (f32[80,256]{1,0:T(8,128)S(1)}, f32[16,128]{1,0:T(8,128)S(1)}, f32[128,4096]{1,0:T(8,128)S(1)}, f32[80,1408]{1,0:T(8,128)S(1)}) custom-call(f32[160,128]{1,0:T(8,128)S(1)} %add.49.own, f32[160,128]{1,0:T(8,128)S(1)} %collective-permute-done.1.one, ...), custom_call_target="tpu_custom_call", output_to_operand_aliasing={{2}: (4, {}), {3}: (5, {})} | custom-call | tf_op jit(solution)/shard_map/first/pallas_call | solution.py:349
  19.9 2.8 %collective-permute-start.8 = (f32[80,256]{1,0:T(8,128)S(1)}, f32[80,256]{1,0:T(8,128)S(1)}, u32[]{:S(2)}, u32[]{:S(2)}) collective-permute-start(f32[80,256]{1,0:T(8,128)S(1)} %edges.3), channel_id=1, source_target_pairs={{0,24},{8,0},{16,8},{24,16},{1,25},{9,1},{17,9},{25,17},{2,26},{10... | collective-permute-start | bytes 245768 | tf_op jit(solution)/shard_map/ppermute | solution.py:364
  22.7 2.3 %collective-permute-start.6 = (f32[80,256]{1,0:T(8,128)S(1)}, f32[80,256]{1,0:T(8,128)S(1)}, u32[]{:S(2)}, u32[]{:S(2)}) collective-permute-start(f32[80,256]{1,0:T(8,128)S(1)} %edges.3), channel_id=1, source_target_pairs={{0,16},{8,24},{16,0},{24,8},{1,17},{9,25},{17,1},{25,9},{2,18},{10... | collective-permute-start | bytes 245768 | tf_op jit(solution)/shard_map/ppermute | solution.py:364
  25.0 5.5 %collective-permute-done.7 = f32[80,256]{1,0:T(8,128)S(1)} collective-permute-done((f32[80,256]{1,0:T(8,128)S(1)}, f32[80,256]{1,0:T(8,128)S(1)}, u32[]{:S(2)}, u32[]{:S(2)}) %collective-permute-start.7) | collective-permute-done | bytes 81952 | tf_op jit(solution)/shard_map/ppermute | solution.py:364
  30.5 3.1 %collective-permute-start.11 = (f32[80,256]{1,0:T(8,128)S(1)}, f32[80,256]{1,0:T(8,128)S(1)}, u32[]{:S(2)}, u32[]{:S(2)}) collective-permute-start(f32[80,256]{1,0:T(8,128)S(1)} %add_add_fusion.2.own), channel_id=1, source_target_pairs={{0,96},{32,0},{64,32},{96,64},{1,97},{33,1},{65,33},{97,65},{2,98}... | collective-permute-start | bytes 245768 | tf_op jit(solution)/shard_map/ppermute | solution.py:364
  35.2 2.4 %collective-permute-done.11.three = f32[80,256]{1,0:T(8,128)S(1)} collective-permute-done((f32[80,256]{1,0:T(8,128)S(1)}, f32[80,256]{1,0:T(8,128)S(1)}, u32[]{:S(2)}, u32[]{:S(2)}) %collective-permute-start.11) | collective-permute-done | bytes 81952 | tf_op jit(solution)/shard_map/ppermute | solution.py:364
  37.6 2.8 %collective-permute-done.10.two = f32[80,256]{1,0:T(8,128)S(1)} collective-permute-done((f32[80,256]{1,0:T(8,128)S(1)}, f32[80,256]{1,0:T(8,128)S(1)}, u32[]{:S(2)}, u32[]{:S(2)}) %collective-permute-start.10) | collective-permute-done | bytes 81952 | tf_op jit(solution)/shard_map/ppermute | solution.py:364
  45.0 1.4 %collective-permute-start.14 = (f32[56,128]{1,0:T(8,128)S(1)}, f32[56,128]{1,0:T(8,128)S(1)}, u32[]{:S(2)}, u32[]{:S(2)}) collective-permute-start(f32[56,128]{1,0:T(8,128)S(1)} %add.53.own), channel_id=1, source_target_pairs={{0,4},{2,6},{4,0},{6,2},{1,5},{3,7},{5,1},{7,3},{8,12},{10,14},{12... | collective-permute-start | bytes 86024 | tf_op jit(solution)/shard_map/ppermute | solution.py:364
  47.9 2.7 %collective-permute-done.14.two = f32[56,128]{1,0:T(8,128)S(1)} collective-permute-done((f32[56,128]{1,0:T(8,128)S(1)}, f32[56,128]{1,0:T(8,128)S(1)}, u32[]{:S(2)}, u32[]{:S(2)}) %collective-permute-start.14) | collective-permute-done | bytes 28704 | tf_op jit(solution)/shard_map/ppermute | solution.py:364
  51.5 1.7 %back.1 = (f32[80,256]{1,0:T(8,128)S(1)}, f32[16,128]{1,0:T(8,128)S(1)}, f32[128,4096]{1,0:T(8,128)S(1)}, f32[80,1408]{1,0:T(8,128)S(1)}) custom-call(f32[56,128]{1,0:T(8,128)S(1)} %add.53.own, f32[56,128]{1,0:T(8,128)S(1)} %collective-permute-done.13.one, f32[56,128]{1,0:T(8,128)S(1)} %collective-permute-done.14.two, ...), custom_call_target="tpu_custom_call", output_to_operand_aliasing={{2}: (4, {}), {3}: (5, {})} | custom-call | tf_op jit(solution)/shard_map/back/pallas_call | solution.py:349
  55.9 1.8 %collective-permute-start.20 = (f32[80,256]{1,0:T(8,128)S(1)}, f32[80,256]{1,0:T(8,128)S(1)}, u32[]{:S(2)}, u32[]{:S(2)}) collective-permute-start(f32[80,256]{1,0:T(8,128)S(1)} %edges.4), channel_id=1, source_target_pairs={{0,24},{8,0},{16,8},{24,16},{1,25},{9,1},{17,9},{25,17},{2,26},{10... | collective-permute-start | bytes 245768 | tf_op jit(solution)/shard_map/ppermute | solution.py:364
  57.9 1.3 %collective-permute-start.18 = (f32[80,256]{1,0:T(8,128)S(1)}, f32[80,256]{1,0:T(8,128)S(1)}, u32[]{:S(2)}, u32[]{:S(2)}) collective-permute-start(f32[80,256]{1,0:T(8,128)S(1)} %edges.4), channel_id=1, source_target_pairs={{0,16},{8,24},{16,0},{24,8},{1,17},{9,25},{17,1},{25,9},{2,18},{10... | collective-permute-start | bytes 245768 | tf_op jit(solution)/shard_map/ppermute | solution.py:364
  59.2 1.9 %collective-permute-done.20 = f32[80,256]{1,0:T(8,128)S(1)} collective-permute-done((f32[80,256]{1,0:T(8,128)S(1)}, f32[80,256]{1,0:T(8,128)S(1)}, u32[]{:S(2)}, u32[]{:S(2)}) %collective-permute-start.20) | collective-permute-done | bytes 81952 | tf_op jit(solution)/shard_map/ppermute | solution.py:364
  61.1 4.7 %collective-permute-done.19 = f32[80,256]{1,0:T(8,128)S(1)} collective-permute-done((f32[80,256]{1,0:T(8,128)S(1)}, f32[80,256]{1,0:T(8,128)S(1)}, u32[]{:S(2)}, u32[]{:S(2)}) %collective-permute-start.19) | collective-permute-done | bytes 81952 | tf_op jit(solution)/shard_map/ppermute | solution.py:364
  67.4 1.3 %collective-permute-start.21 = (f32[80,256]{1,0:T(8,128)S(1)}, f32[80,256]{1,0:T(8,128)S(1)}, u32[]{:S(2)}, u32[]{:S(2)}) collective-permute-start(f32[80,256]{1,0:T(8,128)S(1)} %add_add_fusion.1.own), channel_id=1, source_target_pairs={{0,32},{32,64},{64,96},{96,0},{1,33},{33,65},{65,97},{97,1},{2,34}... | collective-permute-start | bytes 245768 | tf_op jit(solution)/shard_map/ppermute | solution.py:364
  68.7 2.6 %collective-permute-done.23.three = f32[80,256]{1,0:T(8,128)S(1)} collective-permute-done((f32[80,256]{1,0:T(8,128)S(1)}, f32[80,256]{1,0:T(8,128)S(1)}, u32[]{:S(2)}, u32[]{:S(2)}) %collective-permute-start.23) | collective-permute-done | bytes 81952 | tf_op jit(solution)/shard_map/ppermute | solution.py:364
  71.3 1.8 %collective-permute-done.22.two = f32[80,256]{1,0:T(8,128)S(1)} collective-permute-done((f32[80,256]{1,0:T(8,128)S(1)}, f32[80,256]{1,0:T(8,128)S(1)}, u32[]{:S(2)}, u32[]{:S(2)}) %collective-permute-start.22) | collective-permute-done | bytes 81952 | tf_op jit(solution)/shard_map/ppermute | solution.py:364
  74.0 1.3 %next.1 = (f32[64,128]{1,0:T(8,128)S(1)}, f32[128,4096]{1,0:T(8,128)S(1)}, f32[80,1408]{1,0:T(8,128)S(1)}) custom-call(f32[80,256]{1,0:T(8,128)S(1)} %add_add_fusion.1.own, f32[80,256]{1,0:T(8,128)S(1)} %collective-permute-done.21.one, f32[80,256]{1,0:T(8,128)S(1)} %collective-permute-done.22.two, ...), custom_call_target="tpu_custom_call", output_to_operand_aliasing={{1}: (4, {}), {2}: (5, {})} | custom-call | tf_op jit(solution)/shard_map/next/pallas_call | solution.py:349
  77.6 2.1 %collective-permute-start.26 = (f32[64,128]{1,0:T(8,128)S(1)}, f32[64,128]{1,0:T(8,128)S(1)}, u32[]{:S(2)}, u32[]{:S(2)}) collective-permute-start(f32[64,128]{1,0:T(8,128)S(1)} %add.57.own), channel_id=1, source_target_pairs={{0,4},{2,6},{4,0},{6,2},{1,5},{3,7},{5,1},{7,3},{8,12},{10,14},{12... | collective-permute-start | bytes 98312 | tf_op jit(solution)/shard_map/ppermute | solution.py:364
  80.5 2.7 %collective-permute-done.26.two = f32[64,128]{1,0:T(8,128)S(1)} collective-permute-done((f32[64,128]{1,0:T(8,128)S(1)}, f32[64,128]{1,0:T(8,128)S(1)}, u32[]{:S(2)}, u32[]{:S(2)}) %collective-permute-start.26) | collective-permute-done | bytes 32800 | tf_op jit(solution)/shard_map/ppermute | solution.py:364
  83.2 1.6 %collective-permute-done.25.one = f32[64,128]{1,0:T(8,128)S(1)} collective-permute-done((f32[64,128]{1,0:T(8,128)S(1)}, f32[64,128]{1,0:T(8,128)S(1)}, u32[]{:S(2)}, u32[]{:S(2)}) %collective-permute-start.25) | collective-permute-done | bytes 32800 | tf_op jit(solution)/shard_map/ppermute | solution.py:364
  84.8 1.7 %back_again.1 = (f32[80,256]{1,0:T(8,128)S(1)}, f32[16,128]{1,0:T(8,128)S(1)}, f32[128,4096]{1,0:T(8,128)S(1)}, f32[80,1408]{1,0:T(8,128)S(1)}) custom-call(f32[64,128]{1,0:T(8,128)S(1)} %add.57.own, f32[64,128]{1,0:T(8,128)S(1)} %collective-permute-done.25.one, ...), custom_call_target="tpu_custom_call", output_to_operand_aliasing={{2}: (4, {}), {3}: (5, {})} | custom-call | tf_op jit(solution)/shard_map/back_again/pallas_call | solution.py:349
  88.7 2.5 %collective-permute-start.32 = (f32[80,256]{1,0:T(8,128)S(1)}, f32[80,256]{1,0:T(8,128)S(1)}, u32[]{:S(2)}, u32[]{:S(2)}) collective-permute-start(f32[80,256]{1,0:T(8,128)S(1)} %edges.5), channel_id=1, source_target_pairs={{0,24},{8,0},{16,8},{24,16},{1,25},{9,1},{17,9},{25,17},{2,26},{10... | collective-permute-start | bytes 245768 | tf_op jit(solution)/shard_map/ppermute | solution.py:364
  91.2 1.5 %collective-permute-start.30 = (f32[80,256]{1,0:T(8,128)S(1)}, f32[80,256]{1,0:T(8,128)S(1)}, u32[]{:S(2)}, u32[]{:S(2)}) collective-permute-start(f32[80,256]{1,0:T(8,128)S(1)} %edges.5), channel_id=1, source_target_pairs={{0,16},{8,24},{16,0},{24,8},{1,17},{9,25},{17,1},{25,9},{2,18},{10... | collective-permute-start | bytes 245768 | tf_op jit(solution)/shard_map/ppermute | solution.py:364
  92.8 1.3 %collective-permute-done.32 = f32[80,256]{1,0:T(8,128)S(1)} collective-permute-done((f32[80,256]{1,0:T(8,128)S(1)}, f32[80,256]{1,0:T(8,128)S(1)}, u32[]{:S(2)}, u32[]{:S(2)}) %collective-permute-start.32) | collective-permute-done | bytes 81952 | tf_op jit(solution)/shard_map/ppermute | solution.py:364
  94.0 5.1 %collective-permute-done.31 = f32[80,256]{1,0:T(8,128)S(1)} collective-permute-done((f32[80,256]{1,0:T(8,128)S(1)}, f32[80,256]{1,0:T(8,128)S(1)}, u32[]{:S(2)}, u32[]{:S(2)}) %collective-permute-start.31) | collective-permute-done | bytes 81952 | tf_op jit(solution)/shard_map/ppermute | solution.py:364
  99.2 1.8 %collective-permute-start.35 = (f32[80,256]{1,0:T(8,128)S(1)}, f32[80,256]{1,0:T(8,128)S(1)}, u32[]{:S(2)}, u32[]{:S(2)}) collective-permute-start(f32[80,256]{1,0:T(8,128)S(1)} %add_add_fusion.own), channel_id=1, source_target_pairs={{0,96},{32,0},{64,32},{96,64},{1,97},{33,1},{65,33},{97,65},{2,98}... | collective-permute-start | bytes 245768 | tf_op jit(solution)/shard_map/ppermute | solution.py:364
  102.0 2.5 %collective-permute-done.35.three = f32[80,256]{1,0:T(8,128)S(1)} collective-permute-done((f32[80,256]{1,0:T(8,128)S(1)}, f32[80,256]{1,0:T(8,128)S(1)}, u32[]{:S(2)}, u32[]{:S(2)}) %collective-permute-start.35) | collective-permute-done | bytes 81952 | tf_op jit(solution)/shard_map/ppermute | solution.py:364
  104.5 2.9 %collective-permute-done.34.two = f32[80,256]{1,0:T(8,128)S(1)} collective-permute-done((f32[80,256]{1,0:T(8,128)S(1)}, f32[80,256]{1,0:T(8,128)S(1)}, u32[]{:S(2)}, u32[]{:S(2)}) %collective-permute-start.34) | collective-permute-done | bytes 81952 | tf_op jit(solution)/shard_map/ppermute | solution.py:364
  (72 shorter events, 29.9 us)
Async XLA Ops:
  4.2 8.0 %collective-permute-start.3 = (f32[160,128]{1,0:T(8,128)S(1)}, f32[160,128]{1,0:T(8,128)S(1)}, u32[]{:S(2)}, u32[]{:S(2)}) collective-permute-start(f32[160,128]{1,0:T(8,128)S(1)} %add.49.own), channel_id=1, source_target_pairs={{0,6},{2,0},{4,2},{6,4},{1,7},{3,1},{5,3},{7,5},{8,14},{10,8},{12,... | collective-permute-start | bytes 245768 | tf_op jit(solution)/shard_map/ppermute | solution.py:364
  8.4 6.6 %collective-permute-start.2 = (f32[160,128]{1,0:T(8,128)S(1)}, f32[160,128]{1,0:T(8,128)S(1)}, u32[]{:S(2)}, u32[]{:S(2)}) collective-permute-start(f32[160,128]{1,0:T(8,128)S(1)} %add.49.own), channel_id=1, source_target_pairs={{0,4},{2,6},{4,0},{6,2},{1,5},{3,7},{5,1},{7,3},{8,12},{10,14},{12... | collective-permute-start | bytes 245768 | tf_op jit(solution)/shard_map/ppermute | solution.py:364
  8.4 7.2 %collective-permute-start.1 = (f32[160,128]{1,0:T(8,128)S(1)}, f32[160,128]{1,0:T(8,128)S(1)}, u32[]{:S(2)}, u32[]{:S(2)}) collective-permute-start(f32[160,128]{1,0:T(8,128)S(1)} %add.49.own), channel_id=1, source_target_pairs={{0,2},{2,4},{4,6},{6,0},{1,3},{3,5},{5,7},{7,1},{8,10},{10,12},{12... | collective-permute-start | bytes 245768 | tf_op jit(solution)/shard_map/ppermute | solution.py:364
  17.3 1.7 %collective-permute-start.5 = (f32[16,128]{1,0:T(8,128)S(1)}, f32[16,128]{1,0:T(8,128)S(1)}, u32[]{:S(2)}, u32[]{:S(2)}) collective-permute-start(f32[16,128]{1,0:T(8,128)S(1)} %get-tuple-element.27), channel_id=1, source_target_pairs={{1,2},{3,4},{5,6},{2,1},{4,3},{6,5},{9,10},{11,12},{13,14},{10,9},... | collective-permute-start | bytes 24584 | tf_op jit(solution)/shard_map/ppermute | solution.py:377
  18.0 1.9 %collective-permute-start.4 = (f32[16,128]{1,0:T(8,128)S(1)}, f32[16,128]{1,0:T(8,128)S(1)}, u32[]{:S(2)}, u32[]{:S(2)}) collective-permute-start(f32[16,128]{1,0:T(8,128)S(1)} %get-tuple-element.27), channel_id=1, source_target_pairs={{0,1},{1,0},{2,3},{3,2},{4,5},{5,4},{6,7},{7,6},{8,9},{9,8},{10,11... | collective-permute-start | bytes 24584 | tf_op jit(solution)/shard_map/ppermute | solution.py:375
  19.9 5.1 %collective-permute-start.8 = (f32[80,256]{1,0:T(8,128)S(1)}, f32[80,256]{1,0:T(8,128)S(1)}, u32[]{:S(2)}, u32[]{:S(2)}) collective-permute-start(f32[80,256]{1,0:T(8,128)S(1)} %edges.3), channel_id=1, source_target_pairs={{0,24},{8,0},{16,8},{24,16},{1,25},{9,1},{17,9},{25,17},{2,26},{10... | collective-permute-start | bytes 245768 | tf_op jit(solution)/shard_map/ppermute | solution.py:364
  22.7 7.8 %collective-permute-start.7 = (f32[80,256]{1,0:T(8,128)S(1)}, f32[80,256]{1,0:T(8,128)S(1)}, u32[]{:S(2)}, u32[]{:S(2)}) collective-permute-start(f32[80,256]{1,0:T(8,128)S(1)} %edges.3), channel_id=1, source_target_pairs={{0,8},{8,16},{16,24},{24,0},{1,9},{9,17},{17,25},{25,1},{2,10},{10... | collective-permute-start | bytes 245768 | tf_op jit(solution)/shard_map/ppermute | solution.py:364
  22.7 7.8 %collective-permute-start.6 = (f32[80,256]{1,0:T(8,128)S(1)}, f32[80,256]{1,0:T(8,128)S(1)}, u32[]{:S(2)}, u32[]{:S(2)}) collective-permute-start(f32[80,256]{1,0:T(8,128)S(1)} %edges.3), channel_id=1, source_target_pairs={{0,16},{8,24},{16,0},{24,8},{1,17},{9,25},{17,1},{25,9},{2,18},{10... | collective-permute-start | bytes 245768 | tf_op jit(solution)/shard_map/ppermute | solution.py:364
  30.5 7.1 %collective-permute-start.11 = (f32[80,256]{1,0:T(8,128)S(1)}, f32[80,256]{1,0:T(8,128)S(1)}, u32[]{:S(2)}, u32[]{:S(2)}) collective-permute-start(f32[80,256]{1,0:T(8,128)S(1)} %add_add_fusion.2.own), channel_id=1, source_target_pairs={{0,96},{32,0},{64,32},{96,64},{1,97},{33,1},{65,33},{97,65},{2,98}... | collective-permute-start | bytes 245768 | tf_op jit(solution)/shard_map/ppermute | solution.py:364
  33.6 6.8 %collective-permute-start.10 = (f32[80,256]{1,0:T(8,128)S(1)}, f32[80,256]{1,0:T(8,128)S(1)}, u32[]{:S(2)}, u32[]{:S(2)}) collective-permute-start(f32[80,256]{1,0:T(8,128)S(1)} %add_add_fusion.2.own), channel_id=1, source_target_pairs={{0,64},{32,96},{64,0},{96,32},{1,65},{33,97},{65,1},{97,33},{2,66}... | collective-permute-start | bytes 245768 | tf_op jit(solution)/shard_map/ppermute | solution.py:364
  34.2 7.1 %collective-permute-start.9 = (f32[80,256]{1,0:T(8,128)S(1)}, f32[80,256]{1,0:T(8,128)S(1)}, u32[]{:S(2)}, u32[]{:S(2)}) collective-permute-start(f32[80,256]{1,0:T(8,128)S(1)} %add_add_fusion.2.own), channel_id=1, source_target_pairs={{0,32},{32,64},{64,96},{96,0},{1,33},{33,65},{65,97},{97,1},{2,34}... | collective-permute-start | bytes 245768 | tf_op jit(solution)/shard_map/ppermute | solution.py:364
  43.8 4.1 %collective-permute-start.15 = (f32[56,128]{1,0:T(8,128)S(1)}, f32[56,128]{1,0:T(8,128)S(1)}, u32[]{:S(2)}, u32[]{:S(2)}) collective-permute-start(f32[56,128]{1,0:T(8,128)S(1)} %add.53.own), channel_id=1, source_target_pairs={{0,6},{2,0},{4,2},{6,4},{1,7},{3,1},{5,3},{7,5},{8,14},{10,8},{12,... | collective-permute-start | bytes 86024 | tf_op jit(solution)/shard_map/ppermute | solution.py:364
  45.0 5.6 %collective-permute-start.14 = (f32[56,128]{1,0:T(8,128)S(1)}, f32[56,128]{1,0:T(8,128)S(1)}, u32[]{:S(2)}, u32[]{:S(2)}) collective-permute-start(f32[56,128]{1,0:T(8,128)S(1)} %add.53.own), channel_id=1, source_target_pairs={{0,4},{2,6},{4,0},{6,2},{1,5},{3,7},{5,1},{7,3},{8,12},{10,14},{12... | collective-permute-start | bytes 86024 | tf_op jit(solution)/shard_map/ppermute | solution.py:364
  46.4 5.1 %collective-permute-start.13 = (f32[56,128]{1,0:T(8,128)S(1)}, f32[56,128]{1,0:T(8,128)S(1)}, u32[]{:S(2)}, u32[]{:S(2)}) collective-permute-start(f32[56,128]{1,0:T(8,128)S(1)} %add.53.own), channel_id=1, source_target_pairs={{0,2},{2,4},{4,6},{6,0},{1,3},{3,5},{5,7},{7,1},{8,10},{10,12},{12... | collective-permute-start | bytes 86024 | tf_op jit(solution)/shard_map/ppermute | solution.py:364
  53.2 1.8 %collective-permute-start.17 = (f32[16,128]{1,0:T(8,128)S(1)}, f32[16,128]{1,0:T(8,128)S(1)}, u32[]{:S(2)}, u32[]{:S(2)}) collective-permute-start(f32[16,128]{1,0:T(8,128)S(1)} %get-tuple-element.34), channel_id=1, source_target_pairs={{1,2},{3,4},{5,6},{2,1},{4,3},{6,5},{9,10},{11,12},{13,14},{10,9},... | collective-permute-start | bytes 24584 | tf_op jit(solution)/shard_map/ppermute | solution.py:377
  53.8 2.0 %collective-permute-start.16 = (f32[16,128]{1,0:T(8,128)S(1)}, f32[16,128]{1,0:T(8,128)S(1)}, u32[]{:S(2)}, u32[]{:S(2)}) collective-permute-start(f32[16,128]{1,0:T(8,128)S(1)} %get-tuple-element.34), channel_id=1, source_target_pairs={{0,1},{1,0},{2,3},{3,2},{4,5},{5,4},{6,7},{7,6},{8,9},{9,8},{10,11... | collective-permute-start | bytes 24584 | tf_op jit(solution)/shard_map/ppermute | solution.py:375
  55.9 5.2 %collective-permute-start.20 = (f32[80,256]{1,0:T(8,128)S(1)}, f32[80,256]{1,0:T(8,128)S(1)}, u32[]{:S(2)}, u32[]{:S(2)}) collective-permute-start(f32[80,256]{1,0:T(8,128)S(1)} %edges.4), channel_id=1, source_target_pairs={{0,24},{8,0},{16,8},{24,16},{1,25},{9,1},{17,9},{25,17},{2,26},{10... | collective-permute-start | bytes 245768 | tf_op jit(solution)/shard_map/ppermute | solution.py:364
  57.6 8.1 %collective-permute-start.19 = (f32[80,256]{1,0:T(8,128)S(1)}, f32[80,256]{1,0:T(8,128)S(1)}, u32[]{:S(2)}, u32[]{:S(2)}) collective-permute-start(f32[80,256]{1,0:T(8,128)S(1)} %edges.4), channel_id=1, source_target_pairs={{0,8},{8,16},{16,24},{24,0},{1,9},{9,17},{17,25},{25,1},{2,10},{10... | collective-permute-start | bytes 245768 | tf_op jit(solution)/shard_map/ppermute | solution.py:364
  57.9 7.9 %collective-permute-start.18 = (f32[80,256]{1,0:T(8,128)S(1)}, f32[80,256]{1,0:T(8,128)S(1)}, u32[]{:S(2)}, u32[]{:S(2)}) collective-permute-start(f32[80,256]{1,0:T(8,128)S(1)} %edges.4), channel_id=1, source_target_pairs={{0,16},{8,24},{16,0},{24,8},{1,17},{9,25},{17,1},{25,9},{2,18},{10... | collective-permute-start | bytes 245768 | tf_op jit(solution)/shard_map/ppermute | solution.py:364
  65.8 5.4 %collective-permute-start.23 = (f32[80,256]{1,0:T(8,128)S(1)}, f32[80,256]{1,0:T(8,128)S(1)}, u32[]{:S(2)}, u32[]{:S(2)}) collective-permute-start(f32[80,256]{1,0:T(8,128)S(1)} %add_add_fusion.1.own), channel_id=1, source_target_pairs={{0,96},{32,0},{64,32},{96,64},{1,97},{33,1},{65,33},{97,65},{2,98}... | collective-permute-start | bytes 245768 | tf_op jit(solution)/shard_map/ppermute | solution.py:364
  66.6 6.4 %collective-permute-start.22 = (f32[80,256]{1,0:T(8,128)S(1)}, f32[80,256]{1,0:T(8,128)S(1)}, u32[]{:S(2)}, u32[]{:S(2)}) collective-permute-start(f32[80,256]{1,0:T(8,128)S(1)} %add_add_fusion.1.own), channel_id=1, source_target_pairs={{0,64},{32,96},{64,0},{96,32},{1,65},{33,97},{65,1},{97,33},{2,66}... | collective-permute-start | bytes 245768 | tf_op jit(solution)/shard_map/ppermute | solution.py:364
  67.4 6.6 %collective-permute-start.21 = (f32[80,256]{1,0:T(8,128)S(1)}, f32[80,256]{1,0:T(8,128)S(1)}, u32[]{:S(2)}, u32[]{:S(2)}) collective-permute-start(f32[80,256]{1,0:T(8,128)S(1)} %add_add_fusion.1.own), channel_id=1, source_target_pairs={{0,32},{32,64},{64,96},{96,0},{1,33},{33,65},{65,97},{97,1},{2,34}... | collective-permute-start | bytes 245768 | tf_op jit(solution)/shard_map/ppermute | solution.py:364
  76.5 4.0 %collective-permute-start.27 = (f32[64,128]{1,0:T(8,128)S(1)}, f32[64,128]{1,0:T(8,128)S(1)}, u32[]{:S(2)}, u32[]{:S(2)}) collective-permute-start(f32[64,128]{1,0:T(8,128)S(1)} %add.57.own), channel_id=1, source_target_pairs={{0,6},{2,0},{4,2},{6,4},{1,7},{3,1},{5,3},{7,5},{8,14},{10,8},{12,... | collective-permute-start | bytes 98312 | tf_op jit(solution)/shard_map/ppermute | solution.py:364
  77.6 5.6 %collective-permute-start.26 = (f32[64,128]{1,0:T(8,128)S(1)}, f32[64,128]{1,0:T(8,128)S(1)}, u32[]{:S(2)}, u32[]{:S(2)}) collective-permute-start(f32[64,128]{1,0:T(8,128)S(1)} %add.57.own), channel_id=1, source_target_pairs={{0,4},{2,6},{4,0},{6,2},{1,5},{3,7},{5,1},{7,3},{8,12},{10,14},{12... | collective-permute-start | bytes 98312 | tf_op jit(solution)/shard_map/ppermute | solution.py:364
  79.7 5.1 %collective-permute-start.25 = (f32[64,128]{1,0:T(8,128)S(1)}, f32[64,128]{1,0:T(8,128)S(1)}, u32[]{:S(2)}, u32[]{:S(2)}) collective-permute-start(f32[64,128]{1,0:T(8,128)S(1)} %add.57.own), channel_id=1, source_target_pairs={{0,2},{2,4},{4,6},{6,0},{1,3},{3,5},{5,7},{7,1},{8,10},{10,12},{12... | collective-permute-start | bytes 98312 | tf_op jit(solution)/shard_map/ppermute | solution.py:364
  87.1 1.5 %collective-permute-start.28 = (f32[16,128]{1,0:T(8,128)S(1)}, f32[16,128]{1,0:T(8,128)S(1)}, u32[]{:S(2)}, u32[]{:S(2)}) collective-permute-start(f32[16,128]{1,0:T(8,128)S(1)} %get-tuple-element.41), channel_id=1, source_target_pairs={{0,1},{1,0},{2,3},{3,2},{4,5},{5,4},{6,7},{7,6},{8,9},{9,8},{10,11... | collective-permute-start | bytes 24584 | tf_op jit(solution)/shard_map/ppermute | solution.py:375
  88.7 5.4 %collective-permute-start.32 = (f32[80,256]{1,0:T(8,128)S(1)}, f32[80,256]{1,0:T(8,128)S(1)}, u32[]{:S(2)}, u32[]{:S(2)}) collective-permute-start(f32[80,256]{1,0:T(8,128)S(1)} %edges.5), channel_id=1, source_target_pairs={{0,24},{8,0},{16,8},{24,16},{1,25},{9,1},{17,9},{25,17},{2,26},{10... | collective-permute-start | bytes 245768 | tf_op jit(solution)/shard_map/ppermute | solution.py:364
  91.2 8.0 %collective-permute-start.31 = (f32[80,256]{1,0:T(8,128)S(1)}, f32[80,256]{1,0:T(8,128)S(1)}, u32[]{:S(2)}, u32[]{:S(2)}) collective-permute-start(f32[80,256]{1,0:T(8,128)S(1)} %edges.5), channel_id=1, source_target_pairs={{0,8},{8,16},{16,24},{24,0},{1,9},{9,17},{17,25},{25,1},{2,10},{10... | collective-permute-start | bytes 245768 | tf_op jit(solution)/shard_map/ppermute | solution.py:364
  91.2 8.0 %collective-permute-start.30 = (f32[80,256]{1,0:T(8,128)S(1)}, f32[80,256]{1,0:T(8,128)S(1)}, u32[]{:S(2)}, u32[]{:S(2)}) collective-permute-start(f32[80,256]{1,0:T(8,128)S(1)} %edges.5), channel_id=1, source_target_pairs={{0,16},{8,24},{16,0},{24,8},{1,17},{9,25},{17,1},{25,9},{2,18},{10... | collective-permute-start | bytes 245768 | tf_op jit(solution)/shard_map/ppermute | solution.py:364
  99.2 5.2 %collective-permute-start.35 = (f32[80,256]{1,0:T(8,128)S(1)}, f32[80,256]{1,0:T(8,128)S(1)}, u32[]{:S(2)}, u32[]{:S(2)}) collective-permute-start(f32[80,256]{1,0:T(8,128)S(1)} %add_add_fusion.own), channel_id=1, source_target_pairs={{0,96},{32,0},{64,32},{96,64},{1,97},{33,1},{65,33},{97,65},{2,98}... | collective-permute-start | bytes 245768 | tf_op jit(solution)/shard_map/ppermute | solution.py:364
  101.0 6.3 %collective-permute-start.34 = (f32[80,256]{1,0:T(8,128)S(1)}, f32[80,256]{1,0:T(8,128)S(1)}, u32[]{:S(2)}, u32[]{:S(2)}) collective-permute-start(f32[80,256]{1,0:T(8,128)S(1)} %add_add_fusion.own), channel_id=1, source_target_pairs={{0,64},{32,96},{64,0},{96,32},{1,65},{33,97},{65,1},{97,33},{2,66}... | collective-permute-start | bytes 245768 | tf_op jit(solution)/shard_map/ppermute | solution.py:364
  101.9 6.2 %collective-permute-start.33 = (f32[80,256]{1,0:T(8,128)S(1)}, f32[80,256]{1,0:T(8,128)S(1)}, u32[]{:S(2)}, u32[]{:S(2)}) collective-permute-start(f32[80,256]{1,0:T(8,128)S(1)} %add_add_fusion.own), channel_id=1, source_target_pairs={{0,32},{32,64},{64,96},{96,0},{1,33},{33,65},{65,97},{97,1},{2,34}... | collective-permute-start | bytes 245768 | tf_op jit(solution)/shard_map/ppermute | solution.py:364
  (11 other events, 35.6 us)

commit v3 on v2

--- a/solution.py
+++ b/solution.py
@@ -75,8 +75,20 @@
     return state[start : start + rows, lanes]
 
 
-def row_numbers(rows):
-    return lax.broadcasted_iota(jnp.int32, (rows, CHUNK), 0).astype(f32).astype(bf16)
+GHOST_PLACES = ((SCALAR, 8), (SCALAR, 32), (SCALAR, 56), (BEFORE, 56))
+
+
+def put_ghosts(state, ghosts):
+    for at, (lanes, start) in enumerate(GHOST_PLACES):
+        put(state, lanes, start, ghosts[:, 128 * at : 128 * at + 128])
+
+
+def get_ghosts(state):
+    return jnp.concatenate([get(state, lanes, start, 24) for lanes, start in GHOST_PLACES], axis=1)
+
+
+def row_numbers(rows, lanes=CHUNK):
+    return lax.broadcasted_iota(jnp.int32, (rows, lanes), 0).astype(f32).astype(bf16)
 
 
 def hot_rows(numbers, lane_row):
@@ -147,6 +159,58 @@
             work[row : row + 8, at] = weight * h
 
 
+def ghost_kernel(count_ref, flat_ref, source_ref, g_ref, work, earlier_ref, later_ref):
+    knot = flat_ref[...]
+    order = lax.broadcasted_iota(jnp.int32, (32, 128), 0) * 128 + lax.broadcasted_iota(jnp.int32, (32, 128), 1)
+    live = order < count_ref[0]
+    across = jnp.where(
+        lax.broadcasted_iota(jnp.int32, (128, 128), 0) < lax.broadcasted_iota(jnp.int32, (128, 128), 1), 1.0, 0.0
+    ).astype(bf16)
+    down = jnp.where(
+        lax.broadcasted_iota(jnp.int32, (32, 32), 0) > lax.broadcasted_iota(jnp.int32, (32, 32), 1), 1.0, 0.0
+    ).astype(bf16)
+    numbers = row_numbers(256, 128)
+    for chosen, spread_at, ref in ((live & (knot >= 4093), 104, later_ref), (live & (knot < 3), 40, earlier_ref)):
+        mark = jnp.where(chosen, 1.0, 0.0).astype(bf16)
+        rank = dot_nn(mark, across) + jnp.sum(dot_nn(down, mark), axis=1, keepdims=True)
+        rank = jnp.where(chosen, rank, -1.0)
+        total = jnp.zeros((72, 256), f32)
+        for at in chunks():
+            first = at.start // 128
+            slots = jnp.concatenate([hot_rows(numbers, rank[row : row + 1]) for row in range(first, first + CHUNK // 128)], axis=1)
+            data = jnp.concatenate(
+                [work[spread_at : spread_at + 16, at], g_ref[:, at], source_ref[:, at].astype(f32), work[IMAGE, at], jnp.zeros((1, CHUNK), f32)],
+                axis=0,
+            )
+            total = total + dot_nt(split_rows(data), slots)
+        ref[...] = join_rows(total)
+
+
+def ghost_sums(solved, ghosts, values):
+    source = ghosts[21:22].astype(jnp.int32)
+    picked = join_rows(dot_nn(solved, hot_rows(row_numbers(128, 512), (source & 127).astype(f32))))
+    fitted = functools.reduce(jnp.add, [tile(picked, j) * ghosts[16 + j : 17 + j] for j in range(5)])
+    fitted = jnp.where(lax.broadcasted_iota(jnp.int32, (8, 512), 0) == (source >> 7), fitted, 0.0)
+    weighted = ghosts[0:16] * (values - jnp.sum(fitted, axis=0, keepdims=True))
+    return jnp.sum(weighted[:, 0:256], axis=1, keepdims=True), jnp.sum(weighted[:, 256:512], axis=1, keepdims=True)
+
+
+def end_tile(at_tm, high, low):
+    lane = lax.broadcasted_iota(jnp.int32, (8, 128), 1)
+    result = jnp.zeros((8, 128), f32)
+    for place, part in enumerate((high[0:8], high[8:16], low[0:8], low[8:16])):
+        result = jnp.where(lane == at_tm + 16 * place, part, result)
+    return result
+
+
+def end_parts(at_tm, ends):
+    lane = lax.broadcasted_iota(jnp.int32, (8, 128), 1)
+    pick = lambda at: jnp.sum(jnp.where(lane == at, ends, 0.0), axis=1, keepdims=True)
+    earlier = jnp.concatenate([pick(at_tm - 1), pick(at_tm + 15)], axis=0)
+    later = jnp.concatenate([pick(at_tm + 33), pick(at_tm + 49)], axis=0)
+    return earlier, later
+
+
 def tile(value, at):
     return value[8 * at : 8 * at + 8]
 
@@ -186,7 +250,6 @@
 
 
 def eliminate_and_spread(solved, work):
-    solved = split_rows(jnp.concatenate(solved, axis=0))
     source_numbers, knot_numbers = row_numbers(128), row_numbers(256)
     total = jnp.zeros((240, 256), f32)
     for at in chunks():
@@ -197,52 +260,67 @@
     return join_rows(total)
 
 
-def put_knots(total, energy, knots_ref, edge_ref):
-    knots_ref[0:72] = total[0:72]
-    if energy is None:
-        tail = total[76:80]
-    else:
-        tail = jnp.concatenate([energy[0:4], energy[4:8]], axis=1)
-    knots_ref[72:80] = jnp.concatenate([total[72:76], tail], axis=0)
-    lane = lax.broadcasted_iota(jnp.int32, (16, 128), 1)
-    edge_ref[...] = jnp.where(lane == 127, total[64:80, 128:256], jnp.where(lane == 0, total[0:16, 0:128], 0.0))
-
-
-def first_kernel(own, one, two, three, _work, _state, knots_ref, edge_ref, work, state):
+def with_ends(total, earlier, later, energy):
+    lane = lax.broadcasted_iota(jnp.int32, (16, 256), 1)
+    within = lax.broadcasted_iota(jnp.int32, (16, 256), 0) < 12
+    low = total[0:16] + jnp.where(within & (lane == 0), earlier, 0.0)
+    high = total[64:80] + jnp.where(within & (lane == 255), later, 0.0)
+    if energy is not None:
+        high = jnp.concatenate([high[0:12], jnp.concatenate([energy[0:4], energy[4:8]], axis=1)], axis=0)
+    return jnp.concatenate([low, total[16:64], high], axis=0)
+
+
+def first_kernel(own, one, two, three, earlier_ref, later_ref, _work, _state, knots_ref, work, state):
     sums = four((own, one, two, three))
     factor = factorize(factor_of(sums))
     stacked = jnp.concatenate([factor[pair] for pair in entry_pairs], axis=0)
     put(state, FACTOR_A, 0, stacked[0:80])
     put(state, FACTOR_B, 0, stacked[80:120])
     put(state, FACTOR_B, 40, sums[120:160])
-    solved = chol_solve(factor, [tile(sums, 15 + j) for j in range(5)])
-    put_knots(eliminate_and_spread(solved, work), None, knots_ref, edge_ref)
+    ghosts = jnp.concatenate([earlier_ref[...], later_ref[...]], axis=1)
+    put_ghosts(state, ghosts)
+    solved = split_rows(jnp.concatenate(chol_solve(factor, [tile(sums, 15 + j) for j in range(5)]), axis=0))
+    earlier, later = ghost_sums(solved, ghosts, ghosts[22:23])
+    knots_ref[...] = with_ends(eliminate_and_spread(solved, work), earlier, later, None)
 
 
 def kept_factor(state):
     return factor_of(jnp.concatenate([get(state, FACTOR_A, 0, 80), get(state, FACTOR_B, 0, 40)], axis=0))
 
 
-def back_kernel(lanes, own, one, two, three, _work, _state, knots_ref, edge_ref, work, state):
-    sums = four((own, one, two, three))
-    put(state, lanes, 0, sums)
+def back(lanes, at_tm, parts, work, state):
+    sums = four(parts)
+    put(state, lanes, 0, sums[:-8])
     target = [tile(sums, j) for j in range(5)]
     solved = chol_solve(kept_factor(state), target)
     energy = tile(sums, 5)
     for j in range(5):
         energy = energy - target[j] * solved[j]
-    put_knots(eliminate_and_spread(solved, work), energy, knots_ref, edge_ref)
-
-
-def edge_kernel(odd_ref, _knots, twin_ref, other_ref, knots_ref):
-    odd = odd_ref[0] == 1
-    twin, other = twin_ref[...], other_ref[...]
-    earlier = pltpu.roll(jnp.where(odd, twin, other), 1, 1)
-    later = pltpu.roll(jnp.where(odd, other, twin), 127, 1)
-    lane = lax.broadcasted_iota(jnp.int32, (16, 128), 1)
-    within = lax.broadcasted_iota(jnp.int32, (16, 128), 0) < 12
-    knots_ref[0:16, 0:128] += jnp.where(within & (lane == 0), earlier, 0.0)
-    knots_ref[64:80, 128:256] += jnp.where(within & (lane == 127), later, 0.0)
+    solved = split_rows(jnp.concatenate(solved, axis=0))
+    ends = zip(ghost_sums(solved, get_ghosts(state), 0.0), end_parts(at_tm, sums[-8:]))
+    earlier, later = (ghost + image for ghost, image in ends)
+    return with_ends(eliminate_and_spread(solved, work), earlier, later, energy), energy
+
+
+def back_kernel(tm_ref, own, one, two, three, _work, _state, knots_ref, work, state):
+    knots_ref[...], _ = back(BEFORE, tm_ref[0], (own, one, two, three), work, state)
+
+
+def back_to_owners_kernel(tm_ref, own, one, two, three, _work, _state, blocks_ref, work, state):
+    knots, energy = back(AFTER, tm_ref[0], (own, one, two, three), work, state)
+    knots = assembled(knots)
+    place = lax.broadcasted_iota(jnp.int32, (8, 128), 1) >> 4
+    for owner in range(16):
+        half = slice(128 * (owner // 8), 128 * (owner // 8) + 128)
+        block = jnp.zeros((8, 128), f32)
+        for q in range(8):
+            block = jnp.where(place == q, moved(knots[8 * q : 8 * q + 8, half], (16 * (q - owner)) % 128), block)
+        blocks_ref[owner, 0:8] = block
+        blocks_ref[owner, 8:16] = energy
+
+
+def moved(value, lanes):
+    return value if isinstance(lanes, int) and lanes == 0 else pltpu.roll(value, lanes, 1)
 
 
 def assembled(knots):
@@ -264,30 +342,38 @@
     return functools.reduce(jnp.add, [tile(product, at) for at in range(8)])
 
 
-def gather_and_sum(field, work):
+def lane_blocks(value):
+    return functools.reduce(jnp.add, [value[:, start : start + 128] for start in range(0, CHUNK, 128)])
+
+
+def gather_and_sum(at_tm, field, work):
     source_numbers, knot_numbers = row_numbers(128), row_numbers(256)
     parts = split_rows(field)
     total = jnp.zeros((120, 128), f32)
     square = jnp.zeros((1, 128), f32)
+    high = jnp.zeros((16, 128), f32)
+    low = jnp.zeros((16, 128), f32)
     for at in chunks():
-        picked = join_rows(dot_nn(parts, hot_rows(knot_numbers, work[KNOT_LANE, at])))
+        knot_lane = work[KNOT_LANE, at]
+        picked = join_rows(dot_nn(parts, hot_rows(knot_numbers, knot_lane)))
         image = jnp.sum(picked * work[KNOT_SPREAD, at], axis=0, keepdims=True)
         work[IMAGE, at] = image
-        for start in range(0, CHUNK, 128):
-            piece = image[:, start : start + 128]
-            square = square + piece * piece
+        square = square + lane_blocks(image * image)
+        high = high + lane_blocks(work[104:120, at] * jnp.where(knot_lane == 255.0, image, 0.0))
+        low = low + lane_blocks(work[40:56, at] * jnp.where(knot_lane == 0.0, image, 0.0))
         total = total + dot_nt(split_rows(work[SOURCE_SPREAD, at] * image), hot_rows(source_numbers, work[SOURCE_LANE, at]))
-    return join_rows(total), jnp.concatenate([square, jnp.zeros((7, 128), f32)], axis=0)
-
-
-def start_kernel(own, one, two, three, _work, _state, sums_ref, work, state):
+    ends = end_tile(at_tm, jnp.sum(high, axis=1, keepdims=True), jnp.sum(low, axis=1, keepdims=True))
+    return join_rows(total), jnp.concatenate([square, jnp.zeros((7, 128), f32)], axis=0), ends
+
+
+def start_kernel(tm_ref, own, one, two, three, _work, _state, sums_ref, work, state):
     residual = assembled(four((own, one, two, three)))
     put(state, START, 0, residual)
-    sums, square = gather_and_sum(residual, work)
-    sums_ref[...] = jnp.concatenate([sums, square, folded(residual, residual)], axis=0)
-
-
-def next_kernel(own, one, two, three, _work, _state, sums_ref, work, state):
+    sums, square, ends = gather_and_sum(tm_ref[0], residual, work)
+    sums_ref[...] = jnp.concatenate([sums, square, folded(residual, residual), ends], axis=0)
+
+
+def next_kernel(tm_ref, own, one, two, three, _work, _state, sums_ref, work, state):
     knots = four((own, one, two, three))
     direction = get(state, START, 0, 80)
     mapped = assembled(knots) + damping * direction
@@ -297,14 +383,26 @@
     put(state, MAPPED, 0, mapped)
     put(state, RESIDUAL, 0, residual)
     put(state, SCALAR, 0, jnp.zeros((8, 128), f32) + product)
-    sums, square = gather_and_sum(residual, work)
-    sums_ref[...] = jnp.concatenate([sums, square, folded(residual, residual), folded(residual, mapped)], axis=0)
-
-
-def last_kernel(place_ref, own, one, two, three, state, solution_ref, left_ref, source_ref):
-    knots = four((own, one, two, three))
-    residual = get(state, RESIDUAL, 0, 64)
-    image = assembled(knots)[0:64] + damping * residual
+    sums, square, ends = gather_and_sum(tm_ref[0], residual, work)
+    sums_ref[...] = jnp.concatenate([sums, square, folded(residual, residual), folded(residual, mapped), ends], axis=0)
+
+
+def last_kernel(place_ref, blocks_ref, state, solution_ref, left_ref, source_ref):
+    place = place_ref[0]
+    blocks = functools.reduce(jnp.add, [blocks_ref[at] for at in range(16)])
+    lane_place = lax.broadcasted_iota(jnp.int32, (8, 128), 1) >> 4
+
+    def own_lanes(lanes):
+        result = jnp.zeros((8, 128), f32)
+        for q in range(8):
+            rows = get(state, lanes, 8 * q, 8)
+            rows = jnp.where(place >= 8, rows[:, 128:256], rows[:, 0:128])
+            rows = pltpu.roll(rows, (16 * (q - place)) & 127, 1)
+            result = jnp.where(lane_place == q, rows, result)
+        return result
+
+    start, mapped, residual = own_lanes(START), own_lanes(MAPPED), own_lanes(RESIDUAL)
+    image = blocks[0:8] + damping * residual
     before, after = get(state, BEFORE, 0, 56), get(state, AFTER, 0, 64)
     norm_first = jnp.sum(before[48:56])
     product_first = jnp.max(get(state, SCALAR, 0, 8))
@@ -312,23 +410,21 @@
     norm_now = jnp.sum(after[48:56])
     crossed = jnp.sum(after[56:64])
     beta = norm_now / norm_first
-    product = energy_of(knots) + damping * norm_now + beta * (2.0 * crossed + beta * product_first)
+    product = jnp.sum(blocks[8:16]) + damping * norm_now + beta * (2.0 * crossed + beta * product_first)
     alpha = norm_now / product
     from_start = alpha_first + alpha * beta
-    solution = from_start * get(state, START, 0, 64) + alpha * residual
-    left = residual - alpha * (image + beta * get(state, MAPPED, 0, 64))
+    solution = from_start * start + alpha * residual
+    left = residual - alpha * (image + beta * mapped)
     both = split_rows(jnp.concatenate([solution, left], axis=0))
-    row = lax.broadcasted_iota(jnp.int32, (256, 256), 0)
-    lane = lax.broadcasted_iota(jnp.int32, (256, 256), 1)
-    chosen = jnp.where(row == place_ref[0] * 16 + (lane >> 4), 1.0, 0.0).astype(bf16)
-    picked = join_rows(dot_nn(both, chosen))
-    low = lax.broadcasted_iota(jnp.int32, (8, 256), 1) & 15
-    upper = lax.broadcasted_iota(jnp.int32, (8, 256), 0) >> 2
+    held = lax.broadcasted_iota(jnp.int32, (128, 256), 0)
+    wanted = lax.broadcasted_iota(jnp.int32, (128, 256), 1)
+    same = (held & 15) == (wanted >> 4)
+    halves = [
+        join_rows(dot_nn(both, jnp.where(same & ((wanted & 15) == 2 * (held >> 4) + upper), 1.0, 0.0).astype(bf16)))
+        for upper in range(2)
+    ]
     for at, ref in enumerate((solution_ref, left_ref)):
-        own_rows = jnp.zeros((8, 256), f32)
-        for q in range(8):
-            own_rows = jnp.where(low == upper + 2 * q, tile(picked, 8 * at + q), own_rows)
-        own_rows = own_rows[0:4] + own_rows[4:8]
+        own_rows = halves[0][8 * at : 8 * at + 4] + halves[1][8 * at + 4 : 8 * at + 8]
         for c in range(4):
             ref[c] = own_rows[c : c + 1]
     rhs = get(state, FACTOR_B, 40, 40)
@@ -365,30 +461,30 @@
     ]
 
 
+def shifted(value, step):
+    count = lax.axis_size(TM)
+    return lax.ppermute(value, TM, [(at, at + step) for at in range(count) if 0 <= at + step < count])
+
+
 def tm_parts(value):
     value = value + lax.ppermute(value, "tm_1", [(0, 1), (1, 0)])
     return ring_parts(value, "tm_0")
 
 
-def sky_parts(knots, edge, odd):
-    count = lax.axis_size(TM)
-    twin = lax.ppermute(edge, "tm_1", [(0, 1), (1, 0)])
-    swaps = [(low, low + 1) for low in range(1, count - 1, 2)]
-    other = lax.ppermute(edge, TM, swaps + [(high, low) for low, high in swaps])
-    (knots,) = call(edge_kernel, "edges", [KNOTS], odd, knots, twin, other, scalars=1, aliases={1: 0})
+def sky_parts(knots):
     own, one, two, three = ring_parts(knots, "sky_1")
     return ring_parts((own + two) + (one + three), "sky_0")
 
 
 KNOTS = ((80, 256), f32)
-EDGE = ((16, 128), f32)
+GHOSTS = ((24, 256), f32)
 
 
 def shards(obs_source, obs_knot, obs_count, src_design, att_design, obs_phase, obs_value, src_prior):
     at = lax.axis_index(TM)
     first = (at == 0).astype(jnp.int32).reshape(1)
     last = (at == lax.axis_size(TM) - 1).astype(jnp.int32).reshape(1)
-    odd = (at % 2).astype(jnp.int32).reshape(1)
+    tm = at.astype(jnp.int32).reshape(1)
     place = lax.axis_index(SKY).astype(jnp.int32).reshape(1)
     line = lambda value: value.reshape(1, OBS_DEV)
     (state,) = call(open_kernel, "open", [STATE], work_ahead=1 << 32)
@@ -409,30 +505,34 @@
         scalars=2,
         aliases={5: 0},
     )
-    there = [KNOTS, EDGE, WORK, STATE]
-    knots, edge, work, state = call(first_kernel, "first", there, *parts, work, state, aliases={4: 2, 5: 3})
-    parts = sky_parts(knots, edge, odd)
-    sums, work, state = call(
-        start_kernel, "start", [((56, 128), f32), WORK, STATE], *parts, work, state, aliases={4: 1, 5: 2}
-    )
+    earlier, later = call(
+        ghost_kernel,
+        "ghosts",
+        [GHOSTS, GHOSTS],
+        obs_count, obs_knot.reshape(32, 128), line(obs_source), src_design, work,
+        scalars=1,
+    )
+    ends = (shifted(later, 1), shifted(earlier, -1))
+    knots, work, state = call(
+        first_kernel, "first", [KNOTS, WORK, STATE], *parts, *ends, work, state, aliases={6: 1, 7: 2}
+    )
+    parts = sky_parts(knots)
+    kept = dict(scalars=1, aliases={5: 1, 6: 2})
+    sums, work, state = call(start_kernel, "start", [((64, 128), f32), WORK, STATE], tm, *parts, work, state, **kept)
     parts = tm_parts(sums)
-    knots, edge, work, state = call(
-        functools.partial(back_kernel, BEFORE), "back", there, *parts, work, state, aliases={4: 2, 5: 3}
-    )
-    parts = sky_parts(knots, edge, odd)
-    sums, work, state = call(
-        next_kernel, "next", [((64, 128), f32), WORK, STATE], *parts, work, state, aliases={4: 1, 5: 2}
-    )
+    knots, work, state = call(back_kernel, "back", [KNOTS, WORK, STATE], tm, *parts, work, state, **kept)
+    parts = sky_parts(knots)
+    sums, work, state = call(next_kernel, "next", [((72, 128), f32), WORK, STATE], tm, *parts, work, state, **kept)
     parts = tm_parts(sums)
-    knots, edge, work, state = call(
-        functools.partial(back_kernel, AFTER), "back_again", there, *parts, work, state, aliases={4: 2, 5: 3}
-    )
-    parts = sky_parts(knots, edge, odd)
+    blocks, work, state = call(
+        back_to_owners_kernel, "back_to_owners", [((16, 16, 128), f32), WORK, STATE], tm, *parts, work, state, **kept
+    )
+    blocks = lax.all_to_all(blocks, SKY, 0, 0, tiled=True)
     return call(
         last_kernel,
         "last",
         [((4, 1, 256), f32), ((4, 1, 256), f32), ((5, 1024), f32)],
-        place, *parts, state,
+        place, blocks, state,
         scalars=1,
     )
 

time: 109 us -> 96.6 us (0.89)
  waiting for transfers between devices: 56.9 us -> 45.5 us
  starting transfers between devices: 39.9 us -> 36.2 us
  Pallas kernels: 10.6 us -> 12.9 us
    ppermute x27 -> x21, waiting for transfers between devices: 50.8 us -> 29.7 us  [ring_parts(): lax.ppermute(value, axis, [(at, (at + step) % count) for at in range(coun...]
    all_to_all x0 -> x1, waiting for transfers between devices: none -> 7.98 us  [shards(): blocks = lax.all_to_all(blocks, SKY, 0, 0, tiled=True)]
    ppermute x27 -> x21, starting transfers between devices: 34.8 us -> 28 us  [ring_parts(): lax.ppermute(value, axis, [(at, (at + step) % count) for at in range(coun...]
    all_to_all x0 -> x1, starting transfers between devices: none -> 5.25 us  [shards(): blocks = lax.all_to_all(blocks, SKY, 0, 0, tiled=True)]
    pallas_call x12 -> x10, Pallas kernels: 10.6 us -> 12.9 us  [call(): pl.pallas_call(kernel, out_shape=shapes, in_specs=specs, out_specs=[VMEM]...]
    ppermute x6 -> x2, starting transfers between devices: 4.81 us -> 2.58 us  [shifted(): lax.ppermute(value, TM, [(at, at + step) for at in range(count) if 0 <= a...]
    ppermute x6 -> x2, waiting for transfers between devices: 2.48 us -> 4.24 us  [shifted(): lax.ppermute(value, TM, [(at, at + step) for at in range(count) if 0 <= a...]
  transfers between devices with their start and end apart: 36 -> 27, of which waited for: 29 -> 20; matrix products, arithmetic and copies ran while one was open for 0% -> 0% of each run, Pallas kernels for 0% -> 2%
where the time goes in v3:
time: 96.6 us; the launch traced here: 96.3 us
  waiting for transfers between devices  45.5 us (47%)
  starting transfers between devices  36.2 us (37%)
  Pallas kernels  12.9 us (13%)
  between operations  1.58 us (2%)
    ppermute x21, waiting for transfers between devices, ring_parts(): lax.ppermute(value, axis, [(at, (at + step) % count) for at in range(coun...  29.7 us
    ppermute x21, starting transfers between devices, ring_parts(): lax.ppermute(value, axis, [(at, (at + step) % count) for at in range(coun...  28 us
    pallas_call x10, Pallas kernels, call(): pl.pallas_call(kernel, out_shape=shapes, in_specs=specs, out_specs=[VMEM]...  12.9 us
    all_to_all x1, waiting for transfers between devices, shards(): blocks = lax.all_to_all(blocks, SKY, 0, 0, tiled=True)  7.98 us
    all_to_all x1, starting transfers between devices, shards(): blocks = lax.all_to_all(blocks, SKY, 0, 0, tiled=True)  5.25 us
    ppermute x2, waiting for transfers between devices, shifted(): lax.ppermute(value, TM, [(at, at + step) for at in range(count) if 0 <= a...  4.24 us
    ppermute x3, waiting for transfers between devices, tm_parts(): value = value + lax.ppermute(value, 'tm_1', [(0, 1), (1, 0)])  3.57 us
    ppermute x2, starting transfers between devices, shifted(): lax.ppermute(value, TM, [(at, at + step) for at in range(count) if 0 <= a...  2.58 us
  transfers between devices with their start and end apart: 27, of which 20 were waited for; matrix products, arithmetic and copies ran while one was open for 0% of the time, Pallas kernels for 2%

profile of v3, /device:TPU:0, one launch (start us, length us, event | category | flops | bytes accessed | tf_op | source)
XLA Modules:
  0.0 96.3 jit_solution(17898791115953986868)
XLA Ops:
  1.5 1.2 %source_sums.1 = (f32[128,4096]{1,0:T(8,128)S(1)}, f32[160,128]{1,0:T(8,128)S(1)}, f32[80,1408]{1,0:T(8,128)S(1)}) custom-call(s32[1]{0:T(128)S(6)} %copy.35.count_ref, s32[1]{0:T(128)} %bitcast.2.first_ref, s32[1,4096]{1,0:T(1,128)S(1)} %bitcast.11, f32[5,4096]{1,0:T(8,128)S(1)} %copy-done, ...), custom_call_target="tpu_custom_call", output_to_operand_aliasing={{2}: (6, {})} | custom-call | tf_op jit(solution)/shard_map/source_sums/pallas_call | solution.py:445
  2.9 1.3 %collective-permute-done = f32[160,128]{1,0:T(8,128)S(1)} collective-permute-done((f32[160,128]{1,0:T(8,128)S(1)}, f32[160,128]{1,0:T(8,128)S(1)}, u32[]{:S(2)}, u32[]{:S(2)}) %collective-permute-start) | collective-permute-done | bytes 81952 | tf_op jit(solution)/shard_map/ppermute | solution.py:470
  4.2 4.2 %collective-permute-start.3 = (f32[160,128]{1,0:T(8,128)S(1)}, f32[160,128]{1,0:T(8,128)S(1)}, u32[]{:S(2)}, u32[]{:S(2)}) collective-permute-start(f32[160,128]{1,0:T(8,128)S(1)} %add.35.own), channel_id=1, source_target_pairs={{0,6},{2,0},{4,2},{6,4},{1,7},{3,1},{5,3},{7,5},{8,14},{10,8},{12,... | collective-permute-start | bytes 245768 | tf_op jit(solution)/shard_map/ppermute | solution.py:460
  8.4 1.3 %collective-permute-start.1 = (f32[160,128]{1,0:T(8,128)S(1)}, f32[160,128]{1,0:T(8,128)S(1)}, u32[]{:S(2)}, u32[]{:S(2)}) collective-permute-start(f32[160,128]{1,0:T(8,128)S(1)} %add.35.own), channel_id=1, source_target_pairs={{0,2},{2,4},{4,6},{6,0},{1,3},{3,5},{5,7},{7,1},{8,10},{10,12},{12... | collective-permute-start | bytes 245768 | tf_op jit(solution)/shard_map/ppermute | solution.py:460
  10.1 1.6 %ghosts.1 = (f32[24,256]{1,0:T(8,128)S(1)}, f32[24,256]{1,0:T(8,128)S(1)}) custom-call(s32[1]{0:T(128)S(6)} %copy.35.count_ref, s32[32,128]{1,0:T(8,128)S(1)} %bitcast.10, s32[1,4096]{1,0:T(1,128)S(1)} %bitcast.12, f32[5,4096]{1,0:T(8,128)S(1)} %copy-done, f32[128,4096]{1,0:T(8,128)S(1)} %knot_spread.1.work._work), custom_call_target="tpu_custom_call" | custom-call | tf_op jit(solution)/shard_map/ghosts/pallas_call | solution.py:445
  11.7 1.3 %collective-permute-start.4 = (f32[24,256]{1,0:T(8,128)S(1)}, f32[24,256]{1,0:T(8,128)S(1)}, u32[]{:S(2)}, u32[]{:S(2)}) collective-permute-start(f32[24,256]{1,0:T(8,128)S(1)} %get-tuple-element.24), channel_id=1, source_target_pairs={{0,1},{1,2},{2,3},{3,4},{4,5},{5,6},{6,7},{8,9},{9,10},{10,11},{11... | collective-permute-start | bytes 73736 | tf_op jit(solution)/shard_map/ppermute | solution.py:466
  13.0 1.3 %collective-permute-start.5 = (f32[24,256]{1,0:T(8,128)S(1)}, f32[24,256]{1,0:T(8,128)S(1)}, u32[]{:S(2)}, u32[]{:S(2)}) collective-permute-start(f32[24,256]{1,0:T(8,128)S(1)} %get-tuple-element.25), channel_id=1, source_target_pairs={{1,0},{2,1},{3,2},{4,3},{5,4},{6,5},{7,6},{9,8},{10,9},{11,10},{12... | collective-permute-start | bytes 73736 | tf_op jit(solution)/shard_map/ppermute | solution.py:466
  14.3 4.2 %collective-permute-done.5.later_ref = f32[24,256]{1,0:T(8,128)S(1)} collective-permute-done((f32[24,256]{1,0:T(8,128)S(1)}, f32[24,256]{1,0:T(8,128)S(1)}, u32[]{:S(2)}, u32[]{:S(2)}) %collective-permute-start.5) | collective-permute-done | bytes 24608 | tf_op jit(solution)/shard_map/ppermute | solution.py:466
  18.6 1.8 %first.1 = (f32[80,256]{1,0:T(8,128)S(1)}, f32[128,4096]{1,0:T(8,128)S(1)}, f32[80,1408]{1,0:T(8,128)S(1)}) custom-call(f32[160,128]{1,0:T(8,128)S(1)} %add.35.own, f32[160,128]{1,0:T(8,128)S(1)} %collective-permute-done.1.one, f32[160,128]{1,0:T(8,128)S(1)} %collective-permute-done.2.two, ...), custom_call_target="tpu_custom_call", output_to_operand_aliasing={{1}: (6, {}), {2}: (7, {})} | custom-call | tf_op jit(solution)/shard_map/first/pallas_call | solution.py:445
  20.4 2.8 %collective-permute-start.8 = (f32[80,256]{1,0:T(8,128)S(1)}, f32[80,256]{1,0:T(8,128)S(1)}, u32[]{:S(2)}, u32[]{:S(2)}) collective-permute-start(f32[80,256]{1,0:T(8,128)S(1)} %get-tuple-element.27), channel_id=1, source_target_pairs={{0,24},{8,0},{16,8},{24,16},{1,25},{9,1},{17,9},{25,17},{2,26},{10... | collective-permute-start | bytes 245768 | tf_op jit(solution)/shard_map/ppermute | solution.py:460
  23.2 2.3 %collective-permute-start.6 = (f32[80,256]{1,0:T(8,128)S(1)}, f32[80,256]{1,0:T(8,128)S(1)}, u32[]{:S(2)}, u32[]{:S(2)}) collective-permute-start(f32[80,256]{1,0:T(8,128)S(1)} %get-tuple-element.27), channel_id=1, source_target_pairs={{0,16},{8,24},{16,0},{24,8},{1,17},{9,25},{17,1},{25,9},{2,18},{10... | collective-permute-start | bytes 245768 | tf_op jit(solution)/shard_map/ppermute | solution.py:460
  25.5 4.1 %collective-permute-done.7 = f32[80,256]{1,0:T(8,128)S(1)} collective-permute-done((f32[80,256]{1,0:T(8,128)S(1)}, f32[80,256]{1,0:T(8,128)S(1)}, u32[]{:S(2)}, u32[]{:S(2)}) %collective-permute-start.7) | collective-permute-done | bytes 81952 | tf_op jit(solution)/shard_map/ppermute | solution.py:460
  30.0 3.1 %collective-permute-start.11 = (f32[80,256]{1,0:T(8,128)S(1)}, f32[80,256]{1,0:T(8,128)S(1)}, u32[]{:S(2)}, u32[]{:S(2)}) collective-permute-start(f32[80,256]{1,0:T(8,128)S(1)} %add_add_fusion.1.own), channel_id=1, source_target_pairs={{0,96},{32,0},{64,32},{96,64},{1,97},{33,1},{65,33},{97,65},{2,98}... | collective-permute-start | bytes 245768 | tf_op jit(solution)/shard_map/ppermute | solution.py:460
  35.5 4.4 %collective-permute-done.10.two = f32[80,256]{1,0:T(8,128)S(1)} collective-permute-done((f32[80,256]{1,0:T(8,128)S(1)}, f32[80,256]{1,0:T(8,128)S(1)}, u32[]{:S(2)}, u32[]{:S(2)}) %collective-permute-start.10) | collective-permute-done | bytes 81952 | tf_op jit(solution)/shard_map/ppermute | solution.py:460
  39.9 1.8 %collective-permute-done.9.one = f32[80,256]{1,0:T(8,128)S(1)} collective-permute-done((f32[80,256]{1,0:T(8,128)S(1)}, f32[80,256]{1,0:T(8,128)S(1)}, u32[]{:S(2)}, u32[]{:S(2)}) %collective-permute-start.9) | collective-permute-done | bytes 81952 | tf_op jit(solution)/shard_map/ppermute | solution.py:460
  41.7 1.2 %start.1 = (f32[64,128]{1,0:T(8,128)S(1)}, f32[128,4096]{1,0:T(8,128)S(1)}, f32[80,1408]{1,0:T(8,128)S(1)}) custom-call(s32[1]{0:T(128)} %bitcast.1.tm_ref, f32[80,256]{1,0:T(8,128)S(1)} %add_add_fusion.1.own, f32[80,256]{1,0:T(8,128)S(1)} %collective-permute-done.9.one, ...), custom_call_target="tpu_custom_call", output_to_operand_aliasing={{1}: (5, {}), {2}: (6, {})} | custom-call | tf_op jit(solution)/shard_map/start/pallas_call | solution.py:445
  44.4 3.0 %collective-permute-start.14 = (f32[64,128]{1,0:T(8,128)S(1)}, f32[64,128]{1,0:T(8,128)S(1)}, u32[]{:S(2)}, u32[]{:S(2)}) collective-permute-start(f32[64,128]{1,0:T(8,128)S(1)} %add.39.own), channel_id=1, source_target_pairs={{0,4},{2,6},{4,0},{6,2},{1,5},{3,7},{5,1},{7,3},{8,12},{10,14},{12... | collective-permute-start | bytes 98312 | tf_op jit(solution)/shard_map/ppermute | solution.py:460
  48.5 1.3 %collective-permute-done.14.two = f32[64,128]{1,0:T(8,128)S(1)} collective-permute-done((f32[64,128]{1,0:T(8,128)S(1)}, f32[64,128]{1,0:T(8,128)S(1)}, u32[]{:S(2)}, u32[]{:S(2)}) %collective-permute-start.14) | collective-permute-done | bytes 32800 | tf_op jit(solution)/shard_map/ppermute | solution.py:460
  49.8 2.7 %collective-permute-done.13.one = f32[64,128]{1,0:T(8,128)S(1)} collective-permute-done((f32[64,128]{1,0:T(8,128)S(1)}, f32[64,128]{1,0:T(8,128)S(1)}, u32[]{:S(2)}, u32[]{:S(2)}) %collective-permute-start.13) | collective-permute-done | bytes 32800 | tf_op jit(solution)/shard_map/ppermute | solution.py:460
  52.5 1.7 %back.1 = (f32[80,256]{1,0:T(8,128)S(1)}, f32[128,4096]{1,0:T(8,128)S(1)}, f32[80,1408]{1,0:T(8,128)S(1)}) custom-call(s32[1]{0:T(128)} %bitcast.1.tm_ref, f32[64,128]{1,0:T(8,128)S(1)} %add.39.own, f32[64,128]{1,0:T(8,128)S(1)} %collective-permute-done.13.one, ...), custom_call_target="tpu_custom_call", output_to_operand_aliasing={{1}: (5, {}), {2}: (6, {})} | custom-call | tf_op jit(solution)/shard_map/back/pallas_call | solution.py:445
  54.2 2.1 %collective-permute-start.18 = (f32[80,256]{1,0:T(8,128)S(1)}, f32[80,256]{1,0:T(8,128)S(1)}, u32[]{:S(2)}, u32[]{:S(2)}) collective-permute-start(f32[80,256]{1,0:T(8,128)S(1)} %get-tuple-element.33), channel_id=1, source_target_pairs={{0,24},{8,0},{16,8},{24,16},{1,25},{9,1},{17,9},{25,17},{2,26},{10... | collective-permute-start | bytes 245768 | tf_op jit(solution)/shard_map/ppermute | solution.py:460
  56.3 1.7 %collective-permute-start.16 = (f32[80,256]{1,0:T(8,128)S(1)}, f32[80,256]{1,0:T(8,128)S(1)}, u32[]{:S(2)}, u32[]{:S(2)}) collective-permute-start(f32[80,256]{1,0:T(8,128)S(1)} %get-tuple-element.33), channel_id=1, source_target_pairs={{0,16},{8,24},{16,0},{24,8},{1,17},{9,25},{17,1},{25,9},{2,18},{10... | collective-permute-start | bytes 245768 | tf_op jit(solution)/shard_map/ppermute | solution.py:460
  59.2 3.7 %collective-permute-done.17 = f32[80,256]{1,0:T(8,128)S(1)} collective-permute-done((f32[80,256]{1,0:T(8,128)S(1)}, f32[80,256]{1,0:T(8,128)S(1)}, u32[]{:S(2)}, u32[]{:S(2)}) %collective-permute-start.17) | collective-permute-done | bytes 81952 | tf_op jit(solution)/shard_map/ppermute | solution.py:460
  64.2 1.3 %collective-permute-start.19 = (f32[80,256]{1,0:T(8,128)S(1)}, f32[80,256]{1,0:T(8,128)S(1)}, u32[]{:S(2)}, u32[]{:S(2)}) collective-permute-start(f32[80,256]{1,0:T(8,128)S(1)} %add_add_fusion.own), channel_id=1, source_target_pairs={{0,32},{32,64},{64,96},{96,0},{1,33},{33,65},{65,97},{97,1},{2,34}... | collective-permute-start | bytes 245768 | tf_op jit(solution)/shard_map/ppermute | solution.py:460
  65.5 1.9 %collective-permute-done.21.three = f32[80,256]{1,0:T(8,128)S(1)} collective-permute-done((f32[80,256]{1,0:T(8,128)S(1)}, f32[80,256]{1,0:T(8,128)S(1)}, u32[]{:S(2)}, u32[]{:S(2)}) %collective-permute-start.21) | collective-permute-done | bytes 81952 | tf_op jit(solution)/shard_map/ppermute | solution.py:460
  67.4 2.1 %collective-permute-done.20.two = f32[80,256]{1,0:T(8,128)S(1)} collective-permute-done((f32[80,256]{1,0:T(8,128)S(1)}, f32[80,256]{1,0:T(8,128)S(1)}, u32[]{:S(2)}, u32[]{:S(2)}) %collective-permute-start.20) | collective-permute-done | bytes 81952 | tf_op jit(solution)/shard_map/ppermute | solution.py:460
  70.3 1.3 %next.1 = (f32[72,128]{1,0:T(8,128)S(1)}, f32[128,4096]{1,0:T(8,128)S(1)}, f32[80,1408]{1,0:T(8,128)S(1)}) custom-call(s32[1]{0:T(128)} %bitcast.1.tm_ref, f32[80,256]{1,0:T(8,128)S(1)} %add_add_fusion.own, f32[80,256]{1,0:T(8,128)S(1)} %collective-permute-done.19.one, ...), custom_call_target="tpu_custom_call", output_to_operand_aliasing={{1}: (5, {}), {2}: (6, {})} | custom-call | tf_op jit(solution)/shard_map/next/pallas_call | solution.py:445
  74.9 1.9 %collective-permute-done.25.three = f32[72,128]{1,0:T(8,128)S(1)} collective-permute-done((f32[72,128]{1,0:T(8,128)S(1)}, f32[72,128]{1,0:T(8,128)S(1)}, u32[]{:S(2)}, u32[]{:S(2)}) %collective-permute-start.25) | collective-permute-done | bytes 36896 | tf_op jit(solution)/shard_map/ppermute | solution.py:460
  76.8 2.0 %collective-permute-done.24.two = f32[72,128]{1,0:T(8,128)S(1)} collective-permute-done((f32[72,128]{1,0:T(8,128)S(1)}, f32[72,128]{1,0:T(8,128)S(1)}, u32[]{:S(2)}, u32[]{:S(2)}) %collective-permute-start.24) | collective-permute-done | bytes 36896 | tf_op jit(solution)/shard_map/ppermute | solution.py:460
  79.5 2.6 %back_to_owners.1 = (f32[16,16,128]{2,1,0:T(8,128)}, f32[128,4096]{1,0:T(8,128)S(1)}, f32[80,1408]{1,0:T(8,128)S(1)}) custom-call(s32[1]{0:T(128)} %bitcast.1.tm_ref, f32[72,128]{1,0:T(8,128)S(1)} %add.43.own, f32[72,128]{1,0:T(8,128)S(1)} %collective-permute-done.23.one, ...), custom_call_target="tpu_custom_call", output_to_operand_aliasing={{1}: (5, {}), {2}: (6, {})} | custom-call | tf_op jit(solution)/shard_map/back_to_owners/pallas_call | solution.py:445
  82.1 5.2 %all-to-all-start = ((f32[16,16,128]{2,1,0:T(8,128)}), f32[16,16,128]{2,1,0:T(8,128)S(1)}, u32[]{:S(2)}, u32[]{:S(2)}) async-start(f32[16,16,128]{2,1,0:T(8,128)} %get-tuple-element.39), calls=%async_computation | async-start | bytes 262144 | tf_op jit(solution)/shard_map/all_to_all | solution.py:530
  87.4 8.0 %all-to-all-done.blocks_ref = f32[16,16,128]{2,1,0:T(8,128)S(1)} async-done(((f32[16,16,128]{2,1,0:T(8,128)}), f32[16,16,128]{2,1,0:T(8,128)S(1)}, u32[]{:S(2)}, u32[]{:S(2)}) %all-to-all-start) | async-done | bytes 131104 | tf_op jit(solution)/shard_map/all_to_all | solution.py:530
  (51 shorter events, 14.6 us)
Async XLA Ops:
  0.6 0.9 copy-start
  0.6 0.9 copy-start.3
  0.7 9.0 %copy-start.1 = (f32[4,4096]{1,0:T(4,128)S(1)}, f32[4,4096]{1,0:T(4,128)}, u32[]{:S(2)}) copy-start(f32[4,4096]{1,0:T(4,128)} %h_ref.1) | copy-start | bytes 196612
  0.7 8.9 %copy-start.2 = (s32[4096]{0:T(1024)S(1)}, s32[4096]{0:T(1024)}, u32[]{:S(2)}) copy-start(s32[4096]{0:T(1024)} %param.9) | copy-start | bytes 49156
  0.7 8.9 %copy-start.5 = (f32[4096]{0:T(1024)S(1)}, f32[4096]{0:T(1024)}, u32[]{:S(2)}) copy-start(f32[4096]{0:T(1024)} %param.13) | copy-start | bytes 49156
  2.8 1.4 %collective-permute-start = (f32[160,128]{1,0:T(8,128)S(1)}, f32[160,128]{1,0:T(8,128)S(1)}, u32[]{:S(2)}, u32[]{:S(2)}) collective-permute-start(f32[160,128]{1,0:T(8,128)S(1)} %get-tuple-element.22), channel_id=1, source_target_pairs={{0,1},{1,0},{2,3},{3,2},{4,5},{5,4},{6,7},{7,6},{8,9},{9,8},{10,11... | collective-permute-start | bytes 245768 | tf_op jit(solution)/shard_map/ppermute | solution.py:470
  4.2 14.4 %collective-permute-start.3 = (f32[160,128]{1,0:T(8,128)S(1)}, f32[160,128]{1,0:T(8,128)S(1)}, u32[]{:S(2)}, u32[]{:S(2)}) collective-permute-start(f32[160,128]{1,0:T(8,128)S(1)} %add.35.own), channel_id=1, source_target_pairs={{0,6},{2,0},{4,2},{6,4},{1,7},{3,1},{5,3},{7,5},{8,14},{10,8},{12,... | collective-permute-start | bytes 245768 | tf_op jit(solution)/shard_map/ppermute | solution.py:460
  8.4 10.2 %collective-permute-start.2 = (f32[160,128]{1,0:T(8,128)S(1)}, f32[160,128]{1,0:T(8,128)S(1)}, u32[]{:S(2)}, u32[]{:S(2)}) collective-permute-start(f32[160,128]{1,0:T(8,128)S(1)} %add.35.own), channel_id=1, source_target_pairs={{0,4},{2,6},{4,0},{6,2},{1,5},{3,7},{5,1},{7,3},{8,12},{10,14},{12... | collective-permute-start | bytes 245768 | tf_op jit(solution)/shard_map/ppermute | solution.py:460
  8.4 10.2 %collective-permute-start.1 = (f32[160,128]{1,0:T(8,128)S(1)}, f32[160,128]{1,0:T(8,128)S(1)}, u32[]{:S(2)}, u32[]{:S(2)}) collective-permute-start(f32[160,128]{1,0:T(8,128)S(1)} %add.35.own), channel_id=1, source_target_pairs={{0,2},{2,4},{4,6},{6,0},{1,3},{3,5},{5,7},{7,1},{8,10},{10,12},{12... | collective-permute-start | bytes 245768 | tf_op jit(solution)/shard_map/ppermute | solution.py:460
  11.7 2.6 %collective-permute-start.4 = (f32[24,256]{1,0:T(8,128)S(1)}, f32[24,256]{1,0:T(8,128)S(1)}, u32[]{:S(2)}, u32[]{:S(2)}) collective-permute-start(f32[24,256]{1,0:T(8,128)S(1)} %get-tuple-element.24), channel_id=1, source_target_pairs={{0,1},{1,2},{2,3},{3,4},{4,5},{5,6},{6,7},{8,9},{9,10},{10,11},{11... | collective-permute-start | bytes 73736 | tf_op jit(solution)/shard_map/ppermute | solution.py:466
  13.0 5.6 %collective-permute-start.5 = (f32[24,256]{1,0:T(8,128)S(1)}, f32[24,256]{1,0:T(8,128)S(1)}, u32[]{:S(2)}, u32[]{:S(2)}) collective-permute-start(f32[24,256]{1,0:T(8,128)S(1)} %get-tuple-element.25), channel_id=1, source_target_pairs={{1,0},{2,1},{3,2},{4,3},{5,4},{6,5},{7,6},{9,8},{10,9},{11,10},{12... | collective-permute-start | bytes 73736 | tf_op jit(solution)/shard_map/ppermute | solution.py:466
  20.4 5.1 %collective-permute-start.8 = (f32[80,256]{1,0:T(8,128)S(1)}, f32[80,256]{1,0:T(8,128)S(1)}, u32[]{:S(2)}, u32[]{:S(2)}) collective-permute-start(f32[80,256]{1,0:T(8,128)S(1)} %get-tuple-element.27), channel_id=1, source_target_pairs={{0,24},{8,0},{16,8},{24,16},{1,25},{9,1},{17,9},{25,17},{2,26},{10... | collective-permute-start | bytes 245768 | tf_op jit(solution)/shard_map/ppermute | solution.py:460
  23.2 6.4 %collective-permute-start.7 = (f32[80,256]{1,0:T(8,128)S(1)}, f32[80,256]{1,0:T(8,128)S(1)}, u32[]{:S(2)}, u32[]{:S(2)}) collective-permute-start(f32[80,256]{1,0:T(8,128)S(1)} %get-tuple-element.27), channel_id=1, source_target_pairs={{0,8},{8,16},{16,24},{24,0},{1,9},{9,17},{17,25},{25,1},{2,10},{10... | collective-permute-start | bytes 245768 | tf_op jit(solution)/shard_map/ppermute | solution.py:460
  23.2 6.8 %collective-permute-start.6 = (f32[80,256]{1,0:T(8,128)S(1)}, f32[80,256]{1,0:T(8,128)S(1)}, u32[]{:S(2)}, u32[]{:S(2)}) collective-permute-start(f32[80,256]{1,0:T(8,128)S(1)} %get-tuple-element.27), channel_id=1, source_target_pairs={{0,16},{8,24},{16,0},{24,8},{1,17},{9,25},{17,1},{25,9},{2,18},{10... | collective-permute-start | bytes 245768 | tf_op jit(solution)/shard_map/ppermute | solution.py:460
  30.0 5.5 %collective-permute-start.11 = (f32[80,256]{1,0:T(8,128)S(1)}, f32[80,256]{1,0:T(8,128)S(1)}, u32[]{:S(2)}, u32[]{:S(2)}) collective-permute-start(f32[80,256]{1,0:T(8,128)S(1)} %add_add_fusion.1.own), channel_id=1, source_target_pairs={{0,96},{32,0},{64,32},{96,64},{1,97},{33,1},{65,33},{97,65},{2,98}... | collective-permute-start | bytes 245768 | tf_op jit(solution)/shard_map/ppermute | solution.py:460
  33.1 6.8 %collective-permute-start.10 = (f32[80,256]{1,0:T(8,128)S(1)}, f32[80,256]{1,0:T(8,128)S(1)}, u32[]{:S(2)}, u32[]{:S(2)}) collective-permute-start(f32[80,256]{1,0:T(8,128)S(1)} %add_add_fusion.1.own), channel_id=1, source_target_pairs={{0,64},{32,96},{64,0},{96,32},{1,65},{33,97},{65,1},{97,33},{2,66}... | collective-permute-start | bytes 245768 | tf_op jit(solution)/shard_map/ppermute | solution.py:460
  33.7 7.9 %collective-permute-start.9 = (f32[80,256]{1,0:T(8,128)S(1)}, f32[80,256]{1,0:T(8,128)S(1)}, u32[]{:S(2)}, u32[]{:S(2)}) collective-permute-start(f32[80,256]{1,0:T(8,128)S(1)} %add_add_fusion.1.own), channel_id=1, source_target_pairs={{0,32},{32,64},{64,96},{96,0},{1,33},{33,65},{65,97},{97,1},{2,34}... | collective-permute-start | bytes 245768 | tf_op jit(solution)/shard_map/ppermute | solution.py:460
  42.9 1.3 %collective-permute-start.12 = (f32[64,128]{1,0:T(8,128)S(1)}, f32[64,128]{1,0:T(8,128)S(1)}, u32[]{:S(2)}, u32[]{:S(2)}) collective-permute-start(f32[64,128]{1,0:T(8,128)S(1)} %get-tuple-element.30), channel_id=1, source_target_pairs={{0,1},{1,0},{2,3},{3,2},{4,5},{5,4},{6,7},{7,6},{8,9},{9,8},{10,11... | collective-permute-start | bytes 98312 | tf_op jit(solution)/shard_map/ppermute | solution.py:470
  44.2 4.3 %collective-permute-start.15 = (f32[64,128]{1,0:T(8,128)S(1)}, f32[64,128]{1,0:T(8,128)S(1)}, u32[]{:S(2)}, u32[]{:S(2)}) collective-permute-start(f32[64,128]{1,0:T(8,128)S(1)} %add.39.own), channel_id=1, source_target_pairs={{0,6},{2,0},{4,2},{6,4},{1,7},{3,1},{5,3},{7,5},{8,14},{10,8},{12,... | collective-permute-start | bytes 98312 | tf_op jit(solution)/shard_map/ppermute | solution.py:460
  44.4 5.4 %collective-permute-start.14 = (f32[64,128]{1,0:T(8,128)S(1)}, f32[64,128]{1,0:T(8,128)S(1)}, u32[]{:S(2)}, u32[]{:S(2)}) collective-permute-start(f32[64,128]{1,0:T(8,128)S(1)} %add.39.own), channel_id=1, source_target_pairs={{0,4},{2,6},{4,0},{6,2},{1,5},{3,7},{5,1},{7,3},{8,12},{10,14},{12... | collective-permute-start | bytes 98312 | tf_op jit(solution)/shard_map/ppermute | solution.py:460
  47.4 5.1 %collective-permute-start.13 = (f32[64,128]{1,0:T(8,128)S(1)}, f32[64,128]{1,0:T(8,128)S(1)}, u32[]{:S(2)}, u32[]{:S(2)}) collective-permute-start(f32[64,128]{1,0:T(8,128)S(1)} %add.39.own), channel_id=1, source_target_pairs={{0,2},{2,4},{4,6},{6,0},{1,3},{3,5},{5,7},{7,1},{8,10},{10,12},{12... | collective-permute-start | bytes 98312 | tf_op jit(solution)/shard_map/ppermute | solution.py:460
  54.2 5.0 %collective-permute-start.18 = (f32[80,256]{1,0:T(8,128)S(1)}, f32[80,256]{1,0:T(8,128)S(1)}, u32[]{:S(2)}, u32[]{:S(2)}) collective-permute-start(f32[80,256]{1,0:T(8,128)S(1)} %get-tuple-element.33), channel_id=1, source_target_pairs={{0,24},{8,0},{16,8},{24,16},{1,25},{9,1},{17,9},{25,17},{2,26},{10... | collective-permute-start | bytes 245768 | tf_op jit(solution)/shard_map/ppermute | solution.py:460
  56.3 6.5 %collective-permute-start.17 = (f32[80,256]{1,0:T(8,128)S(1)}, f32[80,256]{1,0:T(8,128)S(1)}, u32[]{:S(2)}, u32[]{:S(2)}) collective-permute-start(f32[80,256]{1,0:T(8,128)S(1)} %get-tuple-element.33), channel_id=1, source_target_pairs={{0,8},{8,16},{16,24},{24,0},{1,9},{9,17},{17,25},{25,1},{2,10},{10... | collective-permute-start | bytes 245768 | tf_op jit(solution)/shard_map/ppermute | solution.py:460
  56.3 6.5 %collective-permute-start.16 = (f32[80,256]{1,0:T(8,128)S(1)}, f32[80,256]{1,0:T(8,128)S(1)}, u32[]{:S(2)}, u32[]{:S(2)}) collective-permute-start(f32[80,256]{1,0:T(8,128)S(1)} %get-tuple-element.33), channel_id=1, source_target_pairs={{0,16},{8,24},{16,0},{24,8},{1,17},{9,25},{17,1},{25,9},{2,18},{10... | collective-permute-start | bytes 245768 | tf_op jit(solution)/shard_map/ppermute | solution.py:460
  62.9 4.5 %collective-permute-start.21 = (f32[80,256]{1,0:T(8,128)S(1)}, f32[80,256]{1,0:T(8,128)S(1)}, u32[]{:S(2)}, u32[]{:S(2)}) collective-permute-start(f32[80,256]{1,0:T(8,128)S(1)} %add_add_fusion.own), channel_id=1, source_target_pairs={{0,96},{32,0},{64,32},{96,64},{1,97},{33,1},{65,33},{97,65},{2,98}... | collective-permute-start | bytes 245768 | tf_op jit(solution)/shard_map/ppermute | solution.py:460
  63.5 6.0 %collective-permute-start.20 = (f32[80,256]{1,0:T(8,128)S(1)}, f32[80,256]{1,0:T(8,128)S(1)}, u32[]{:S(2)}, u32[]{:S(2)}) collective-permute-start(f32[80,256]{1,0:T(8,128)S(1)} %add_add_fusion.own), channel_id=1, source_target_pairs={{0,64},{32,96},{64,0},{96,32},{1,65},{33,97},{65,1},{97,33},{2,66}... | collective-permute-start | bytes 245768 | tf_op jit(solution)/shard_map/ppermute | solution.py:460
  64.2 6.1 %collective-permute-start.19 = (f32[80,256]{1,0:T(8,128)S(1)}, f32[80,256]{1,0:T(8,128)S(1)}, u32[]{:S(2)}, u32[]{:S(2)}) collective-permute-start(f32[80,256]{1,0:T(8,128)S(1)} %add_add_fusion.own), channel_id=1, source_target_pairs={{0,32},{32,64},{64,96},{96,0},{1,33},{33,65},{65,97},{97,1},{2,34}... | collective-permute-start | bytes 245768 | tf_op jit(solution)/shard_map/ppermute | solution.py:460
  71.6 1.3 %collective-permute-start.22 = (f32[72,128]{1,0:T(8,128)S(1)}, f32[72,128]{1,0:T(8,128)S(1)}, u32[]{:S(2)}, u32[]{:S(2)}) collective-permute-start(f32[72,128]{1,0:T(8,128)S(1)} %get-tuple-element.36), channel_id=1, source_target_pairs={{0,1},{1,0},{2,3},{3,2},{4,5},{5,4},{6,7},{7,6},{8,9},{9,8},{10,11... | collective-permute-start | bytes 110600 | tf_op jit(solution)/shard_map/ppermute | solution.py:470
  72.9 4.0 %collective-permute-start.25 = (f32[72,128]{1,0:T(8,128)S(1)}, f32[72,128]{1,0:T(8,128)S(1)}, u32[]{:S(2)}, u32[]{:S(2)}) collective-permute-start(f32[72,128]{1,0:T(8,128)S(1)} %add.43.own), channel_id=1, source_target_pairs={{0,6},{2,0},{4,2},{6,4},{1,7},{3,1},{5,3},{7,5},{8,14},{10,8},{12,... | collective-permute-start | bytes 110600 | tf_op jit(solution)/shard_map/ppermute | solution.py:460
  73.2 5.6 %collective-permute-start.24 = (f32[72,128]{1,0:T(8,128)S(1)}, f32[72,128]{1,0:T(8,128)S(1)}, u32[]{:S(2)}, u32[]{:S(2)}) collective-permute-start(f32[72,128]{1,0:T(8,128)S(1)} %add.43.own), channel_id=1, source_target_pairs={{0,4},{2,6},{4,0},{6,2},{1,5},{3,7},{5,1},{7,3},{8,12},{10,14},{12... | collective-permute-start | bytes 110600 | tf_op jit(solution)/shard_map/ppermute | solution.py:460
  74.3 5.2 %collective-permute-start.23 = (f32[72,128]{1,0:T(8,128)S(1)}, f32[72,128]{1,0:T(8,128)S(1)}, u32[]{:S(2)}, u32[]{:S(2)}) collective-permute-start(f32[72,128]{1,0:T(8,128)S(1)} %add.43.own), channel_id=1, source_target_pairs={{0,2},{2,4},{4,6},{6,0},{1,3},{3,5},{5,7},{7,1},{8,10},{10,12},{12... | collective-permute-start | bytes 110600 | tf_op jit(solution)/shard_map/ppermute | solution.py:460
  82.1 13.2 %all-to-all-start = ((f32[16,16,128]{2,1,0:T(8,128)}), f32[16,16,128]{2,1,0:T(8,128)S(1)}, u32[]{:S(2)}, u32[]{:S(2)}) async-start(f32[16,16,128]{2,1,0:T(8,128)} %get-tuple-element.39), calls=%async_computation | async-start | bytes 262144 | tf_op jit(solution)/shard_map/all_to_all | solution.py:530
  (2 other events, 1.8 us)

commit v4 on v3

--- a/solution.py
+++ b/solution.py
@@ -13,7 +13,7 @@
 SKY_TM = ("sky_0", "sky_1", "tm_0", "tm_1")
 
 OBS_DEV = 4096
-CHUNK = 1024
+CHUNK = 4096
 damping = 0.5
 entry_pairs = [(row_at, col_at) for row_at in range(5) for col_at in range(row_at + 1)]
 
@@ -159,7 +159,7 @@
             work[row : row + 8, at] = weight * h
 
 
-def ghost_kernel(count_ref, flat_ref, source_ref, g_ref, work, earlier_ref, later_ref):
+def ghost_kernel(count_ref, tm_ref, flat_ref, source_ref, g_ref, work, earlier_ref, later_ref, twin_ref):
     knot = flat_ref[...]
     order = lax.broadcasted_iota(jnp.int32, (32, 128), 0) * 128 + lax.broadcasted_iota(jnp.int32, (32, 128), 1)
     live = order < count_ref[0]
@@ -170,7 +170,8 @@
         lax.broadcasted_iota(jnp.int32, (32, 32), 0) > lax.broadcasted_iota(jnp.int32, (32, 32), 1), 1.0, 0.0
     ).astype(bf16)
     numbers = row_numbers(256, 128)
-    for chosen, spread_at, ref in ((live & (knot >= 4093), 104, later_ref), (live & (knot < 3), 40, earlier_ref)):
+    at_low = live & (knot < 3) & (tm_ref[0] > 0)
+    for chosen, spread_at, ref in ((live & (knot >= 4093), 104, later_ref), (at_low, 40, earlier_ref)):
         mark = jnp.where(chosen, 1.0, 0.0).astype(bf16)
         rank = dot_nn(mark, across) + jnp.sum(dot_nn(down, mark), axis=1, keepdims=True)
         rank = jnp.where(chosen, rank, -1.0)
@@ -183,7 +184,10 @@
                 axis=0,
             )
             total = total + dot_nt(split_rows(data), slots)
-        ref[...] = join_rows(total)
+        total = join_rows(total)
+        ref[0:24] = total[:, 0:128]
+        ref[24:48] = total[:, 128:256]
+    twin_ref[...] = jnp.where((tm_ref[0] & 1) == 1, earlier_ref[...], later_ref[...])
 
 
 def ghost_sums(solved, ghosts, values):
@@ -270,14 +274,17 @@
     return jnp.concatenate([low, total[16:64], high], axis=0)
 
 
-def first_kernel(own, one, two, three, earlier_ref, later_ref, _work, _state, knots_ref, work, state):
-    sums = four((own, one, two, three))
+def first_kernel(tm_ref, own, one, two, three, twin, _work, _state, knots_ref, work, state):
+    sums = (own[0:160] + two[...]) + (one[0:160] + three[0:160])
+    odd = (tm_ref[0] & 1) == 1
+    earlier = jnp.where(odd, twin[...], one[160:208])
+    later = jnp.where(odd, three[160:208], twin[...])
     factor = factorize(factor_of(sums))
     stacked = jnp.concatenate([factor[pair] for pair in entry_pairs], axis=0)
     put(state, FACTOR_A, 0, stacked[0:80])
     put(state, FACTOR_B, 0, stacked[80:120])
     put(state, FACTOR_B, 40, sums[120:160])
-    ghosts = jnp.concatenate([earlier_ref[...], later_ref[...]], axis=1)
+    ghosts = jnp.concatenate([earlier[0:24], earlier[24:48], later[0:24], later[24:48]], axis=1)
     put_ghosts(state, ghosts)
     solved = split_rows(jnp.concatenate(chol_solve(factor, [tile(sums, 15 + j) for j in range(5)]), axis=0))
     earlier, later = ghost_sums(solved, ghosts, ghosts[22:23])
@@ -461,13 +468,18 @@
     ]
 
 
-def shifted(value, step):
-    count = lax.axis_size(TM)
-    return lax.ppermute(value, TM, [(at, at + step) for at in range(count) if 0 <= at + step < count])
+def crossing(value, step):
+    chips = lax.axis_size("tm_0")
+    pairs = [(2 * at + core, 2 * ((at + step) % chips) + 1 - core) for at in range(chips) for core in range(2)]
+    return lax.ppermute(value, TM, pairs)
+
+
+def to_twin(value):
+    return lax.ppermute(value, "tm_1", [(0, 1), (1, 0)])
 
 
 def tm_parts(value):
-    value = value + lax.ppermute(value, "tm_1", [(0, 1), (1, 0)])
+    value = value + to_twin(value)
     return ring_parts(value, "tm_0")
 
 
@@ -477,7 +489,7 @@
 
 
 KNOTS = ((80, 256), f32)
-GHOSTS = ((24, 256), f32)
+GHOSTS = ((48, 128), f32)
 
 
 def shards(obs_source, obs_knot, obs_count, src_design, att_design, obs_phase, obs_value, src_prior):
@@ -496,7 +508,7 @@
         aliases={6: 2},
         scalars=2,
     )
-    parts = tm_parts(sums)
+    twin_sums = to_twin(sums)
     (work,) = call(
         knot_kernel,
         "knot_spread",
@@ -505,16 +517,24 @@
         scalars=2,
         aliases={5: 0},
     )
-    earlier, later = call(
+    earlier, later, twin = call(
         ghost_kernel,
         "ghosts",
-        [GHOSTS, GHOSTS],
-        obs_count, obs_knot.reshape(32, 128), line(obs_source), src_design, work,
-        scalars=1,
-    )
-    ends = (shifted(later, 1), shifted(earlier, -1))
+        [GHOSTS] * 3,
+        obs_count, tm, obs_knot.reshape(32, 128), line(obs_source), src_design, work,
+        scalars=2,
+    )
+    sums = sums + twin_sums
+    onward = jnp.concatenate([sums, later], axis=0)
+    parts = (
+        onward,
+        crossing(onward, 1),
+        lax.ppermute(sums, "tm_0", [(at, (at + 2) % 4) for at in range(4)]),
+        crossing(jnp.concatenate([sums, earlier], axis=0), -1),
+        to_twin(twin),
+    )
     knots, work, state = call(
-        first_kernel, "first", [KNOTS, WORK, STATE], *parts, *ends, work, state, aliases={6: 1, 7: 2}
+        first_kernel, "first", [KNOTS, WORK, STATE], tm, *parts, work, state, scalars=1, aliases={6: 1, 7: 2}
     )
     parts = sky_parts(knots)
     kept = dict(scalars=1, aliases={5: 1, 6: 2})

time: 96.6 us -> 92 us (0.952)
  starting transfers between devices: 36.2 us -> 33.2 us
  Pallas kernels: 12.9 us -> 11.1 us
    ppermute x21 -> x18, starting transfers between devices: 28 us -> 21.8 us  [ring_parts(): lax.ppermute(value, axis, [(at, (at + step) % count) for at in range(coun...]
    ppermute x5 -> x7, starting transfers between devices: 2.93 us -> 6.22 us  [the longest x2 4.26 us: crossing(): return lax.ppermute(value, TM, pairs)]
    pallas_call x10, Pallas kernels: 12.9 us -> 11.1 us  [call(): pl.pallas_call(kernel, out_shape=shapes, in_specs=specs, out_specs=[VMEM]...]
    ppermute x5 -> x7, waiting for transfers between devices: 7.82 us -> 8.7 us  [the longest x1 4.23 us: shards(): lax.ppermute(sums, 'tm_0', [(at, (at + 2) % 4) for at in range(4)])]
    ppermute x21 -> x18, waiting for transfers between devices: 29.7 us -> 29 us  [ring_parts(): lax.ppermute(value, axis, [(at, (at + step) % count) for at in range(coun...]
  transfers between devices with their start and end apart: 27 -> 26, of which waited for: 20 -> 21; matrix products, arithmetic and copies ran while one was open for 0% -> 0% of each run, Pallas kernels for 2% -> 2%
where the time goes in v4:
time: 92 us; the launch traced here: 91.8 us
  waiting for transfers between devices  45.7 us (50%)
  starting transfers between devices  33.2 us (36%)
  Pallas kernels  11.1 us (12%)
  between operations  1.61 us (2%)
    ppermute x18, waiting for transfers between devices, ring_parts(): lax.ppermute(value, axis, [(at, (at + step) % count) for at in range(coun...  29 us
    ppermute x18, starting transfers between devices, ring_parts(): lax.ppermute(value, axis, [(at, (at + step) % count) for at in range(coun...  21.8 us
    pallas_call x10, Pallas kernels, call(): pl.pallas_call(kernel, out_shape=shapes, in_specs=specs, out_specs=[VMEM]...  11.1 us
    all_to_all x1, waiting for transfers between devices, shards(): blocks = lax.all_to_all(blocks, SKY, 0, 0, tiled=True)  7.98 us
    all_to_all x1, starting transfers between devices, shards(): blocks = lax.all_to_all(blocks, SKY, 0, 0, tiled=True)  5.25 us
    ppermute x2, starting transfers between devices, crossing(): return lax.ppermute(value, TM, pairs)  4.26 us
    ppermute x1, waiting for transfers between devices, shards(): lax.ppermute(sums, 'tm_0', [(at, (at + 2) % 4) for at in range(4)])  4.23 us
    ppermute x4, waiting for transfers between devices, to_twin(): return lax.ppermute(value, 'tm_1', [(0, 1), (1, 0)])  3.43 us
  transfers between devices with their start and end apart: 26, of which 21 were waited for; matrix products, arithmetic and copies ran while one was open for 0% of the time, Pallas kernels for 2%

profile of v4, /device:TPU:0, one launch (start us, length us, event | category | flops | bytes accessed | tf_op | source)
XLA Modules:
  0.0 91.8 jit_solution(6962142115456340287)
XLA Ops:
  1.5 1.2 %source_sums.1 = (f32[128,4096]{1,0:T(8,128)S(1)}, f32[160,128]{1,0:T(8,128)S(1)}, f32[80,1408]{1,0:T(8,128)S(1)}) custom-call(s32[1]{0:T(128)S(6)} %copy.35.count_ref, s32[1]{0:T(128)} %bitcast.2.first_ref, s32[1,4096]{1,0:T(1,128)S(1)} %bitcast.11, f32[5,4096]{1,0:T(8,128)S(1)} %copy-done, ...), custom_call_target="tpu_custom_call", output_to_operand_aliasing={{2}: (6, {})} | custom-call | tf_op jit(solution)/shard_map/source_sums/pallas_call | solution.py:452
  3.5 1.6 %ghosts.1 = (f32[48,128]{1,0:T(8,128)S(1)}, f32[48,128]{1,0:T(8,128)S(1)}, f32[48,128]{1,0:T(8,128)S(1)}) custom-call(s32[1]{0:T(128)S(6)} %copy.35.count_ref, s32[1]{0:T(128)} %bitcast.1.tm_ref, s32[32,128]{1,0:T(8,128)S(1)} %bitcast.10, s32[1,4096]{1,0:T(1,128)S(1)} %bitcast.12, f32[5,4096]{1,0:T(8,128)S(1)} %copy-done, f32[128,4096]{1,0:T(8,128)S(1)} %knot_spread.1.work._work), custom_call_target="tpu_custom_call" | custom-call | tf_op jit(solution)/shard_map/ghosts/pallas_call | solution.py:452
  5.1 4.3 %collective-permute-start.3 = (f32[208,128]{1,0:T(8,128)S(1)}, f32[208,128]{1,0:T(8,128)S(1)}, u32[]{:S(2)}, u32[]{:S(2)}) collective-permute-start(f32[208,128]{1,0:T(8,128)S(1)} %get-tuple-element.43), channel_id=1, source_target_pairs={{0,7},{1,6},{2,1},{3,0},{4,3},{5,2},{6,5},{7,4},{8,15},{9,14},{10,... | collective-permute-start | bytes 319496 | tf_op jit(solution)/shard_map/ppermute | solution.py:474
  9.4 1.5 %collective-permute-start.2 = (f32[160,128]{1,0:T(8,128)S(1)}, f32[160,128]{1,0:T(8,128)S(1)}, u32[]{:S(2)}, u32[]{:S(2)}) collective-permute-start(f32[160,128]{1,0:T(8,128)S(1)} %add.35), channel_id=1, source_target_pairs={{0,4},{2,6},{4,0},{6,2},{1,5},{3,7},{5,1},{7,3},{8,12},{10,14},{12... | collective-permute-start | bytes 245768 | tf_op jit(solution)/shard_map/ppermute | solution.py:532
  11.1 1.0 %collective-permute-done.4.twin = f32[48,128]{1,0:T(8,128)S(1)} collective-permute-done((f32[48,128]{1,0:T(8,128)S(1)}, f32[48,128]{1,0:T(8,128)S(1)}, u32[]{:S(2)}, u32[]{:S(2)}) %collective-permute-start.4) | collective-permute-done | bytes 24608 | tf_op jit(solution)/shard_map/ppermute | solution.py:478
  12.1 4.2 %collective-permute-done.2.two = f32[160,128]{1,0:T(8,128)S(1)} collective-permute-done((f32[160,128]{1,0:T(8,128)S(1)}, f32[160,128]{1,0:T(8,128)S(1)}, u32[]{:S(2)}, u32[]{:S(2)}) %collective-permute-start.2) | collective-permute-done | bytes 81952 | tf_op jit(solution)/shard_map/ppermute | solution.py:532
  17.4 1.2 %first.1 = (f32[80,256]{1,0:T(8,128)S(1)}, f32[128,4096]{1,0:T(8,128)S(1)}, f32[80,1408]{1,0:T(8,128)S(1)}) custom-call(s32[1]{0:T(128)} %bitcast.1.tm_ref, f32[208,128]{1,0:T(8,128)S(1)} %get-tuple-element.44.own, f32[208,128]{1,0:T(8,128)S(1)} %collective-permute-done.1.one, ...), custom_call_target="tpu_custom_call", output_to_operand_aliasing={{1}: (6, {}), {2}: (7, {})} | custom-call | tf_op jit(solution)/shard_map/first/pallas_call | solution.py:452
  18.6 2.8 %collective-permute-start.7 = (f32[80,256]{1,0:T(8,128)S(1)}, f32[80,256]{1,0:T(8,128)S(1)}, u32[]{:S(2)}, u32[]{:S(2)}) collective-permute-start(f32[80,256]{1,0:T(8,128)S(1)} %get-tuple-element.29), channel_id=1, source_target_pairs={{0,24},{8,0},{16,8},{24,16},{1,25},{9,1},{17,9},{25,17},{2,26},{10... | collective-permute-start | bytes 245768 | tf_op jit(solution)/shard_map/ppermute | solution.py:467
  21.4 2.3 %collective-permute-start.5 = (f32[80,256]{1,0:T(8,128)S(1)}, f32[80,256]{1,0:T(8,128)S(1)}, u32[]{:S(2)}, u32[]{:S(2)}) collective-permute-start(f32[80,256]{1,0:T(8,128)S(1)} %get-tuple-element.29), channel_id=1, source_target_pairs={{0,16},{8,24},{16,0},{24,8},{1,17},{9,25},{17,1},{25,9},{2,18},{10... | collective-permute-start | bytes 245768 | tf_op jit(solution)/shard_map/ppermute | solution.py:467
  23.7 4.9 %collective-permute-done.6 = f32[80,256]{1,0:T(8,128)S(1)} collective-permute-done((f32[80,256]{1,0:T(8,128)S(1)}, f32[80,256]{1,0:T(8,128)S(1)}, u32[]{:S(2)}, u32[]{:S(2)}) %collective-permute-start.6) | collective-permute-done | bytes 81952 | tf_op jit(solution)/shard_map/ppermute | solution.py:467
  28.6 3.1 %collective-permute-start.10 = (f32[80,256]{1,0:T(8,128)S(1)}, f32[80,256]{1,0:T(8,128)S(1)}, u32[]{:S(2)}, u32[]{:S(2)}) collective-permute-start(f32[80,256]{1,0:T(8,128)S(1)} %add_add_fusion.1.own), channel_id=1, source_target_pairs={{0,96},{32,0},{64,32},{96,64},{1,97},{33,1},{65,33},{97,65},{2,98}... | collective-permute-start | bytes 245768 | tf_op jit(solution)/shard_map/ppermute | solution.py:467
  34.0 3.7 %collective-permute-done.9.two = f32[80,256]{1,0:T(8,128)S(1)} collective-permute-done((f32[80,256]{1,0:T(8,128)S(1)}, f32[80,256]{1,0:T(8,128)S(1)}, u32[]{:S(2)}, u32[]{:S(2)}) %collective-permute-start.9) | collective-permute-done | bytes 81952 | tf_op jit(solution)/shard_map/ppermute | solution.py:467
  38.5 1.2 %start.1 = (f32[64,128]{1,0:T(8,128)S(1)}, f32[128,4096]{1,0:T(8,128)S(1)}, f32[80,1408]{1,0:T(8,128)S(1)}) custom-call(s32[1]{0:T(128)} %bitcast.1.tm_ref, f32[80,256]{1,0:T(8,128)S(1)} %add_add_fusion.1.own, f32[80,256]{1,0:T(8,128)S(1)} %collective-permute-done.8.one, ...), custom_call_target="tpu_custom_call", output_to_operand_aliasing={{1}: (5, {}), {2}: (6, {})} | custom-call | tf_op jit(solution)/shard_map/start/pallas_call | solution.py:452
  39.8 1.2 %collective-permute-done.11 = f32[64,128]{1,0:T(8,128)S(1)} collective-permute-done((f32[64,128]{1,0:T(8,128)S(1)}, f32[64,128]{1,0:T(8,128)S(1)}, u32[]{:S(2)}, u32[]{:S(2)}) %collective-permute-start.11) | collective-permute-done | bytes 32800 | tf_op jit(solution)/shard_map/ppermute | solution.py:478
  41.8 1.3 %collective-permute-start.12 = (f32[64,128]{1,0:T(8,128)S(1)}, f32[64,128]{1,0:T(8,128)S(1)}, u32[]{:S(2)}, u32[]{:S(2)}) collective-permute-start(f32[64,128]{1,0:T(8,128)S(1)} %add.39.own), channel_id=1, source_target_pairs={{0,2},{2,4},{4,6},{6,0},{1,3},{3,5},{5,7},{7,1},{8,10},{10,12},{12... | collective-permute-start | bytes 98312 | tf_op jit(solution)/shard_map/ppermute | solution.py:467
  43.0 1.9 %collective-permute-done.14.three = f32[64,128]{1,0:T(8,128)S(1)} collective-permute-done((f32[64,128]{1,0:T(8,128)S(1)}, f32[64,128]{1,0:T(8,128)S(1)}, u32[]{:S(2)}, u32[]{:S(2)}) %collective-permute-start.14) | collective-permute-done | bytes 32800 | tf_op jit(solution)/shard_map/ppermute | solution.py:467
  44.9 2.3 %collective-permute-done.13.two = f32[64,128]{1,0:T(8,128)S(1)} collective-permute-done((f32[64,128]{1,0:T(8,128)S(1)}, f32[64,128]{1,0:T(8,128)S(1)}, u32[]{:S(2)}, u32[]{:S(2)}) %collective-permute-start.13) | collective-permute-done | bytes 32800 | tf_op jit(solution)/shard_map/ppermute | solution.py:467
  47.6 1.1 %back.1 = (f32[80,256]{1,0:T(8,128)S(1)}, f32[128,4096]{1,0:T(8,128)S(1)}, f32[80,1408]{1,0:T(8,128)S(1)}) custom-call(s32[1]{0:T(128)} %bitcast.1.tm_ref, f32[64,128]{1,0:T(8,128)S(1)} %add.39.own, f32[64,128]{1,0:T(8,128)S(1)} %collective-permute-done.12.one, ...), custom_call_target="tpu_custom_call", output_to_operand_aliasing={{1}: (5, {}), {2}: (6, {})} | custom-call | tf_op jit(solution)/shard_map/back/pallas_call | solution.py:452
  48.7 2.4 %collective-permute-start.17 = (f32[80,256]{1,0:T(8,128)S(1)}, f32[80,256]{1,0:T(8,128)S(1)}, u32[]{:S(2)}, u32[]{:S(2)}) collective-permute-start(f32[80,256]{1,0:T(8,128)S(1)} %get-tuple-element.35), channel_id=1, source_target_pairs={{0,24},{8,0},{16,8},{24,16},{1,25},{9,1},{17,9},{25,17},{2,26},{10... | collective-permute-start | bytes 245768 | tf_op jit(solution)/shard_map/ppermute | solution.py:467
  51.1 1.5 %collective-permute-start.15 = (f32[80,256]{1,0:T(8,128)S(1)}, f32[80,256]{1,0:T(8,128)S(1)}, u32[]{:S(2)}, u32[]{:S(2)}) collective-permute-start(f32[80,256]{1,0:T(8,128)S(1)} %get-tuple-element.35), channel_id=1, source_target_pairs={{0,16},{8,24},{16,0},{24,8},{1,17},{9,25},{17,1},{25,9},{2,18},{10... | collective-permute-start | bytes 245768 | tf_op jit(solution)/shard_map/ppermute | solution.py:467
  53.2 4.4 %collective-permute-done.16 = f32[80,256]{1,0:T(8,128)S(1)} collective-permute-done((f32[80,256]{1,0:T(8,128)S(1)}, f32[80,256]{1,0:T(8,128)S(1)}, u32[]{:S(2)}, u32[]{:S(2)}) %collective-permute-start.16) | collective-permute-done | bytes 81952 | tf_op jit(solution)/shard_map/ppermute | solution.py:467
  59.2 1.3 %collective-permute-start.18 = (f32[80,256]{1,0:T(8,128)S(1)}, f32[80,256]{1,0:T(8,128)S(1)}, u32[]{:S(2)}, u32[]{:S(2)}) collective-permute-start(f32[80,256]{1,0:T(8,128)S(1)} %add_add_fusion.own), channel_id=1, source_target_pairs={{0,32},{32,64},{64,96},{96,0},{1,33},{33,65},{65,97},{97,1},{2,34}... | collective-permute-start | bytes 245768 | tf_op jit(solution)/shard_map/ppermute | solution.py:467
  60.5 1.9 %collective-permute-done.20.three = f32[80,256]{1,0:T(8,128)S(1)} collective-permute-done((f32[80,256]{1,0:T(8,128)S(1)}, f32[80,256]{1,0:T(8,128)S(1)}, u32[]{:S(2)}, u32[]{:S(2)}) %collective-permute-start.20) | collective-permute-done | bytes 81952 | tf_op jit(solution)/shard_map/ppermute | solution.py:467
  62.4 2.1 %collective-permute-done.19.two = f32[80,256]{1,0:T(8,128)S(1)} collective-permute-done((f32[80,256]{1,0:T(8,128)S(1)}, f32[80,256]{1,0:T(8,128)S(1)}, u32[]{:S(2)}, u32[]{:S(2)}) %collective-permute-start.19) | collective-permute-done | bytes 81952 | tf_op jit(solution)/shard_map/ppermute | solution.py:467
  65.3 1.2 %next.1 = (f32[72,128]{1,0:T(8,128)S(1)}, f32[128,4096]{1,0:T(8,128)S(1)}, f32[80,1408]{1,0:T(8,128)S(1)}) custom-call(s32[1]{0:T(128)} %bitcast.1.tm_ref, f32[80,256]{1,0:T(8,128)S(1)} %add_add_fusion.own, f32[80,256]{1,0:T(8,128)S(1)} %collective-permute-done.18.one, ...), custom_call_target="tpu_custom_call", output_to_operand_aliasing={{1}: (5, {}), {2}: (6, {})} | custom-call | tf_op jit(solution)/shard_map/next/pallas_call | solution.py:452
  66.7 1.2 %collective-permute-done.21 = f32[72,128]{1,0:T(8,128)S(1)} collective-permute-done((f32[72,128]{1,0:T(8,128)S(1)}, f32[72,128]{1,0:T(8,128)S(1)}, u32[]{:S(2)}, u32[]{:S(2)}) %collective-permute-start.21) | collective-permute-done | bytes 36896 | tf_op jit(solution)/shard_map/ppermute | solution.py:478
  67.9 1.6 %collective-permute-start.24 = (f32[72,128]{1,0:T(8,128)S(1)}, f32[72,128]{1,0:T(8,128)S(1)}, u32[]{:S(2)}, u32[]{:S(2)}) collective-permute-start(f32[72,128]{1,0:T(8,128)S(1)} %add.43.own), channel_id=1, source_target_pairs={{0,6},{2,0},{4,2},{6,4},{1,7},{3,1},{5,3},{7,5},{8,14},{10,8},{12,... | collective-permute-start | bytes 110600 | tf_op jit(solution)/shard_map/ppermute | solution.py:467
  71.0 1.2 %collective-permute-done.24.three = f32[72,128]{1,0:T(8,128)S(1)} collective-permute-done((f32[72,128]{1,0:T(8,128)S(1)}, f32[72,128]{1,0:T(8,128)S(1)}, u32[]{:S(2)}, u32[]{:S(2)}) %collective-permute-start.24) | collective-permute-done | bytes 36896 | tf_op jit(solution)/shard_map/ppermute | solution.py:467
  72.2 2.8 %collective-permute-done.23.two = f32[72,128]{1,0:T(8,128)S(1)} collective-permute-done((f32[72,128]{1,0:T(8,128)S(1)}, f32[72,128]{1,0:T(8,128)S(1)}, u32[]{:S(2)}, u32[]{:S(2)}) %collective-permute-start.23) | collective-permute-done | bytes 36896 | tf_op jit(solution)/shard_map/ppermute | solution.py:467
  75.6 2.0 %back_to_owners.1 = (f32[16,16,128]{2,1,0:T(8,128)}, f32[128,4096]{1,0:T(8,128)S(1)}, f32[80,1408]{1,0:T(8,128)S(1)}) custom-call(s32[1]{0:T(128)} %bitcast.1.tm_ref, f32[72,128]{1,0:T(8,128)S(1)} %add.43.own, f32[72,128]{1,0:T(8,128)S(1)} %collective-permute-done.22.one, ...), custom_call_target="tpu_custom_call", output_to_operand_aliasing={{1}: (5, {}), {2}: (6, {})} | custom-call | tf_op jit(solution)/shard_map/back_to_owners/pallas_call | solution.py:452
  77.6 5.2 %all-to-all-start = ((f32[16,16,128]{2,1,0:T(8,128)}), f32[16,16,128]{2,1,0:T(8,128)S(1)}, u32[]{:S(2)}, u32[]{:S(2)}) async-start(f32[16,16,128]{2,1,0:T(8,128)} %get-tuple-element.41), calls=%async_computation | async-start | bytes 262144 | tf_op jit(solution)/shard_map/all_to_all | solution.py:550
  82.9 8.0 %all-to-all-done.blocks_ref = f32[16,16,128]{2,1,0:T(8,128)S(1)} async-done(((f32[16,16,128]{2,1,0:T(8,128)}), f32[16,16,128]{2,1,0:T(8,128)S(1)}, u32[]{:S(2)}, u32[]{:S(2)}) %all-to-all-start) | async-done | bytes 131104 | tf_op jit(solution)/shard_map/all_to_all | solution.py:550
  (50 shorter events, 12.5 us)
Async XLA Ops:
  0.6 0.9 copy-start
  0.6 0.9 copy-start.3
  0.7 0.9 copy-start.4
  0.7 2.2 %copy-start.1 = (f32[4,4096]{1,0:T(4,128)S(1)}, f32[4,4096]{1,0:T(4,128)}, u32[]{:S(2)}) copy-start(f32[4,4096]{1,0:T(4,128)} %h_ref.1) | copy-start | bytes 196612
  0.7 2.2 %copy-start.2 = (s32[4096]{0:T(1024)S(1)}, s32[4096]{0:T(1024)}, u32[]{:S(2)}) copy-start(s32[4096]{0:T(1024)} %param.9) | copy-start | bytes 49156
  0.7 2.2 %copy-start.5 = (f32[4096]{0:T(1024)S(1)}, f32[4096]{0:T(1024)}, u32[]{:S(2)}) copy-start(f32[4096]{0:T(1024)} %param.13) | copy-start | bytes 49156
  2.8 2.2 %collective-permute-start = (f32[160,128]{1,0:T(8,128)S(1)}, f32[160,128]{1,0:T(8,128)S(1)}, u32[]{:S(2)}, u32[]{:S(2)}) collective-permute-start(f32[160,128]{1,0:T(8,128)S(1)} %get-tuple-element.23), channel_id=1, source_target_pairs={{0,1},{1,0},{2,3},{3,2},{4,5},{5,4},{6,7},{7,6},{8,9},{9,8},{10,11... | collective-permute-start | bytes 245768 | tf_op jit(solution)/shard_map/ppermute | solution.py:478
  5.1 11.2 %collective-permute-start.3 = (f32[208,128]{1,0:T(8,128)S(1)}, f32[208,128]{1,0:T(8,128)S(1)}, u32[]{:S(2)}, u32[]{:S(2)}) collective-permute-start(f32[208,128]{1,0:T(8,128)S(1)} %get-tuple-element.43), channel_id=1, source_target_pairs={{0,7},{1,6},{2,1},{3,0},{4,3},{5,2},{6,5},{7,4},{8,15},{9,14},{10,... | collective-permute-start | bytes 319496 | tf_op jit(solution)/shard_map/ppermute | solution.py:474
  9.4 8.0 %collective-permute-start.1 = (f32[208,128]{1,0:T(8,128)S(1)}, f32[208,128]{1,0:T(8,128)S(1)}, u32[]{:S(2)}, u32[]{:S(2)}) collective-permute-start(f32[208,128]{1,0:T(8,128)S(1)} %get-tuple-element.44.own), channel_id=1, source_target_pairs={{0,3},{1,2},{2,5},{3,4},{4,7},{5,6},{6,1},{7,0},{8,11},{9,10},{10,... | collective-permute-start | bytes 319496 | tf_op jit(solution)/shard_map/ppermute | solution.py:474
  9.4 7.0 %collective-permute-start.2 = (f32[160,128]{1,0:T(8,128)S(1)}, f32[160,128]{1,0:T(8,128)S(1)}, u32[]{:S(2)}, u32[]{:S(2)}) collective-permute-start(f32[160,128]{1,0:T(8,128)S(1)} %add.35), channel_id=1, source_target_pairs={{0,4},{2,6},{4,0},{6,2},{1,5},{3,7},{5,1},{7,3},{8,12},{10,14},{12... | collective-permute-start | bytes 245768 | tf_op jit(solution)/shard_map/ppermute | solution.py:532
  10.9 1.2 %collective-permute-start.4 = (f32[48,128]{1,0:T(8,128)S(1)}, f32[48,128]{1,0:T(8,128)S(1)}, u32[]{:S(2)}, u32[]{:S(2)}) collective-permute-start(f32[48,128]{1,0:T(8,128)S(1)} %get-tuple-element.27), channel_id=1, source_target_pairs={{0,1},{1,0},{2,3},{3,2},{4,5},{5,4},{6,7},{7,6},{8,9},{9,8},{10,11... | collective-permute-start | bytes 73736 | tf_op jit(solution)/shard_map/ppermute | solution.py:478
  18.6 5.1 %collective-permute-start.7 = (f32[80,256]{1,0:T(8,128)S(1)}, f32[80,256]{1,0:T(8,128)S(1)}, u32[]{:S(2)}, u32[]{:S(2)}) collective-permute-start(f32[80,256]{1,0:T(8,128)S(1)} %get-tuple-element.29), channel_id=1, source_target_pairs={{0,24},{8,0},{16,8},{24,16},{1,25},{9,1},{17,9},{25,17},{2,26},{10... | collective-permute-start | bytes 245768 | tf_op jit(solution)/shard_map/ppermute | solution.py:467
  21.4 7.2 %collective-permute-start.6 = (f32[80,256]{1,0:T(8,128)S(1)}, f32[80,256]{1,0:T(8,128)S(1)}, u32[]{:S(2)}, u32[]{:S(2)}) collective-permute-start(f32[80,256]{1,0:T(8,128)S(1)} %get-tuple-element.29), channel_id=1, source_target_pairs={{0,8},{8,16},{16,24},{24,0},{1,9},{9,17},{17,25},{25,1},{2,10},{10... | collective-permute-start | bytes 245768 | tf_op jit(solution)/shard_map/ppermute | solution.py:467
  21.4 7.2 %collective-permute-start.5 = (f32[80,256]{1,0:T(8,128)S(1)}, f32[80,256]{1,0:T(8,128)S(1)}, u32[]{:S(2)}, u32[]{:S(2)}) collective-permute-start(f32[80,256]{1,0:T(8,128)S(1)} %get-tuple-element.29), channel_id=1, source_target_pairs={{0,16},{8,24},{16,0},{24,8},{1,17},{9,25},{17,1},{25,9},{2,18},{10... | collective-permute-start | bytes 245768 | tf_op jit(solution)/shard_map/ppermute | solution.py:467
  28.6 5.4 %collective-permute-start.10 = (f32[80,256]{1,0:T(8,128)S(1)}, f32[80,256]{1,0:T(8,128)S(1)}, u32[]{:S(2)}, u32[]{:S(2)}) collective-permute-start(f32[80,256]{1,0:T(8,128)S(1)} %add_add_fusion.1.own), channel_id=1, source_target_pairs={{0,96},{32,0},{64,32},{96,64},{1,97},{33,1},{65,33},{97,65},{2,98}... | collective-permute-start | bytes 245768 | tf_op jit(solution)/shard_map/ppermute | solution.py:467
  31.7 6.0 %collective-permute-start.9 = (f32[80,256]{1,0:T(8,128)S(1)}, f32[80,256]{1,0:T(8,128)S(1)}, u32[]{:S(2)}, u32[]{:S(2)}) collective-permute-start(f32[80,256]{1,0:T(8,128)S(1)} %add_add_fusion.1.own), channel_id=1, source_target_pairs={{0,64},{32,96},{64,0},{96,32},{1,65},{33,97},{65,1},{97,33},{2,66}... | collective-permute-start | bytes 245768 | tf_op jit(solution)/shard_map/ppermute | solution.py:467
  32.3 6.2 %collective-permute-start.8 = (f32[80,256]{1,0:T(8,128)S(1)}, f32[80,256]{1,0:T(8,128)S(1)}, u32[]{:S(2)}, u32[]{:S(2)}) collective-permute-start(f32[80,256]{1,0:T(8,128)S(1)} %add_add_fusion.1.own), channel_id=1, source_target_pairs={{0,32},{32,64},{64,96},{96,0},{1,33},{33,65},{65,97},{97,1},{2,34}... | collective-permute-start | bytes 245768 | tf_op jit(solution)/shard_map/ppermute | solution.py:467
  39.7 1.3 %collective-permute-start.11 = (f32[64,128]{1,0:T(8,128)S(1)}, f32[64,128]{1,0:T(8,128)S(1)}, u32[]{:S(2)}, u32[]{:S(2)}) collective-permute-start(f32[64,128]{1,0:T(8,128)S(1)} %get-tuple-element.32), channel_id=1, source_target_pairs={{0,1},{1,0},{2,3},{3,2},{4,5},{5,4},{6,7},{7,6},{8,9},{9,8},{10,11... | collective-permute-start | bytes 98312 | tf_op jit(solution)/shard_map/ppermute | solution.py:478
  41.0 3.9 %collective-permute-start.14 = (f32[64,128]{1,0:T(8,128)S(1)}, f32[64,128]{1,0:T(8,128)S(1)}, u32[]{:S(2)}, u32[]{:S(2)}) collective-permute-start(f32[64,128]{1,0:T(8,128)S(1)} %add.39.own), channel_id=1, source_target_pairs={{0,6},{2,0},{4,2},{6,4},{1,7},{3,1},{5,3},{7,5},{8,14},{10,8},{12,... | collective-permute-start | bytes 98312 | tf_op jit(solution)/shard_map/ppermute | solution.py:467
  41.8 5.4 %collective-permute-start.13 = (f32[64,128]{1,0:T(8,128)S(1)}, f32[64,128]{1,0:T(8,128)S(1)}, u32[]{:S(2)}, u32[]{:S(2)}) collective-permute-start(f32[64,128]{1,0:T(8,128)S(1)} %add.39.own), channel_id=1, source_target_pairs={{0,4},{2,6},{4,0},{6,2},{1,5},{3,7},{5,1},{7,3},{8,12},{10,14},{12... | collective-permute-start | bytes 98312 | tf_op jit(solution)/shard_map/ppermute | solution.py:467
  41.8 5.8 %collective-permute-start.12 = (f32[64,128]{1,0:T(8,128)S(1)}, f32[64,128]{1,0:T(8,128)S(1)}, u32[]{:S(2)}, u32[]{:S(2)}) collective-permute-start(f32[64,128]{1,0:T(8,128)S(1)} %add.39.own), channel_id=1, source_target_pairs={{0,2},{2,4},{4,6},{6,0},{1,3},{3,5},{5,7},{7,1},{8,10},{10,12},{12... | collective-permute-start | bytes 98312 | tf_op jit(solution)/shard_map/ppermute | solution.py:467
  48.7 4.5 %collective-permute-start.17 = (f32[80,256]{1,0:T(8,128)S(1)}, f32[80,256]{1,0:T(8,128)S(1)}, u32[]{:S(2)}, u32[]{:S(2)}) collective-permute-start(f32[80,256]{1,0:T(8,128)S(1)} %get-tuple-element.35), channel_id=1, source_target_pairs={{0,24},{8,0},{16,8},{24,16},{1,25},{9,1},{17,9},{25,17},{2,26},{10... | collective-permute-start | bytes 245768 | tf_op jit(solution)/shard_map/ppermute | solution.py:467
  51.1 6.5 %collective-permute-start.16 = (f32[80,256]{1,0:T(8,128)S(1)}, f32[80,256]{1,0:T(8,128)S(1)}, u32[]{:S(2)}, u32[]{:S(2)}) collective-permute-start(f32[80,256]{1,0:T(8,128)S(1)} %get-tuple-element.35), channel_id=1, source_target_pairs={{0,8},{8,16},{16,24},{24,0},{1,9},{9,17},{17,25},{25,1},{2,10},{10... | collective-permute-start | bytes 245768 | tf_op jit(solution)/shard_map/ppermute | solution.py:467
  51.1 6.5 %collective-permute-start.15 = (f32[80,256]{1,0:T(8,128)S(1)}, f32[80,256]{1,0:T(8,128)S(1)}, u32[]{:S(2)}, u32[]{:S(2)}) collective-permute-start(f32[80,256]{1,0:T(8,128)S(1)} %get-tuple-element.35), channel_id=1, source_target_pairs={{0,16},{8,24},{16,0},{24,8},{1,17},{9,25},{17,1},{25,9},{2,18},{10... | collective-permute-start | bytes 245768 | tf_op jit(solution)/shard_map/ppermute | solution.py:467
  57.7 4.7 %collective-permute-start.20 = (f32[80,256]{1,0:T(8,128)S(1)}, f32[80,256]{1,0:T(8,128)S(1)}, u32[]{:S(2)}, u32[]{:S(2)}) collective-permute-start(f32[80,256]{1,0:T(8,128)S(1)} %add_add_fusion.own), channel_id=1, source_target_pairs={{0,96},{32,0},{64,32},{96,64},{1,97},{33,1},{65,33},{97,65},{2,98}... | collective-permute-start | bytes 245768 | tf_op jit(solution)/shard_map/ppermute | solution.py:467
  58.5 6.0 %collective-permute-start.19 = (f32[80,256]{1,0:T(8,128)S(1)}, f32[80,256]{1,0:T(8,128)S(1)}, u32[]{:S(2)}, u32[]{:S(2)}) collective-permute-start(f32[80,256]{1,0:T(8,128)S(1)} %add_add_fusion.own), channel_id=1, source_target_pairs={{0,64},{32,96},{64,0},{96,32},{1,65},{33,97},{65,1},{97,33},{2,66}... | collective-permute-start | bytes 245768 | tf_op jit(solution)/shard_map/ppermute | solution.py:467
  59.2 6.1 %collective-permute-start.18 = (f32[80,256]{1,0:T(8,128)S(1)}, f32[80,256]{1,0:T(8,128)S(1)}, u32[]{:S(2)}, u32[]{:S(2)}) collective-permute-start(f32[80,256]{1,0:T(8,128)S(1)} %add_add_fusion.own), channel_id=1, source_target_pairs={{0,32},{32,64},{64,96},{96,0},{1,33},{33,65},{65,97},{97,1},{2,34}... | collective-permute-start | bytes 245768 | tf_op jit(solution)/shard_map/ppermute | solution.py:467
  66.6 1.3 %collective-permute-start.21 = (f32[72,128]{1,0:T(8,128)S(1)}, f32[72,128]{1,0:T(8,128)S(1)}, u32[]{:S(2)}, u32[]{:S(2)}) collective-permute-start(f32[72,128]{1,0:T(8,128)S(1)} %get-tuple-element.38), channel_id=1, source_target_pairs={{0,1},{1,0},{2,3},{3,2},{4,5},{5,4},{6,7},{7,6},{8,9},{9,8},{10,11... | collective-permute-start | bytes 110600 | tf_op jit(solution)/shard_map/ppermute | solution.py:478
  67.9 4.3 %collective-permute-start.24 = (f32[72,128]{1,0:T(8,128)S(1)}, f32[72,128]{1,0:T(8,128)S(1)}, u32[]{:S(2)}, u32[]{:S(2)}) collective-permute-start(f32[72,128]{1,0:T(8,128)S(1)} %add.43.own), channel_id=1, source_target_pairs={{0,6},{2,0},{4,2},{6,4},{1,7},{3,1},{5,3},{7,5},{8,14},{10,8},{12,... | collective-permute-start | bytes 110600 | tf_op jit(solution)/shard_map/ppermute | solution.py:467
  69.5 5.5 %collective-permute-start.23 = (f32[72,128]{1,0:T(8,128)S(1)}, f32[72,128]{1,0:T(8,128)S(1)}, u32[]{:S(2)}, u32[]{:S(2)}) collective-permute-start(f32[72,128]{1,0:T(8,128)S(1)} %add.43.own), channel_id=1, source_target_pairs={{0,4},{2,6},{4,0},{6,2},{1,5},{3,7},{5,1},{7,3},{8,12},{10,14},{12... | collective-permute-start | bytes 110600 | tf_op jit(solution)/shard_map/ppermute | solution.py:467
  70.4 5.2 %collective-permute-start.22 = (f32[72,128]{1,0:T(8,128)S(1)}, f32[72,128]{1,0:T(8,128)S(1)}, u32[]{:S(2)}, u32[]{:S(2)}) collective-permute-start(f32[72,128]{1,0:T(8,128)S(1)} %add.43.own), channel_id=1, source_target_pairs={{0,2},{2,4},{4,6},{6,0},{1,3},{3,5},{5,7},{7,1},{8,10},{10,12},{12... | collective-permute-start | bytes 110600 | tf_op jit(solution)/shard_map/ppermute | solution.py:467
  77.6 13.2 %all-to-all-start = ((f32[16,16,128]{2,1,0:T(8,128)}), f32[16,16,128]{2,1,0:T(8,128)S(1)}, u32[]{:S(2)}, u32[]{:S(2)}) async-start(f32[16,16,128]{2,1,0:T(8,128)} %get-tuple-element.41), calls=%async_computation | async-start | bytes 262144 | tf_op jit(solution)/shard_map/all_to_all | solution.py:550
  (1 other events, 0.9 us)

commit v5 on v4

--- a/solution.py
+++ b/solution.py
@@ -48,7 +48,7 @@
 
 
 def four(refs):
-    own, one, two, three = (ref[...] for ref in refs)
+    own, one, three, two = (ref[...] for ref in refs)
     return (own + two) + (one + three)
 
 
@@ -267,14 +267,15 @@
 def with_ends(total, earlier, later, energy):
     lane = lax.broadcasted_iota(jnp.int32, (16, 256), 1)
     within = lax.broadcasted_iota(jnp.int32, (16, 256), 0) < 12
-    low = total[0:16] + jnp.where(within & (lane == 0), earlier, 0.0)
-    high = total[64:80] + jnp.where(within & (lane == 255), later, 0.0)
-    if energy is not None:
-        high = jnp.concatenate([high[0:12], jnp.concatenate([energy[0:4], energy[4:8]], axis=1)], axis=0)
-    return jnp.concatenate([low, total[16:64], high], axis=0)
-
-
-def first_kernel(tm_ref, own, one, two, three, twin, _work, _state, knots_ref, work, state):
+    beyond = jnp.where(within, total[64:80], 0.0)
+    low = total[0:16] + jnp.where(lane == 0, jnp.where(within, earlier, 0.0), pltpu.roll(beyond, 1, 1))
+    after_end = beyond[:, 255:256] + jnp.where(lax.broadcasted_iota(jnp.int32, (16, 1), 0) < 12, later, 0.0)
+    lane = lax.broadcasted_iota(jnp.int32, (8, 128), 1)
+    beside = jnp.where(lane == 0, after_end[0:8], jnp.where(lane == 1, after_end[8:16], 0.0))
+    return jnp.concatenate([low, total[16:64], jnp.concatenate([energy, beside], axis=1)], axis=0)
+
+
+def first_kernel(tm_ref, own, one, three, two, twin, _work, _state, knots_ref, work, state):
     sums = (own[0:160] + two[...]) + (one[0:160] + three[0:160])
     odd = (tm_ref[0] & 1) == 1
     earlier = jnp.where(odd, twin[...], one[160:208])
@@ -288,7 +289,7 @@
     put_ghosts(state, ghosts)
     solved = split_rows(jnp.concatenate(chol_solve(factor, [tile(sums, 15 + j) for j in range(5)]), axis=0))
     earlier, later = ghost_sums(solved, ghosts, ghosts[22:23])
-    knots_ref[...] = with_ends(eliminate_and_spread(solved, work), earlier, later, None)
+    knots_ref[...] = with_ends(eliminate_and_spread(solved, work), earlier, later, jnp.zeros((8, 128), f32))
 
 
 def kept_factor(state):
@@ -300,7 +301,7 @@
     put(state, lanes, 0, sums[:-8])
     target = [tile(sums, j) for j in range(5)]
     solved = chol_solve(kept_factor(state), target)
-    energy = tile(sums, 5)
+    energy = jnp.where(lax.broadcasted_iota(jnp.int32, (8, 128), 0) == 0, tile(sums, 5), 0.0)
     for j in range(5):
         energy = energy - target[j] * solved[j]
     solved = split_rows(jnp.concatenate(solved, axis=0))
@@ -309,44 +310,42 @@
     return with_ends(eliminate_and_spread(solved, work), earlier, later, energy), energy
 
 
-def back_kernel(tm_ref, own, one, two, three, _work, _state, knots_ref, work, state):
-    knots_ref[...], _ = back(BEFORE, tm_ref[0], (own, one, two, three), work, state)
-
-
-def back_to_owners_kernel(tm_ref, own, one, two, three, _work, _state, blocks_ref, work, state):
-    knots, energy = back(AFTER, tm_ref[0], (own, one, two, three), work, state)
-    knots = assembled(knots)
-    place = lax.broadcasted_iota(jnp.int32, (8, 128), 1) >> 4
-    for owner in range(16):
-        half = slice(128 * (owner // 8), 128 * (owner // 8) + 128)
-        block = jnp.zeros((8, 128), f32)
-        for q in range(8):
-            block = jnp.where(place == q, moved(knots[8 * q : 8 * q + 8, half], (16 * (q - owner)) % 128), block)
-        blocks_ref[owner, 0:8] = block
-        blocks_ref[owner, 8:16] = energy
-
-
-def moved(value, lanes):
-    return value if isinstance(lanes, int) and lanes == 0 else pltpu.roll(value, lanes, 1)
+def back_kernel(tm_ref, own, one, three, two, _work, _state, knots_ref, work, state):
+    knots_ref[...], _ = back(BEFORE, tm_ref[0], (own, one, three, two), work, state)
+
+
+def back_to_owners_kernel(tm_ref, own, one, three, two, _work, _state, blocks_ref, work, state):
+    knots, energy = back(AFTER, tm_ref[0], (own, one, three, two), work, state)
+    group = lax.broadcasted_iota(jnp.int32, (8, 128), 1) >> 4
+    for half in range(2):
+        tiles = [knots[8 * q : 8 * q + 8, 128 * half : 128 * half + 128] for q in range(8)]
+        for stage in (1, 2, 4):
+            at_first = (group & stage) == 0
+            for q in range(8):
+                if q & stage == 0:
+                    here, there = tiles[q], tiles[q + stage]
+                    tiles[q] = jnp.where(at_first, here, pltpu.roll(there, 16 * stage, 1))
+                    tiles[q + stage] = jnp.where(at_first, pltpu.roll(here, 128 - 16 * stage, 1), there)
+        for at in range(8):
+            blocks_ref[8 * half + at, 0:8] = tiles[at]
+            blocks_ref[8 * half + at, 8:16] = energy
 
 
 def assembled(knots):
     lane = lax.broadcasted_iota(jnp.int32, (16, 256), 1)
     row = lax.broadcasted_iota(jnp.int32, (16, 256), 0)
-    beyond = jnp.where(row < 12, knots[64:80], 0.0)
-    low = knots[0:16] + jnp.where(lane == 0, 0.0, pltpu.roll(beyond, 1, 1))
-    high = jnp.where(row < 12, jnp.where(lane == 255, beyond, pltpu.roll(low, 255, 1)), 0.0)
-    return jnp.concatenate([low, knots[16:64], high], axis=0)
+    after_end = jnp.concatenate([knots[64:72, 128:129], knots[64:72, 129:130]], axis=0)
+    following = jnp.where(lane == 255, after_end, pltpu.roll(knots[0:16], 255, 1))
+    return jnp.concatenate([knots[0:64], jnp.where(row < 12, following, 0.0)], axis=0)
 
 
 def energy_of(knots):
-    return jnp.sum(knots[76:80])
+    return jnp.sum(knots[64:72, 0:128])
 
 
 def folded(left, right):
     product = left[0:64] * right[0:64]
-    product = product[:, 0:128] + product[:, 128:256]
-    return functools.reduce(jnp.add, [tile(product, at) for at in range(8)])
+    return jnp.sum(product[:, 0:128] + product[:, 128:256], axis=0, keepdims=True)
 
 
 def lane_blocks(value):
@@ -370,56 +369,71 @@
         low = low + lane_blocks(work[40:56, at] * jnp.where(knot_lane == 0.0, image, 0.0))
         total = total + dot_nt(split_rows(work[SOURCE_SPREAD, at] * image), hot_rows(source_numbers, work[SOURCE_LANE, at]))
     ends = end_tile(at_tm, jnp.sum(high, axis=1, keepdims=True), jnp.sum(low, axis=1, keepdims=True))
-    return join_rows(total), jnp.concatenate([square, jnp.zeros((7, 128), f32)], axis=0), ends
-
-
-def start_kernel(tm_ref, own, one, two, three, _work, _state, sums_ref, work, state):
-    residual = assembled(four((own, one, two, three)))
+    return join_rows(total), square, ends
+
+
+def start_kernel(tm_ref, own, one, three, two, _work, _state, sums_ref, work, state):
+    residual = assembled(four((own, one, three, two)))
     put(state, START, 0, residual)
     sums, square, ends = gather_and_sum(tm_ref[0], residual, work)
-    sums_ref[...] = jnp.concatenate([sums, square, folded(residual, residual), ends], axis=0)
-
-
-def next_kernel(tm_ref, own, one, two, three, _work, _state, sums_ref, work, state):
-    knots = four((own, one, two, three))
+    norm = folded(residual, residual)
+    sums_ref[...] = jnp.concatenate([sums, square, norm, jnp.zeros((6, 128), f32), ends], axis=0)
+
+
+def next_kernel(tm_ref, own, one, three, two, _work, _state, sums_ref, work, state):
+    knots = four((own, one, three, two))
     direction = get(state, START, 0, 80)
     mapped = assembled(knots) + damping * direction
-    norm_now = jnp.sum(get(state, BEFORE, 48, 8))
+    norm_now = jnp.sum(get(state, BEFORE, 41, 1))
     product = energy_of(knots) + damping * norm_now
     residual = direction - (norm_now / product) * mapped
     put(state, MAPPED, 0, mapped)
     put(state, RESIDUAL, 0, residual)
     put(state, SCALAR, 0, jnp.zeros((8, 128), f32) + product)
     sums, square, ends = gather_and_sum(tm_ref[0], residual, work)
-    sums_ref[...] = jnp.concatenate([sums, square, folded(residual, residual), folded(residual, mapped), ends], axis=0)
-
-
-def last_kernel(place_ref, blocks_ref, state, solution_ref, left_ref, source_ref):
+    norm, crossed = folded(residual, residual), folded(residual, mapped)
+    sums_ref[...] = jnp.concatenate([sums, square, norm, crossed, jnp.zeros((5, 128), f32), ends], axis=0)
+
+
+OWN = ((152, 128), f32)
+
+
+def own_kernel(place_ref, state, own_ref):
     place = place_ref[0]
-    blocks = functools.reduce(jnp.add, [blocks_ref[at] for at in range(16)])
     lane_place = lax.broadcasted_iota(jnp.int32, (8, 128), 1) >> 4
-
-    def own_lanes(lanes):
+    for at, lanes in enumerate((START, MAPPED, RESIDUAL)):
         result = jnp.zeros((8, 128), f32)
         for q in range(8):
             rows = get(state, lanes, 8 * q, 8)
             rows = jnp.where(place >= 8, rows[:, 128:256], rows[:, 0:128])
             rows = pltpu.roll(rows, (16 * (q - place)) & 127, 1)
             result = jnp.where(lane_place == q, rows, result)
-        return result
-
-    start, mapped, residual = own_lanes(START), own_lanes(MAPPED), own_lanes(RESIDUAL)
-    image = blocks[0:8] + damping * residual
-    before, after = get(state, BEFORE, 0, 56), get(state, AFTER, 0, 64)
-    norm_first = jnp.sum(before[48:56])
+        own_ref[8 * at : 8 * at + 8] = result
+    factor = kept_factor(state)
+    for at, value in enumerate((get(state, FACTOR_B, 40, 40), get(state, BEFORE, 0, 40), get(state, AFTER, 0, 40))):
+        start = 24 + 40 * at
+        own_ref[start : start + 40] = jnp.concatenate(chol_solve(factor, [tile(value, j) for j in range(5)]), axis=0)
+    norm_first = jnp.sum(get(state, BEFORE, 41, 1))
+    norm_now = jnp.sum(get(state, AFTER, 41, 1))
+    crossed = jnp.sum(get(state, AFTER, 42, 1))
     product_first = jnp.max(get(state, SCALAR, 0, 8))
     alpha_first = norm_first / product_first
-    norm_now = jnp.sum(after[48:56])
-    crossed = jnp.sum(after[56:64])
     beta = norm_now / norm_first
-    product = jnp.sum(blocks[8:16]) + damping * norm_now + beta * (2.0 * crossed + beta * product_first)
-    alpha = norm_now / product
+    product = damping * norm_now + beta * (2.0 * crossed + beta * product_first)
+    row = lax.broadcasted_iota(jnp.int32, (8, 128), 0)
+    scalars = jnp.zeros((8, 128), f32)
+    for at, value in enumerate((alpha_first, beta, norm_now, product)):
+        scalars = jnp.where(row == at, value, scalars)
+    own_ref[144:152] = scalars
+
+
+def last_kernel(blocks_ref, own_ref, solution_ref, left_ref, source_ref):
+    blocks = functools.reduce(jnp.add, [blocks_ref[at] for at in range(16)])
+    start, mapped, residual = own_ref[0:8], own_ref[8:16], own_ref[16:24]
+    alpha_first, beta, norm_now, product = (own_ref[144 + at : 145 + at] for at in range(4))
+    alpha = norm_now / (jnp.sum(blocks[8:16]) + product)
     from_start = alpha_first + alpha * beta
+    image = blocks[0:8] + damping * residual
     solution = from_start * start + alpha * residual
     left = residual - alpha * (image + beta * mapped)
     both = split_rows(jnp.concatenate([solution, left], axis=0))
@@ -434,12 +448,11 @@
         own_rows = halves[0][8 * at : 8 * at + 4] + halves[1][8 * at + 4 : 8 * at + 8]
         for c in range(4):
             ref[c] = own_rows[c : c + 1]
-    rhs = get(state, FACTOR_B, 40, 40)
-    target = [tile(rhs, j) - from_start * tile(before, j) - alpha * tile(after, j) for j in range(5)]
-    solved = chol_solve(kept_factor(state), target)
     for j in range(5):
+        plain, before, after = (own_ref[start + 8 * j : start + 8 * j + 8] for start in (24, 64, 104))
+        solved = plain - from_start * before - alpha * after
         for a in range(8):
-            source_ref[j : j + 1, 128 * a : 128 * a + 128] = solved[j][a : a + 1]
+            source_ref[j : j + 1, 128 * a : 128 * a + 128] = solved[a : a + 1]
 
 
 VMEM = pl.BlockSpec(memory_space=pltpu.VMEM)
@@ -464,7 +477,7 @@
 def ring_parts(value, axis):
     count = lax.axis_size(axis)
     return [value] + [
-        lax.ppermute(value, axis, [(at, (at + step) % count) for at in range(count)]) for step in (1, 2, 3)
+        lax.ppermute(value, axis, [(at, (at + step) % count) for at in range(count)]) for step in (1, 3, 2)
     ]
 
 
@@ -484,12 +497,13 @@
 
 
 def sky_parts(knots):
-    own, one, two, three = ring_parts(knots, "sky_1")
-    return ring_parts((own + two) + (one + three), "sky_0")
-
-
-KNOTS = ((80, 256), f32)
+    own, one, three, two = ring_parts(knots, "sky_1")
+    return ring_parts((one + three) + (two + own), "sky_0")
+
+
+KNOTS = ((72, 256), f32)
 GHOSTS = ((48, 128), f32)
+SUMS = ((56, 128), f32)
 
 
 def shards(obs_source, obs_knot, obs_count, src_design, att_design, obs_phase, obs_value, src_prior):
@@ -529,8 +543,8 @@
     parts = (
         onward,
         crossing(onward, 1),
+        crossing(jnp.concatenate([sums, earlier], axis=0), -1),
         lax.ppermute(sums, "tm_0", [(at, (at + 2) % 4) for at in range(4)]),
-        crossing(jnp.concatenate([sums, earlier], axis=0), -1),
         to_twin(twin),
     )
     knots, work, state = call(
@@ -538,22 +552,22 @@
     )
     parts = sky_parts(knots)
     kept = dict(scalars=1, aliases={5: 1, 6: 2})
-    sums, work, state = call(start_kernel, "start", [((64, 128), f32), WORK, STATE], tm, *parts, work, state, **kept)
+    sums, work, state = call(start_kernel, "start", [SUMS, WORK, STATE], tm, *parts, work, state, **kept)
     parts = tm_parts(sums)
     knots, work, state = call(back_kernel, "back", [KNOTS, WORK, STATE], tm, *parts, work, state, **kept)
     parts = sky_parts(knots)
-    sums, work, state = call(next_kernel, "next", [((72, 128), f32), WORK, STATE], tm, *parts, work, state, **kept)
+    sums, work, state = call(next_kernel, "next", [SUMS, WORK, STATE], tm, *parts, work, state, **kept)
     parts = tm_parts(sums)
     blocks, work, state = call(
         back_to_owners_kernel, "back_to_owners", [((16, 16, 128), f32), WORK, STATE], tm, *parts, work, state, **kept
     )
+    (own,) = call(own_kernel, "own", [OWN], place, state, scalars=1)
     blocks = lax.all_to_all(blocks, SKY, 0, 0, tiled=True)
     return call(
         last_kernel,
         "last",
         [((4, 1, 256), f32), ((4, 1, 256), f32), ((5, 1024), f32)],
-        place, blocks, state,
-        scalars=1,
+        blocks, own,
     )
 
 

time: 92 us -> 89.2 us (0.970)
  starting transfers between devices: 33.2 us -> 31.2 us
    all_to_all x1, starting transfers between devices: 5.25 us -> 3.51 us  [shards(): blocks = lax.all_to_all(blocks, SKY, 0, 0, tiled=True)]
    pallas_call x10 -> x11, Pallas kernels: 11.1 us -> 11.3 us  [call(): pl.pallas_call(kernel, out_shape=shapes, in_specs=specs, out_specs=[VMEM]...]
  transfers between devices with their start and end apart: 26 -> 26, of which waited for: 21 -> 20; matrix products, arithmetic and copies ran while one was open for 0% -> 0% of each run, Pallas kernels for 2% -> 3%
where the time goes in v5:
time: 89.2 us; the launch traced here: 89 us
  waiting for transfers between devices  44.8 us (50%)
  starting transfers between devices  31.2 us (35%)
  Pallas kernels  11.3 us (13%)
  between operations  1.6 us (2%)
    ppermute x18, waiting for transfers between devices, ring_parts(): lax.ppermute(value, axis, [(at, (at + step) % count) for at in range(coun...  28.3 us
    ppermute x18, starting transfers between devices, ring_parts(): lax.ppermute(value, axis, [(at, (at + step) % count) for at in range(coun...  21.4 us
    pallas_call x11, Pallas kernels, call(): pl.pallas_call(kernel, out_shape=shapes, in_specs=specs, out_specs=[VMEM]...  11.3 us
    all_to_all x1, waiting for transfers between devices, shards(): blocks = lax.all_to_all(blocks, SKY, 0, 0, tiled=True)  7.77 us
    ppermute x2, starting transfers between devices, crossing(): return lax.ppermute(value, TM, pairs)  4.26 us
    ppermute x1, waiting for transfers between devices, shards(): lax.ppermute(sums, 'tm_0', [(at, (at + 2) % 4) for at in range(4)])  4.23 us
    all_to_all x1, starting transfers between devices, shards(): blocks = lax.all_to_all(blocks, SKY, 0, 0, tiled=True)  3.51 us
    ppermute x4, waiting for transfers between devices, to_twin(): return lax.ppermute(value, 'tm_1', [(0, 1), (1, 0)])  3.42 us
  transfers between devices with their start and end apart: 26, of which 20 were waited for; matrix products, arithmetic and copies ran while one was open for 0% of the time, Pallas kernels for 3%

profile of v5, /device:TPU:0, one launch (start us, length us, event | category | flops | bytes accessed | tf_op | source)
XLA Modules:
  0.0 89.0 jit_solution(5687103536733103755)
XLA Ops:
  1.5 1.2 %source_sums.1 = (f32[128,4096]{1,0:T(8,128)S(1)}, f32[160,128]{1,0:T(8,128)S(1)}, f32[80,1408]{1,0:T(8,128)S(1)}) custom-call(s32[1]{0:T(128)S(6)} %copy.35.count_ref, s32[1]{0:T(128)} %bitcast.1.first_ref, s32[1,4096]{1,0:T(1,128)S(1)} %bitcast.11, f32[5,4096]{1,0:T(8,128)S(1)} %copy-done, ...), custom_call_target="tpu_custom_call", output_to_operand_aliasing={{2}: (6, {})} | custom-call | tf_op jit(solution)/shard_map/source_sums/pallas_call | solution.py:465
  3.5 1.6 %ghosts.1 = (f32[48,128]{1,0:T(8,128)S(1)}, f32[48,128]{1,0:T(8,128)S(1)}, f32[48,128]{1,0:T(8,128)S(1)}) custom-call(s32[1]{0:T(128)S(6)} %copy.35.count_ref, s32[1]{0:T(128)} %bitcast.tm_ref, s32[32,128]{1,0:T(8,128)S(1)} %bitcast.10, s32[1,4096]{1,0:T(1,128)S(1)} %bitcast.12, f32[5,4096]{1,0:T(8,128)S(1)} %copy-done, f32[128,4096]{1,0:T(8,128)S(1)} %knot_spread.1.work._work), custom_call_target="tpu_custom_call" | custom-call | tf_op jit(solution)/shard_map/ghosts/pallas_call | solution.py:465
  5.1 4.3 %collective-permute-start.2 = (f32[208,128]{1,0:T(8,128)S(1)}, f32[208,128]{1,0:T(8,128)S(1)}, u32[]{:S(2)}, u32[]{:S(2)}) collective-permute-start(f32[208,128]{1,0:T(8,128)S(1)} %get-tuple-element.43), channel_id=1, source_target_pairs={{0,7},{1,6},{2,1},{3,0},{4,3},{5,2},{6,5},{7,4},{8,15},{9,14},{10,... | collective-permute-start | bytes 319496 | tf_op jit(solution)/shard_map/ppermute | solution.py:487
  9.4 1.5 %collective-permute-start.3 = (f32[160,128]{1,0:T(8,128)S(1)}, f32[160,128]{1,0:T(8,128)S(1)}, u32[]{:S(2)}, u32[]{:S(2)}) collective-permute-start(f32[160,128]{1,0:T(8,128)S(1)} %add.34), channel_id=1, source_target_pairs={{0,4},{2,6},{4,0},{6,2},{1,5},{3,7},{5,1},{7,3},{8,12},{10,14},{12... | collective-permute-start | bytes 245768 | tf_op jit(solution)/shard_map/ppermute | solution.py:547
  12.1 4.2 %collective-permute-done.3.two = f32[160,128]{1,0:T(8,128)S(1)} collective-permute-done((f32[160,128]{1,0:T(8,128)S(1)}, f32[160,128]{1,0:T(8,128)S(1)}, u32[]{:S(2)}, u32[]{:S(2)}) %collective-permute-start.3) | collective-permute-done | bytes 81952 | tf_op jit(solution)/shard_map/ppermute | solution.py:547
  17.4 1.3 %first.1 = (f32[72,256]{1,0:T(8,128)S(1)}, f32[128,4096]{1,0:T(8,128)S(1)}, f32[80,1408]{1,0:T(8,128)S(1)}) custom-call(s32[1]{0:T(128)} %bitcast.tm_ref, f32[208,128]{1,0:T(8,128)S(1)} %get-tuple-element.44.own, f32[208,128]{1,0:T(8,128)S(1)} %collective-permute-done.1.one, ...), custom_call_target="tpu_custom_call", output_to_operand_aliasing={{1}: (6, {}), {2}: (7, {})} | custom-call | tf_op jit(solution)/shard_map/first/pallas_call | solution.py:465
  18.6 3.1 %collective-permute-start.7 = (f32[72,256]{1,0:T(8,128)S(1)}, f32[72,256]{1,0:T(8,128)S(1)}, u32[]{:S(2)}, u32[]{:S(2)}) collective-permute-start(f32[72,256]{1,0:T(8,128)S(1)} %get-tuple-element.29), channel_id=1, source_target_pairs={{0,16},{8,24},{16,0},{24,8},{1,17},{9,25},{17,1},{25,9},{2,18},{10... | collective-permute-start | bytes 221192 | tf_op jit(solution)/shard_map/ppermute | solution.py:480
  21.7 1.1 %collective-permute-start.6 = (f32[72,256]{1,0:T(8,128)S(1)}, f32[72,256]{1,0:T(8,128)S(1)}, u32[]{:S(2)}, u32[]{:S(2)}) collective-permute-start(f32[72,256]{1,0:T(8,128)S(1)} %get-tuple-element.29), channel_id=1, source_target_pairs={{0,24},{8,0},{16,8},{24,16},{1,25},{9,1},{17,9},{25,17},{2,26},{10... | collective-permute-start | bytes 221192 | tf_op jit(solution)/shard_map/ppermute | solution.py:480
  24.5 1.7 %collective-permute-done.6 = f32[72,256]{1,0:T(8,128)S(1)} collective-permute-done((f32[72,256]{1,0:T(8,128)S(1)}, f32[72,256]{1,0:T(8,128)S(1)}, u32[]{:S(2)}, u32[]{:S(2)}) %collective-permute-start.6) | collective-permute-done | bytes 73760 | tf_op jit(solution)/shard_map/ppermute | solution.py:480
  26.2 2.2 %collective-permute-done.5 = f32[72,256]{1,0:T(8,128)S(1)} collective-permute-done((f32[72,256]{1,0:T(8,128)S(1)}, f32[72,256]{1,0:T(8,128)S(1)}, u32[]{:S(2)}, u32[]{:S(2)}) %collective-permute-start.5) | collective-permute-done | bytes 73760 | tf_op jit(solution)/shard_map/ppermute | solution.py:480
  28.4 3.3 %collective-permute-start.10 = (f32[72,256]{1,0:T(8,128)S(1)}, f32[72,256]{1,0:T(8,128)S(1)}, u32[]{:S(2)}, u32[]{:S(2)}) collective-permute-start(f32[72,256]{1,0:T(8,128)S(1)} %add_add_fusion.1.own), channel_id=1, source_target_pairs={{0,64},{32,96},{64,0},{96,32},{1,65},{33,97},{65,1},{97,33},{2,66}... | collective-permute-start | bytes 221192 | tf_op jit(solution)/shard_map/ppermute | solution.py:480
  34.7 1.3 %collective-permute-done.9.three = f32[72,256]{1,0:T(8,128)S(1)} collective-permute-done((f32[72,256]{1,0:T(8,128)S(1)}, f32[72,256]{1,0:T(8,128)S(1)}, u32[]{:S(2)}, u32[]{:S(2)}) %collective-permute-start.9) | collective-permute-done | bytes 73760 | tf_op jit(solution)/shard_map/ppermute | solution.py:480
  36.0 2.3 %collective-permute-done.8.one = f32[72,256]{1,0:T(8,128)S(1)} collective-permute-done((f32[72,256]{1,0:T(8,128)S(1)}, f32[72,256]{1,0:T(8,128)S(1)}, u32[]{:S(2)}, u32[]{:S(2)}) %collective-permute-start.8) | collective-permute-done | bytes 73760 | tf_op jit(solution)/shard_map/ppermute | solution.py:480
  38.3 1.2 %start.1 = (f32[56,128]{1,0:T(8,128)S(1)}, f32[128,4096]{1,0:T(8,128)S(1)}, f32[80,1408]{1,0:T(8,128)S(1)}) custom-call(s32[1]{0:T(128)} %bitcast.tm_ref, f32[72,256]{1,0:T(8,128)S(1)} %add_add_fusion.1.own, f32[72,256]{1,0:T(8,128)S(1)} %collective-permute-done.8.one, ...), custom_call_target="tpu_custom_call", output_to_operand_aliasing={{1}: (5, {}), {2}: (6, {})} | custom-call | tf_op jit(solution)/shard_map/start/pallas_call | solution.py:465
  39.6 1.2 %collective-permute-done.11 = f32[56,128]{1,0:T(8,128)S(1)} collective-permute-done((f32[56,128]{1,0:T(8,128)S(1)}, f32[56,128]{1,0:T(8,128)S(1)}, u32[]{:S(2)}, u32[]{:S(2)}) %collective-permute-start.11) | collective-permute-done | bytes 28704 | tf_op jit(solution)/shard_map/ppermute | solution.py:491
  43.3 3.0 %collective-permute-done.14.two = f32[56,128]{1,0:T(8,128)S(1)} collective-permute-done((f32[56,128]{1,0:T(8,128)S(1)}, f32[56,128]{1,0:T(8,128)S(1)}, u32[]{:S(2)}, u32[]{:S(2)}) %collective-permute-start.14) | collective-permute-done | bytes 28704 | tf_op jit(solution)/shard_map/ppermute | solution.py:480
  46.3 1.1 %collective-permute-done.12.one = f32[56,128]{1,0:T(8,128)S(1)} collective-permute-done((f32[56,128]{1,0:T(8,128)S(1)}, f32[56,128]{1,0:T(8,128)S(1)}, u32[]{:S(2)}, u32[]{:S(2)}) %collective-permute-start.12) | collective-permute-done | bytes 28704 | tf_op jit(solution)/shard_map/ppermute | solution.py:480
  47.4 1.2 %back.1 = (f32[72,256]{1,0:T(8,128)S(1)}, f32[128,4096]{1,0:T(8,128)S(1)}, f32[80,1408]{1,0:T(8,128)S(1)}) custom-call(s32[1]{0:T(128)} %bitcast.tm_ref, f32[56,128]{1,0:T(8,128)S(1)} %add.38.own, f32[56,128]{1,0:T(8,128)S(1)} %collective-permute-done.12.one, ...), custom_call_target="tpu_custom_call", output_to_operand_aliasing={{1}: (5, {}), {2}: (6, {})} | custom-call | tf_op jit(solution)/shard_map/back/pallas_call | solution.py:465
  49.0 1.9 %collective-permute-start.16 = (f32[72,256]{1,0:T(8,128)S(1)}, f32[72,256]{1,0:T(8,128)S(1)}, u32[]{:S(2)}, u32[]{:S(2)}) collective-permute-start(f32[72,256]{1,0:T(8,128)S(1)} %get-tuple-element.35), channel_id=1, source_target_pairs={{0,24},{8,0},{16,8},{24,16},{1,25},{9,1},{17,9},{25,17},{2,26},{10... | collective-permute-start | bytes 221192 | tf_op jit(solution)/shard_map/ppermute | solution.py:480
  51.0 3.6 %collective-permute-done.17 = f32[72,256]{1,0:T(8,128)S(1)} collective-permute-done((f32[72,256]{1,0:T(8,128)S(1)}, f32[72,256]{1,0:T(8,128)S(1)}, u32[]{:S(2)}, u32[]{:S(2)}) %collective-permute-start.17) | collective-permute-done | bytes 73760 | tf_op jit(solution)/shard_map/ppermute | solution.py:480
  54.7 1.8 %collective-permute-done.15 = f32[72,256]{1,0:T(8,128)S(1)} collective-permute-done((f32[72,256]{1,0:T(8,128)S(1)}, f32[72,256]{1,0:T(8,128)S(1)}, u32[]{:S(2)}, u32[]{:S(2)}) %collective-permute-start.15) | collective-permute-done | bytes 73760 | tf_op jit(solution)/shard_map/ppermute | solution.py:480
  57.1 1.9 %collective-permute-start.19 = (f32[72,256]{1,0:T(8,128)S(1)}, f32[72,256]{1,0:T(8,128)S(1)}, u32[]{:S(2)}, u32[]{:S(2)}) collective-permute-start(f32[72,256]{1,0:T(8,128)S(1)} %add_add_fusion.own), channel_id=1, source_target_pairs={{0,96},{32,0},{64,32},{96,64},{1,97},{33,1},{65,33},{97,65},{2,98}... | collective-permute-start | bytes 221192 | tf_op jit(solution)/shard_map/ppermute | solution.py:480
  59.1 3.4 %collective-permute-done.20.two = f32[72,256]{1,0:T(8,128)S(1)} collective-permute-done((f32[72,256]{1,0:T(8,128)S(1)}, f32[72,256]{1,0:T(8,128)S(1)}, u32[]{:S(2)}, u32[]{:S(2)}) %collective-permute-start.20) | collective-permute-done | bytes 73760 | tf_op jit(solution)/shard_map/ppermute | solution.py:480
  62.5 2.1 %collective-permute-done.18.one = f32[72,256]{1,0:T(8,128)S(1)} collective-permute-done((f32[72,256]{1,0:T(8,128)S(1)}, f32[72,256]{1,0:T(8,128)S(1)}, u32[]{:S(2)}, u32[]{:S(2)}) %collective-permute-start.18) | collective-permute-done | bytes 73760 | tf_op jit(solution)/shard_map/ppermute | solution.py:480
  64.6 1.3 %next.1 = (f32[56,128]{1,0:T(8,128)S(1)}, f32[128,4096]{1,0:T(8,128)S(1)}, f32[80,1408]{1,0:T(8,128)S(1)}) custom-call(s32[1]{0:T(128)} %bitcast.tm_ref, f32[72,256]{1,0:T(8,128)S(1)} %add_add_fusion.own, f32[72,256]{1,0:T(8,128)S(1)} %collective-permute-done.18.one, ...), custom_call_target="tpu_custom_call", output_to_operand_aliasing={{1}: (5, {}), {2}: (6, {})} | custom-call | tf_op jit(solution)/shard_map/next/pallas_call | solution.py:465
  65.9 1.2 %collective-permute-done.21 = f32[56,128]{1,0:T(8,128)S(1)} collective-permute-done((f32[56,128]{1,0:T(8,128)S(1)}, f32[56,128]{1,0:T(8,128)S(1)}, u32[]{:S(2)}, u32[]{:S(2)}) %collective-permute-start.21) | collective-permute-done | bytes 28704 | tf_op jit(solution)/shard_map/ppermute | solution.py:491
  67.1 1.4 %collective-permute-start.24 = (f32[56,128]{1,0:T(8,128)S(1)}, f32[56,128]{1,0:T(8,128)S(1)}, u32[]{:S(2)}, u32[]{:S(2)}) collective-permute-start(f32[56,128]{1,0:T(8,128)S(1)} %add.42.own), channel_id=1, source_target_pairs={{0,4},{2,6},{4,0},{6,2},{1,5},{3,7},{5,1},{7,3},{8,12},{10,14},{12... | collective-permute-start | bytes 86024 | tf_op jit(solution)/shard_map/ppermute | solution.py:480
  70.6 1.9 %collective-permute-done.24.two = f32[56,128]{1,0:T(8,128)S(1)} collective-permute-done((f32[56,128]{1,0:T(8,128)S(1)}, f32[56,128]{1,0:T(8,128)S(1)}, u32[]{:S(2)}, u32[]{:S(2)}) %collective-permute-start.24) | collective-permute-done | bytes 28704 | tf_op jit(solution)/shard_map/ppermute | solution.py:480
  72.5 2.2 %collective-permute-done.22.one = f32[56,128]{1,0:T(8,128)S(1)} collective-permute-done((f32[56,128]{1,0:T(8,128)S(1)}, f32[56,128]{1,0:T(8,128)S(1)}, u32[]{:S(2)}, u32[]{:S(2)}) %collective-permute-start.22) | collective-permute-done | bytes 28704 | tf_op jit(solution)/shard_map/ppermute | solution.py:480
  74.7 2.0 %back_to_owners.1 = (f32[16,16,128]{2,1,0:T(8,128)}, f32[128,4096]{1,0:T(8,128)S(1)}, f32[80,1408]{1,0:T(8,128)S(1)}) custom-call(s32[1]{0:T(128)} %bitcast.tm_ref, f32[56,128]{1,0:T(8,128)S(1)} %add.42.own, f32[56,128]{1,0:T(8,128)S(1)} %collective-permute-done.22.one, ...), custom_call_target="tpu_custom_call", output_to_operand_aliasing={{1}: (5, {}), {2}: (6, {})} | custom-call | tf_op jit(solution)/shard_map/back_to_owners/pallas_call | solution.py:465
  76.7 3.5 %all-to-all-start = ((f32[16,16,128]{2,1,0:T(8,128)}), f32[16,16,128]{2,1,0:T(8,128)S(1)}, u32[]{:S(2)}, u32[]{:S(2)}) async-start(f32[16,16,128]{2,1,0:T(8,128)} %get-tuple-element.41), calls=%async_computation | async-start | bytes 262144 | tf_op jit(solution)/shard_map/all_to_all | solution.py:565
  80.4 7.8 %all-to-all-done.blocks_ref = f32[16,16,128]{2,1,0:T(8,128)S(1)} async-done(((f32[16,16,128]{2,1,0:T(8,128)}), f32[16,16,128]{2,1,0:T(8,128)S(1)}, u32[]{:S(2)}, u32[]{:S(2)}) %all-to-all-start) | async-done | bytes 131104 | tf_op jit(solution)/shard_map/all_to_all | solution.py:565
  (51 shorter events, 14.7 us)
Async XLA Ops:
  0.6 0.9 %copy-start = (f32[5,4096]{1,0:T(8,128)S(1)}, f32[5,4096]{1,0:T(8,128)}, u32[]{:S(2)}) copy-start(f32[5,4096]{1,0:T(8,128)} %g_ref.3) | copy-start | bytes 245764
  0.6 0.9 %copy-start.3 = (s32[4096]{0:T(1024)S(1)}, s32[4096]{0:T(1024)}, u32[]{:S(2)}) copy-start(s32[4096]{0:T(1024)} %param.8) | copy-start | bytes 49156
  0.7 0.9 %copy-start.4 = (f32[5,1024]{1,0:T(8,128)S(1)}, f32[5,1024]{1,0:T(8,128)}, u32[]{:S(2)}) copy-start(f32[5,1024]{1,0:T(8,128)} %prior_ref.1) | copy-start | bytes 61444
  0.7 2.2 %copy-start.1 = (f32[4,4096]{1,0:T(4,128)S(1)}, f32[4,4096]{1,0:T(4,128)}, u32[]{:S(2)}) copy-start(f32[4,4096]{1,0:T(4,128)} %h_ref.1) | copy-start | bytes 196612
  0.7 2.2 %copy-start.2 = (s32[4096]{0:T(1024)S(1)}, s32[4096]{0:T(1024)}, u32[]{:S(2)}) copy-start(s32[4096]{0:T(1024)} %param.9) | copy-start | bytes 49156
  0.7 2.2 %copy-start.5 = (f32[4096]{0:T(1024)S(1)}, f32[4096]{0:T(1024)}, u32[]{:S(2)}) copy-start(f32[4096]{0:T(1024)} %param.13) | copy-start | bytes 49156
  2.8 2.2 %collective-permute-start = (f32[160,128]{1,0:T(8,128)S(1)}, f32[160,128]{1,0:T(8,128)S(1)}, u32[]{:S(2)}, u32[]{:S(2)}) collective-permute-start(f32[160,128]{1,0:T(8,128)S(1)} %get-tuple-element.23), channel_id=1, source_target_pairs={{0,1},{1,0},{2,3},{3,2},{4,5},{5,4},{6,7},{7,6},{8,9},{9,8},{10,11... | collective-permute-start | bytes 245768 | tf_op jit(solution)/shard_map/ppermute | solution.py:491
  5.1 11.2 %collective-permute-start.2 = (f32[208,128]{1,0:T(8,128)S(1)}, f32[208,128]{1,0:T(8,128)S(1)}, u32[]{:S(2)}, u32[]{:S(2)}) collective-permute-start(f32[208,128]{1,0:T(8,128)S(1)} %get-tuple-element.43), channel_id=1, source_target_pairs={{0,7},{1,6},{2,1},{3,0},{4,3},{5,2},{6,5},{7,4},{8,15},{9,14},{10,... | collective-permute-start | bytes 319496 | tf_op jit(solution)/shard_map/ppermute | solution.py:487
  9.4 8.0 %collective-permute-start.1 = (f32[208,128]{1,0:T(8,128)S(1)}, f32[208,128]{1,0:T(8,128)S(1)}, u32[]{:S(2)}, u32[]{:S(2)}) collective-permute-start(f32[208,128]{1,0:T(8,128)S(1)} %get-tuple-element.44.own), channel_id=1, source_target_pairs={{0,3},{1,2},{2,5},{3,4},{4,7},{5,6},{6,1},{7,0},{8,11},{9,10},{10,... | collective-permute-start | bytes 319496 | tf_op jit(solution)/shard_map/ppermute | solution.py:487
  9.4 7.0 %collective-permute-start.3 = (f32[160,128]{1,0:T(8,128)S(1)}, f32[160,128]{1,0:T(8,128)S(1)}, u32[]{:S(2)}, u32[]{:S(2)}) collective-permute-start(f32[160,128]{1,0:T(8,128)S(1)} %add.34), channel_id=1, source_target_pairs={{0,4},{2,6},{4,0},{6,2},{1,5},{3,7},{5,1},{7,3},{8,12},{10,14},{12... | collective-permute-start | bytes 245768 | tf_op jit(solution)/shard_map/ppermute | solution.py:547
  10.9 1.2 %collective-permute-start.4 = (f32[48,128]{1,0:T(8,128)S(1)}, f32[48,128]{1,0:T(8,128)S(1)}, u32[]{:S(2)}, u32[]{:S(2)}) collective-permute-start(f32[48,128]{1,0:T(8,128)S(1)} %get-tuple-element.27), channel_id=1, source_target_pairs={{0,1},{1,0},{2,3},{3,2},{4,5},{5,4},{6,7},{7,6},{8,9},{9,8},{10,11... | collective-permute-start | bytes 73736 | tf_op jit(solution)/shard_map/ppermute | solution.py:491
  18.6 5.9 %collective-permute-start.7 = (f32[72,256]{1,0:T(8,128)S(1)}, f32[72,256]{1,0:T(8,128)S(1)}, u32[]{:S(2)}, u32[]{:S(2)}) collective-permute-start(f32[72,256]{1,0:T(8,128)S(1)} %get-tuple-element.29), channel_id=1, source_target_pairs={{0,16},{8,24},{16,0},{24,8},{1,17},{9,25},{17,1},{25,9},{2,18},{10... | collective-permute-start | bytes 221192 | tf_op jit(solution)/shard_map/ppermute | solution.py:480
  21.7 4.5 %collective-permute-start.6 = (f32[72,256]{1,0:T(8,128)S(1)}, f32[72,256]{1,0:T(8,128)S(1)}, u32[]{:S(2)}, u32[]{:S(2)}) collective-permute-start(f32[72,256]{1,0:T(8,128)S(1)} %get-tuple-element.29), channel_id=1, source_target_pairs={{0,24},{8,0},{16,8},{24,16},{1,25},{9,1},{17,9},{25,17},{2,26},{10... | collective-permute-start | bytes 221192 | tf_op jit(solution)/shard_map/ppermute | solution.py:480
  22.8 5.6 %collective-permute-start.5 = (f32[72,256]{1,0:T(8,128)S(1)}, f32[72,256]{1,0:T(8,128)S(1)}, u32[]{:S(2)}, u32[]{:S(2)}) collective-permute-start(f32[72,256]{1,0:T(8,128)S(1)} %get-tuple-element.29), channel_id=1, source_target_pairs={{0,8},{8,16},{16,24},{24,0},{1,9},{9,17},{17,25},{25,1},{2,10},{10... | collective-permute-start | bytes 221192 | tf_op jit(solution)/shard_map/ppermute | solution.py:480
  28.4 6.3 %collective-permute-start.10 = (f32[72,256]{1,0:T(8,128)S(1)}, f32[72,256]{1,0:T(8,128)S(1)}, u32[]{:S(2)}, u32[]{:S(2)}) collective-permute-start(f32[72,256]{1,0:T(8,128)S(1)} %add_add_fusion.1.own), channel_id=1, source_target_pairs={{0,64},{32,96},{64,0},{96,32},{1,65},{33,97},{65,1},{97,33},{2,66}... | collective-permute-start | bytes 221192 | tf_op jit(solution)/shard_map/ppermute | solution.py:480
  31.7 4.4 %collective-permute-start.9 = (f32[72,256]{1,0:T(8,128)S(1)}, f32[72,256]{1,0:T(8,128)S(1)}, u32[]{:S(2)}, u32[]{:S(2)}) collective-permute-start(f32[72,256]{1,0:T(8,128)S(1)} %add_add_fusion.1.own), channel_id=1, source_target_pairs={{0,96},{32,0},{64,32},{96,64},{1,97},{33,1},{65,33},{97,65},{2,98}... | collective-permute-start | bytes 221192 | tf_op jit(solution)/shard_map/ppermute | solution.py:480
  32.7 5.6 %collective-permute-start.8 = (f32[72,256]{1,0:T(8,128)S(1)}, f32[72,256]{1,0:T(8,128)S(1)}, u32[]{:S(2)}, u32[]{:S(2)}) collective-permute-start(f32[72,256]{1,0:T(8,128)S(1)} %add_add_fusion.1.own), channel_id=1, source_target_pairs={{0,32},{32,64},{64,96},{96,0},{1,33},{33,65},{65,97},{97,1},{2,34}... | collective-permute-start | bytes 221192 | tf_op jit(solution)/shard_map/ppermute | solution.py:480
  39.5 1.3 %collective-permute-start.11 = (f32[56,128]{1,0:T(8,128)S(1)}, f32[56,128]{1,0:T(8,128)S(1)}, u32[]{:S(2)}, u32[]{:S(2)}) collective-permute-start(f32[56,128]{1,0:T(8,128)S(1)} %get-tuple-element.32), channel_id=1, source_target_pairs={{0,1},{1,0},{2,3},{3,2},{4,5},{5,4},{6,7},{7,6},{8,9},{9,8},{10,11... | collective-permute-start | bytes 86024 | tf_op jit(solution)/shard_map/ppermute | solution.py:491
  40.8 5.5 %collective-permute-start.14 = (f32[56,128]{1,0:T(8,128)S(1)}, f32[56,128]{1,0:T(8,128)S(1)}, u32[]{:S(2)}, u32[]{:S(2)}) collective-permute-start(f32[56,128]{1,0:T(8,128)S(1)} %add.38.own), channel_id=1, source_target_pairs={{0,4},{2,6},{4,0},{6,2},{1,5},{3,7},{5,1},{7,3},{8,12},{10,14},{12... | collective-permute-start | bytes 86024 | tf_op jit(solution)/shard_map/ppermute | solution.py:480
  41.3 5.0 %collective-permute-start.13 = (f32[56,128]{1,0:T(8,128)S(1)}, f32[56,128]{1,0:T(8,128)S(1)}, u32[]{:S(2)}, u32[]{:S(2)}) collective-permute-start(f32[56,128]{1,0:T(8,128)S(1)} %add.38.own), channel_id=1, source_target_pairs={{0,6},{2,0},{4,2},{6,4},{1,7},{3,1},{5,3},{7,5},{8,14},{10,8},{12,... | collective-permute-start | bytes 86024 | tf_op jit(solution)/shard_map/ppermute | solution.py:480
  42.3 5.1 %collective-permute-start.12 = (f32[56,128]{1,0:T(8,128)S(1)}, f32[56,128]{1,0:T(8,128)S(1)}, u32[]{:S(2)}, u32[]{:S(2)}) collective-permute-start(f32[56,128]{1,0:T(8,128)S(1)} %add.38.own), channel_id=1, source_target_pairs={{0,2},{2,4},{4,6},{6,0},{1,3},{3,5},{5,7},{7,1},{8,10},{10,12},{12... | collective-permute-start | bytes 86024 | tf_op jit(solution)/shard_map/ppermute | solution.py:480
  48.5 6.1 %collective-permute-start.17 = (f32[72,256]{1,0:T(8,128)S(1)}, f32[72,256]{1,0:T(8,128)S(1)}, u32[]{:S(2)}, u32[]{:S(2)}) collective-permute-start(f32[72,256]{1,0:T(8,128)S(1)} %get-tuple-element.35), channel_id=1, source_target_pairs={{0,16},{8,24},{16,0},{24,8},{1,17},{9,25},{17,1},{25,9},{2,18},{10... | collective-permute-start | bytes 221192 | tf_op jit(solution)/shard_map/ppermute | solution.py:480
  49.0 5.6 %collective-permute-start.16 = (f32[72,256]{1,0:T(8,128)S(1)}, f32[72,256]{1,0:T(8,128)S(1)}, u32[]{:S(2)}, u32[]{:S(2)}) collective-permute-start(f32[72,256]{1,0:T(8,128)S(1)} %get-tuple-element.35), channel_id=1, source_target_pairs={{0,24},{8,0},{16,8},{24,16},{1,25},{9,1},{17,9},{25,17},{2,26},{10... | collective-permute-start | bytes 221192 | tf_op jit(solution)/shard_map/ppermute | solution.py:480
  50.9 5.6 %collective-permute-start.15 = (f32[72,256]{1,0:T(8,128)S(1)}, f32[72,256]{1,0:T(8,128)S(1)}, u32[]{:S(2)}, u32[]{:S(2)}) collective-permute-start(f32[72,256]{1,0:T(8,128)S(1)} %get-tuple-element.35), channel_id=1, source_target_pairs={{0,8},{8,16},{16,24},{24,0},{1,9},{9,17},{17,25},{25,1},{2,10},{10... | collective-permute-start | bytes 221192 | tf_op jit(solution)/shard_map/ppermute | solution.py:480
  56.5 5.9 %collective-permute-start.20 = (f32[72,256]{1,0:T(8,128)S(1)}, f32[72,256]{1,0:T(8,128)S(1)}, u32[]{:S(2)}, u32[]{:S(2)}) collective-permute-start(f32[72,256]{1,0:T(8,128)S(1)} %add_add_fusion.own), channel_id=1, source_target_pairs={{0,64},{32,96},{64,0},{96,32},{1,65},{33,97},{65,1},{97,33},{2,66}... | collective-permute-start | bytes 221192 | tf_op jit(solution)/shard_map/ppermute | solution.py:480
  57.1 5.4 %collective-permute-start.19 = (f32[72,256]{1,0:T(8,128)S(1)}, f32[72,256]{1,0:T(8,128)S(1)}, u32[]{:S(2)}, u32[]{:S(2)}) collective-permute-start(f32[72,256]{1,0:T(8,128)S(1)} %add_add_fusion.own), channel_id=1, source_target_pairs={{0,96},{32,0},{64,32},{96,64},{1,97},{33,1},{65,33},{97,65},{2,98}... | collective-permute-start | bytes 221192 | tf_op jit(solution)/shard_map/ppermute | solution.py:480
  59.0 5.6 %collective-permute-start.18 = (f32[72,256]{1,0:T(8,128)S(1)}, f32[72,256]{1,0:T(8,128)S(1)}, u32[]{:S(2)}, u32[]{:S(2)}) collective-permute-start(f32[72,256]{1,0:T(8,128)S(1)} %add_add_fusion.own), channel_id=1, source_target_pairs={{0,32},{32,64},{64,96},{96,0},{1,33},{33,65},{65,97},{97,1},{2,34}... | collective-permute-start | bytes 221192 | tf_op jit(solution)/shard_map/ppermute | solution.py:480
  65.8 1.3 %collective-permute-start.21 = (f32[56,128]{1,0:T(8,128)S(1)}, f32[56,128]{1,0:T(8,128)S(1)}, u32[]{:S(2)}, u32[]{:S(2)}) collective-permute-start(f32[56,128]{1,0:T(8,128)S(1)} %get-tuple-element.38), channel_id=1, source_target_pairs={{0,1},{1,0},{2,3},{3,2},{4,5},{5,4},{6,7},{7,6},{8,9},{9,8},{10,11... | collective-permute-start | bytes 86024 | tf_op jit(solution)/shard_map/ppermute | solution.py:491
  67.1 5.4 %collective-permute-start.24 = (f32[56,128]{1,0:T(8,128)S(1)}, f32[56,128]{1,0:T(8,128)S(1)}, u32[]{:S(2)}, u32[]{:S(2)}) collective-permute-start(f32[56,128]{1,0:T(8,128)S(1)} %add.42.own), channel_id=1, source_target_pairs={{0,4},{2,6},{4,0},{6,2},{1,5},{3,7},{5,1},{7,3},{8,12},{10,14},{12... | collective-permute-start | bytes 86024 | tf_op jit(solution)/shard_map/ppermute | solution.py:480
  68.6 3.9 %collective-permute-start.23 = (f32[56,128]{1,0:T(8,128)S(1)}, f32[56,128]{1,0:T(8,128)S(1)}, u32[]{:S(2)}, u32[]{:S(2)}) collective-permute-start(f32[56,128]{1,0:T(8,128)S(1)} %add.42.own), channel_id=1, source_target_pairs={{0,6},{2,0},{4,2},{6,4},{1,7},{3,1},{5,3},{7,5},{8,14},{10,8},{12,... | collective-permute-start | bytes 86024 | tf_op jit(solution)/shard_map/ppermute | solution.py:480
  69.6 5.1 %collective-permute-start.22 = (f32[56,128]{1,0:T(8,128)S(1)}, f32[56,128]{1,0:T(8,128)S(1)}, u32[]{:S(2)}, u32[]{:S(2)}) collective-permute-start(f32[56,128]{1,0:T(8,128)S(1)} %add.42.own), channel_id=1, source_target_pairs={{0,2},{2,4},{4,6},{6,0},{1,3},{3,5},{5,7},{7,1},{8,10},{10,12},{12... | collective-permute-start | bytes 86024 | tf_op jit(solution)/shard_map/ppermute | solution.py:480
  76.7 11.5 %all-to-all-start = ((f32[16,16,128]{2,1,0:T(8,128)}), f32[16,16,128]{2,1,0:T(8,128)S(1)}, u32[]{:S(2)}, u32[]{:S(2)}) async-start(f32[16,16,128]{2,1,0:T(8,128)} %get-tuple-element.41), calls=%async_computation | async-start | bytes 262144 | tf_op jit(solution)/shard_map/all_to_all | solution.py:565
  (1 other events, 0.9 us)

commit v6 on v5

--- a/solution.py
+++ b/solution.py
@@ -13,6 +13,7 @@
 SKY_TM = ("sky_0", "sky_1", "tm_0", "tm_1")
 
 OBS_DEV = 4096
+SEGMENTS = 8
 CHUNK = 4096
 damping = 0.5
 entry_pairs = [(row_at, col_at) for row_at in range(5) for col_at in range(row_at + 1)]
@@ -126,6 +127,25 @@
             sums_ref[8 * at : 8 * at + 8] += prior * once
 
 
+def spline_taps(phase):
+    squared = phase * phase
+    cubed = squared * phase
+    rest = 1.0 - phase
+    return (
+        rest * rest * rest / 6.0,
+        (3.0 * cubed - 6.0 * squared + 4.0) / 6.0,
+        (-3.0 * cubed + 3.0 * squared + 3.0 * phase + 1.0) / 6.0,
+        cubed / 6.0,
+    )
+
+
+def tap_at(taps, gap):
+    weight = jnp.where(gap == 0, taps[0], 0.0)
+    for m in range(1, 4):
+        weight = jnp.where(gap == m, taps[m], weight)
+    return weight
+
+
 def knot_kernel(count_ref, last_ref, knot_ref, h_ref, phase_ref, _work, work):
     upper = lax.broadcasted_iota(jnp.int32, (8, CHUNK), 0) >> 2
     for at in chunks():
@@ -135,31 +155,18 @@
         work[KNOT_LANE, at] = high.astype(f32)
         h = jnp.where(live, h_ref[:, at], 0.0)
         h = jnp.concatenate([h, h], axis=0)
-        phase = phase_ref[:, at]
-        squared = phase * phase
-        cubed = squared * phase
-        rest = 1.0 - phase
-        taps = (
-            rest * rest * rest / 6.0,
-            (3.0 * cubed - 6.0 * squared + 4.0) / 6.0,
-            (-3.0 * cubed + 3.0 * squared + 3.0 * phase + 1.0) / 6.0,
-            cubed / 6.0,
-        )
-        taps = [jnp.broadcast_to(tap, (8, CHUNK)) for tap in taps]
+        taps = [jnp.broadcast_to(tap, (8, CHUNK)) for tap in spline_taps(phase_ref[:, at])]
         ahead = upper - (knot & 15)
         kept = jnp.where((high == 255) & (last_ref[0] == 1), 0.0, 1.0)
         for q in range(10):
-            gap = ahead + 2 * q
-            weight = jnp.where(gap == 0, taps[0], 0.0)
-            for m in range(1, 4):
-                weight = jnp.where(gap == m, taps[m], weight)
+            weight = tap_at(taps, ahead + 2 * q)
             if q >= 8:
                 weight = weight * kept
             row = KNOT_SPREAD.start + 8 * q
             work[row : row + 8, at] = weight * h
 
 
-def ghost_kernel(count_ref, tm_ref, flat_ref, source_ref, g_ref, work, earlier_ref, later_ref, twin_ref):
+def ghost_kernel(count_ref, tm_ref, flat_ref, knot_ref, source_ref, g_ref, h_ref, phase_ref, work, earlier_ref, later_ref, twin_ref):
     knot = flat_ref[...]
     order = lax.broadcasted_iota(jnp.int32, (32, 128), 0) * 128 + lax.broadcasted_iota(jnp.int32, (32, 128), 1)
     live = order < count_ref[0]
@@ -171,23 +178,35 @@
     ).astype(bf16)
     numbers = row_numbers(256, 128)
     at_low = live & (knot < 3) & (tm_ref[0] > 0)
-    for chosen, spread_at, ref in ((live & (knot >= 4093), 104, later_ref), (at_low, 40, earlier_ref)):
+    at_high = live & (knot >= 4093) & (tm_ref[0] < SEGMENTS - 1)
+    totals = []
+    for chosen, origin in ((at_high, 4096), (at_low, 0)):
         mark = jnp.where(chosen, 1.0, 0.0).astype(bf16)
         rank = dot_nn(mark, across) + jnp.sum(dot_nn(down, mark), axis=1, keepdims=True)
         rank = jnp.where(chosen, rank, -1.0)
-        total = jnp.zeros((72, 256), f32)
+        total = jnp.zeros((48, 256), f32)
         for at in chunks():
             first = at.start // 128
             slots = jnp.concatenate([hot_rows(numbers, rank[row : row + 1]) for row in range(first, first + CHUNK // 128)], axis=1)
+            place = (knot_ref[:, at] - origin).astype(f32)
             data = jnp.concatenate(
-                [work[spread_at : spread_at + 16, at], g_ref[:, at], source_ref[:, at].astype(f32), work[IMAGE, at], jnp.zeros((1, CHUNK), f32)],
+                [g_ref[:, at], source_ref[:, at].astype(f32), work[IMAGE, at], phase_ref[:, at], place, h_ref[:, at], jnp.zeros((3, CHUNK), f32)],
                 axis=0,
             )
             total = total + dot_nt(split_rows(data), slots)
-        total = join_rows(total)
-        ref[0:24] = total[:, 0:128]
-        ref[24:48] = total[:, 128:256]
+        totals.append(join_rows(total))
+    for total, ref in zip(totals, (later_ref, earlier_ref)):
+        ref[0:16] = total[:, 0:128]
+        ref[16:32] = total[:, 128:256]
     twin_ref[...] = jnp.where((tm_ref[0] & 1) == 1, earlier_ref[...], later_ref[...])
+
+
+def unpacked(packed):
+    taps = [jnp.broadcast_to(tap, (16, 512)) for tap in spline_taps(packed[7:8])]
+    row = lax.broadcasted_iota(jnp.int32, (16, 512), 0)
+    weight = tap_at(taps, (row >> 2) - packed[8:9].astype(jnp.int32))
+    h = jnp.concatenate([packed[9:13]] * 4, axis=0)
+    return jnp.concatenate([weight * h, packed[0:7], jnp.zeros((1, 512), f32)], axis=0)
 
 
 def ghost_sums(solved, ghosts, values):
@@ -278,14 +297,14 @@
 def first_kernel(tm_ref, own, one, three, two, twin, _work, _state, knots_ref, work, state):
     sums = (own[0:160] + two[...]) + (one[0:160] + three[0:160])
     odd = (tm_ref[0] & 1) == 1
-    earlier = jnp.where(odd, twin[...], one[160:208])
-    later = jnp.where(odd, three[160:208], twin[...])
+    earlier = jnp.where(odd, twin[...], one[160:192])
+    later = jnp.where(odd, three[160:192], twin[...])
     factor = factorize(factor_of(sums))
     stacked = jnp.concatenate([factor[pair] for pair in entry_pairs], axis=0)
     put(state, FACTOR_A, 0, stacked[0:80])
     put(state, FACTOR_B, 0, stacked[80:120])
     put(state, FACTOR_B, 40, sums[120:160])
-    ghosts = jnp.concatenate([earlier[0:24], earlier[24:48], later[0:24], later[24:48]], axis=1)
+    ghosts = unpacked(jnp.concatenate([earlier[0:16], earlier[16:32], later[0:16], later[16:32]], axis=1))
     put_ghosts(state, ghosts)
     solved = split_rows(jnp.concatenate(chol_solve(factor, [tile(sums, 15 + j) for j in range(5)]), axis=0))
     earlier, later = ghost_sums(solved, ghosts, ghosts[22:23])
@@ -502,7 +521,7 @@
 
 
 KNOTS = ((72, 256), f32)
-GHOSTS = ((48, 128), f32)
+GHOSTS = ((32, 128), f32)
 SUMS = ((56, 128), f32)
 
 
@@ -523,19 +542,11 @@
         scalars=2,
     )
     twin_sums = to_twin(sums)
-    (work,) = call(
-        knot_kernel,
-        "knot_spread",
-        [WORK],
-        obs_count, last, line(obs_knot), att_design, line(obs_phase), work,
-        scalars=2,
-        aliases={5: 0},
-    )
     earlier, later, twin = call(
         ghost_kernel,
         "ghosts",
         [GHOSTS] * 3,
-        obs_count, tm, obs_knot.reshape(32, 128), line(obs_source), src_design, work,
+        obs_count, tm, obs_knot.reshape(32, 128), line(obs_knot), line(obs_source), src_design, att_design, line(obs_phase), work,
         scalars=2,
     )
     sums = sums + twin_sums
@@ -546,6 +557,14 @@
         crossing(jnp.concatenate([sums, earlier], axis=0), -1),
         lax.ppermute(sums, "tm_0", [(at, (at + 2) % 4) for at in range(4)]),
         to_twin(twin),
+    )
+    (work,) = call(
+        knot_kernel,
+        "knot_spread",
+        [WORK],
+        obs_count, last, line(obs_knot), att_design, line(obs_phase), work,
+        scalars=2,
+        aliases={5: 0},
     )
     knots, work, state = call(
         first_kernel, "first", [KNOTS, WORK, STATE], tm, *parts, work, state, scalars=1, aliases={6: 1, 7: 2}

time: 89.2 us -> 88.7 us (level)
  transfers between devices with their start and end apart: 26 -> 26, of which waited for: 20 -> 20; matrix products, arithmetic and copies ran while one was open for 0% -> 0% of each run, Pallas kernels for 3% -> 2%
where the time goes in v6:
time: 88.7 us; the launch traced here: 88.5 us
  waiting for transfers between devices  44.1 us (50%)
  starting transfers between devices  31.3 us (35%)
  Pallas kernels  11.2 us (13%)
  between operations  1.58 us (2%)
    ppermute x18, waiting for transfers between devices, ring_parts(): lax.ppermute(value, axis, [(at, (at + step) % count) for at in range(coun...  28.4 us
    ppermute x18, starting transfers between devices, ring_parts(): lax.ppermute(value, axis, [(at, (at + step) % count) for at in range(coun...  21.6 us
    pallas_call x11, Pallas kernels, call(): pl.pallas_call(kernel, out_shape=shapes, in_specs=specs, out_specs=[VMEM]...  11.2 us
    all_to_all x1, waiting for transfers between devices, shards(): blocks = lax.all_to_all(blocks, SKY, 0, 0, tiled=True)  7.77 us
    ppermute x2, starting transfers between devices, crossing(): return lax.ppermute(value, TM, pairs)  4.26 us
    ppermute x1, waiting for transfers between devices, shards(): lax.ppermute(sums, 'tm_0', [(at, (at + 2) % 4) for at in range(4)])  4.07 us
    all_to_all x1, starting transfers between devices, shards(): blocks = lax.all_to_all(blocks, SKY, 0, 0, tiled=True)  3.51 us
    ppermute x4, waiting for transfers between devices, to_twin(): return lax.ppermute(value, 'tm_1', [(0, 1), (1, 0)])  2.89 us
  transfers between devices with their start and end apart: 26, of which 20 were waited for; matrix products, arithmetic and copies ran while one was open for 0% of the time, Pallas kernels for 2%

profile of v6, /device:TPU:0, one launch (start us, length us, event | category | flops | bytes accessed | tf_op | source)
XLA Modules:
  0.0 88.5 jit_solution(13604949375774703255)
XLA Ops:
  1.5 1.2 %source_sums.1 = (f32[128,4096]{1,0:T(8,128)S(1)}, f32[160,128]{1,0:T(8,128)S(1)}, f32[80,1408]{1,0:T(8,128)S(1)}) custom-call(s32[1]{0:T(128)S(6)} %copy.35.count_ref, s32[1]{0:T(128)} %bitcast.1.first_ref, s32[1,4096]{1,0:T(1,128)S(1)} %bitcast.14, f32[5,4096]{1,0:T(8,128)S(1)} %copy-done, ...), custom_call_target="tpu_custom_call", output_to_operand_aliasing={{2}: (6, {})} | custom-call | tf_op jit(solution)/shard_map/source_sums/pallas_call | solution.py:484
  2.9 1.5 %ghosts.1 = (f32[32,128]{1,0:T(8,128)S(1)}, f32[32,128]{1,0:T(8,128)S(1)}, f32[32,128]{1,0:T(8,128)S(1)}) custom-call(s32[1]{0:T(128)S(6)} %copy.35.count_ref, s32[1]{0:T(128)} %bitcast.tm_ref, s32[32,128]{1,0:T(8,128)S(1)} %bitcast.9, s32[1,4096]{1,0:T(1,128)S(1)} %bitcast.10, s32[1,4096]{1,0:T(1,128)S(1)} %bitcast.15, f32[5,4096]{1,0:T(8,128)S(1)} %copy-done, ...), custom_call_target="tpu_custom_call" | custom-call | tf_op jit(solution)/shard_map/ghosts/pallas_call | solution.py:484
  4.5 4.3 %collective-permute-start.2 = (f32[192,128]{1,0:T(8,128)S(1)}, f32[192,128]{1,0:T(8,128)S(1)}, u32[]{:S(2)}, u32[]{:S(2)}) collective-permute-start(f32[192,128]{1,0:T(8,128)S(1)} %get-tuple-element.43), channel_id=1, source_target_pairs={{0,7},{1,6},{2,1},{3,0},{4,3},{5,2},{6,5},{7,4},{8,15},{9,14},{10,... | collective-permute-start | bytes 294920 | tf_op jit(solution)/shard_map/ppermute | solution.py:506
  8.8 1.5 %collective-permute-start.3 = (f32[160,128]{1,0:T(8,128)S(1)}, f32[160,128]{1,0:T(8,128)S(1)}, u32[]{:S(2)}, u32[]{:S(2)}) collective-permute-start(f32[160,128]{1,0:T(8,128)S(1)} %add.34), channel_id=1, source_target_pairs={{0,4},{2,6},{4,0},{6,2},{1,5},{3,7},{5,1},{7,3},{8,12},{10,14},{12... | collective-permute-start | bytes 245768 | tf_op jit(solution)/shard_map/ppermute | solution.py:558
  11.5 4.1 %collective-permute-done.3.two = f32[160,128]{1,0:T(8,128)S(1)} collective-permute-done((f32[160,128]{1,0:T(8,128)S(1)}, f32[160,128]{1,0:T(8,128)S(1)}, u32[]{:S(2)}, u32[]{:S(2)}) %collective-permute-start.3) | collective-permute-done | bytes 81952 | tf_op jit(solution)/shard_map/ppermute | solution.py:558
  16.6 1.3 %first.1 = (f32[72,256]{1,0:T(8,128)S(1)}, f32[128,4096]{1,0:T(8,128)S(1)}, f32[80,1408]{1,0:T(8,128)S(1)}) custom-call(s32[1]{0:T(128)} %bitcast.tm_ref, f32[192,128]{1,0:T(8,128)S(1)} %get-tuple-element.44.own, f32[192,128]{1,0:T(8,128)S(1)} %collective-permute-done.1.one, ...), custom_call_target="tpu_custom_call", output_to_operand_aliasing={{1}: (6, {}), {2}: (7, {})} | custom-call | tf_op jit(solution)/shard_map/first/pallas_call | solution.py:484
  17.9 3.1 %collective-permute-start.7 = (f32[72,256]{1,0:T(8,128)S(1)}, f32[72,256]{1,0:T(8,128)S(1)}, u32[]{:S(2)}, u32[]{:S(2)}) collective-permute-start(f32[72,256]{1,0:T(8,128)S(1)} %get-tuple-element.29), channel_id=1, source_target_pairs={{0,16},{8,24},{16,0},{24,8},{1,17},{9,25},{17,1},{25,9},{2,18},{10... | collective-permute-start | bytes 221192 | tf_op jit(solution)/shard_map/ppermute | solution.py:499
  23.8 1.7 %collective-permute-done.6 = f32[72,256]{1,0:T(8,128)S(1)} collective-permute-done((f32[72,256]{1,0:T(8,128)S(1)}, f32[72,256]{1,0:T(8,128)S(1)}, u32[]{:S(2)}, u32[]{:S(2)}) %collective-permute-start.6) | collective-permute-done | bytes 73760 | tf_op jit(solution)/shard_map/ppermute | solution.py:499
  25.4 2.2 %collective-permute-done.5 = f32[72,256]{1,0:T(8,128)S(1)} collective-permute-done((f32[72,256]{1,0:T(8,128)S(1)}, f32[72,256]{1,0:T(8,128)S(1)}, u32[]{:S(2)}, u32[]{:S(2)}) %collective-permute-start.5) | collective-permute-done | bytes 73760 | tf_op jit(solution)/shard_map/ppermute | solution.py:499
  27.7 3.3 %collective-permute-start.10 = (f32[72,256]{1,0:T(8,128)S(1)}, f32[72,256]{1,0:T(8,128)S(1)}, u32[]{:S(2)}, u32[]{:S(2)}) collective-permute-start(f32[72,256]{1,0:T(8,128)S(1)} %add_add_fusion.1.own), channel_id=1, source_target_pairs={{0,64},{32,96},{64,0},{96,32},{1,65},{33,97},{65,1},{97,33},{2,66}... | collective-permute-start | bytes 221192 | tf_op jit(solution)/shard_map/ppermute | solution.py:499
  34.0 1.3 %collective-permute-done.9.three = f32[72,256]{1,0:T(8,128)S(1)} collective-permute-done((f32[72,256]{1,0:T(8,128)S(1)}, f32[72,256]{1,0:T(8,128)S(1)}, u32[]{:S(2)}, u32[]{:S(2)}) %collective-permute-start.9) | collective-permute-done | bytes 73760 | tf_op jit(solution)/shard_map/ppermute | solution.py:499
  35.3 2.3 %collective-permute-done.8.one = f32[72,256]{1,0:T(8,128)S(1)} collective-permute-done((f32[72,256]{1,0:T(8,128)S(1)}, f32[72,256]{1,0:T(8,128)S(1)}, u32[]{:S(2)}, u32[]{:S(2)}) %collective-permute-start.8) | collective-permute-done | bytes 73760 | tf_op jit(solution)/shard_map/ppermute | solution.py:499
  37.5 1.2 %start.1 = (f32[56,128]{1,0:T(8,128)S(1)}, f32[128,4096]{1,0:T(8,128)S(1)}, f32[80,1408]{1,0:T(8,128)S(1)}) custom-call(s32[1]{0:T(128)} %bitcast.tm_ref, f32[72,256]{1,0:T(8,128)S(1)} %add_add_fusion.1.own, f32[72,256]{1,0:T(8,128)S(1)} %collective-permute-done.8.one, ...), custom_call_target="tpu_custom_call", output_to_operand_aliasing={{1}: (5, {}), {2}: (6, {})} | custom-call | tf_op jit(solution)/shard_map/start/pallas_call | solution.py:484
  38.9 1.2 %collective-permute-done.11 = f32[56,128]{1,0:T(8,128)S(1)} collective-permute-done((f32[56,128]{1,0:T(8,128)S(1)}, f32[56,128]{1,0:T(8,128)S(1)}, u32[]{:S(2)}, u32[]{:S(2)}) %collective-permute-start.11) | collective-permute-done | bytes 28704 | tf_op jit(solution)/shard_map/ppermute | solution.py:510
  40.5 1.2 %collective-permute-start.13 = (f32[56,128]{1,0:T(8,128)S(1)}, f32[56,128]{1,0:T(8,128)S(1)}, u32[]{:S(2)}, u32[]{:S(2)}) collective-permute-start(f32[56,128]{1,0:T(8,128)S(1)} %add.38.own), channel_id=1, source_target_pairs={{0,6},{2,0},{4,2},{6,4},{1,7},{3,1},{5,3},{7,5},{8,14},{10,8},{12,... | collective-permute-start | bytes 86024 | tf_op jit(solution)/shard_map/ppermute | solution.py:499
  42.5 2.9 %collective-permute-done.14.two = f32[56,128]{1,0:T(8,128)S(1)} collective-permute-done((f32[56,128]{1,0:T(8,128)S(1)}, f32[56,128]{1,0:T(8,128)S(1)}, u32[]{:S(2)}, u32[]{:S(2)}) %collective-permute-start.14) | collective-permute-done | bytes 28704 | tf_op jit(solution)/shard_map/ppermute | solution.py:499
  45.4 1.3 %collective-permute-done.12.one = f32[56,128]{1,0:T(8,128)S(1)} collective-permute-done((f32[56,128]{1,0:T(8,128)S(1)}, f32[56,128]{1,0:T(8,128)S(1)}, u32[]{:S(2)}, u32[]{:S(2)}) %collective-permute-start.12) | collective-permute-done | bytes 28704 | tf_op jit(solution)/shard_map/ppermute | solution.py:499
  46.8 1.2 %back.1 = (f32[72,256]{1,0:T(8,128)S(1)}, f32[128,4096]{1,0:T(8,128)S(1)}, f32[80,1408]{1,0:T(8,128)S(1)}) custom-call(s32[1]{0:T(128)} %bitcast.tm_ref, f32[56,128]{1,0:T(8,128)S(1)} %add.38.own, f32[56,128]{1,0:T(8,128)S(1)} %collective-permute-done.12.one, ...), custom_call_target="tpu_custom_call", output_to_operand_aliasing={{1}: (5, {}), {2}: (6, {})} | custom-call | tf_op jit(solution)/shard_map/back/pallas_call | solution.py:484
  48.4 1.9 %collective-permute-start.16 = (f32[72,256]{1,0:T(8,128)S(1)}, f32[72,256]{1,0:T(8,128)S(1)}, u32[]{:S(2)}, u32[]{:S(2)}) collective-permute-start(f32[72,256]{1,0:T(8,128)S(1)} %get-tuple-element.35), channel_id=1, source_target_pairs={{0,24},{8,0},{16,8},{24,16},{1,25},{9,1},{17,9},{25,17},{2,26},{10... | collective-permute-start | bytes 221192 | tf_op jit(solution)/shard_map/ppermute | solution.py:499
  50.5 3.4 %collective-permute-done.17 = f32[72,256]{1,0:T(8,128)S(1)} collective-permute-done((f32[72,256]{1,0:T(8,128)S(1)}, f32[72,256]{1,0:T(8,128)S(1)}, u32[]{:S(2)}, u32[]{:S(2)}) %collective-permute-start.17) | collective-permute-done | bytes 73760 | tf_op jit(solution)/shard_map/ppermute | solution.py:499
  53.9 2.0 %collective-permute-done.15 = f32[72,256]{1,0:T(8,128)S(1)} collective-permute-done((f32[72,256]{1,0:T(8,128)S(1)}, f32[72,256]{1,0:T(8,128)S(1)}, u32[]{:S(2)}, u32[]{:S(2)}) %collective-permute-start.15) | collective-permute-done | bytes 73760 | tf_op jit(solution)/shard_map/ppermute | solution.py:499
  56.6 2.0 %collective-permute-start.19 = (f32[72,256]{1,0:T(8,128)S(1)}, f32[72,256]{1,0:T(8,128)S(1)}, u32[]{:S(2)}, u32[]{:S(2)}) collective-permute-start(f32[72,256]{1,0:T(8,128)S(1)} %add_add_fusion.own), channel_id=1, source_target_pairs={{0,96},{32,0},{64,32},{96,64},{1,97},{33,1},{65,33},{97,65},{2,98}... | collective-permute-start | bytes 221192 | tf_op jit(solution)/shard_map/ppermute | solution.py:499
  58.7 3.4 %collective-permute-done.20.two = f32[72,256]{1,0:T(8,128)S(1)} collective-permute-done((f32[72,256]{1,0:T(8,128)S(1)}, f32[72,256]{1,0:T(8,128)S(1)}, u32[]{:S(2)}, u32[]{:S(2)}) %collective-permute-start.20) | collective-permute-done | bytes 73760 | tf_op jit(solution)/shard_map/ppermute | solution.py:499
  62.0 2.1 %collective-permute-done.18.one = f32[72,256]{1,0:T(8,128)S(1)} collective-permute-done((f32[72,256]{1,0:T(8,128)S(1)}, f32[72,256]{1,0:T(8,128)S(1)}, u32[]{:S(2)}, u32[]{:S(2)}) %collective-permute-start.18) | collective-permute-done | bytes 73760 | tf_op jit(solution)/shard_map/ppermute | solution.py:499
  64.2 1.3 %next.1 = (f32[56,128]{1,0:T(8,128)S(1)}, f32[128,4096]{1,0:T(8,128)S(1)}, f32[80,1408]{1,0:T(8,128)S(1)}) custom-call(s32[1]{0:T(128)} %bitcast.tm_ref, f32[72,256]{1,0:T(8,128)S(1)} %add_add_fusion.own, f32[72,256]{1,0:T(8,128)S(1)} %collective-permute-done.18.one, ...), custom_call_target="tpu_custom_call", output_to_operand_aliasing={{1}: (5, {}), {2}: (6, {})} | custom-call | tf_op jit(solution)/shard_map/next/pallas_call | solution.py:484
  65.5 1.2 %collective-permute-done.21 = f32[56,128]{1,0:T(8,128)S(1)} collective-permute-done((f32[56,128]{1,0:T(8,128)S(1)}, f32[56,128]{1,0:T(8,128)S(1)}, u32[]{:S(2)}, u32[]{:S(2)}) %collective-permute-start.21) | collective-permute-done | bytes 28704 | tf_op jit(solution)/shard_map/ppermute | solution.py:510
  66.7 1.4 %collective-permute-start.24 = (f32[56,128]{1,0:T(8,128)S(1)}, f32[56,128]{1,0:T(8,128)S(1)}, u32[]{:S(2)}, u32[]{:S(2)}) collective-permute-start(f32[56,128]{1,0:T(8,128)S(1)} %add.42.own), channel_id=1, source_target_pairs={{0,4},{2,6},{4,0},{6,2},{1,5},{3,7},{5,1},{7,3},{8,12},{10,14},{12... | collective-permute-start | bytes 86024 | tf_op jit(solution)/shard_map/ppermute | solution.py:499
  70.2 1.9 %collective-permute-done.24.two = f32[56,128]{1,0:T(8,128)S(1)} collective-permute-done((f32[56,128]{1,0:T(8,128)S(1)}, f32[56,128]{1,0:T(8,128)S(1)}, u32[]{:S(2)}, u32[]{:S(2)}) %collective-permute-start.24) | collective-permute-done | bytes 28704 | tf_op jit(solution)/shard_map/ppermute | solution.py:499
  72.1 2.0 %collective-permute-done.22.one = f32[56,128]{1,0:T(8,128)S(1)} collective-permute-done((f32[56,128]{1,0:T(8,128)S(1)}, f32[56,128]{1,0:T(8,128)S(1)}, u32[]{:S(2)}, u32[]{:S(2)}) %collective-permute-start.22) | collective-permute-done | bytes 28704 | tf_op jit(solution)/shard_map/ppermute | solution.py:499
  74.1 2.0 %back_to_owners.1 = (f32[16,16,128]{2,1,0:T(8,128)}, f32[128,4096]{1,0:T(8,128)S(1)}, f32[80,1408]{1,0:T(8,128)S(1)}) custom-call(s32[1]{0:T(128)} %bitcast.tm_ref, f32[56,128]{1,0:T(8,128)S(1)} %add.42.own, f32[56,128]{1,0:T(8,128)S(1)} %collective-permute-done.22.one, ...), custom_call_target="tpu_custom_call", output_to_operand_aliasing={{1}: (5, {}), {2}: (6, {})} | custom-call | tf_op jit(solution)/shard_map/back_to_owners/pallas_call | solution.py:484
  76.1 3.5 %all-to-all-start = ((f32[16,16,128]{2,1,0:T(8,128)}), f32[16,16,128]{2,1,0:T(8,128)S(1)}, u32[]{:S(2)}, u32[]{:S(2)}) async-start(f32[16,16,128]{2,1,0:T(8,128)} %get-tuple-element.41), calls=%async_computation | async-start | bytes 262144 | tf_op jit(solution)/shard_map/all_to_all | solution.py:584
  79.8 7.8 %all-to-all-done.blocks_ref = f32[16,16,128]{2,1,0:T(8,128)S(1)} async-done(((f32[16,16,128]{2,1,0:T(8,128)}), f32[16,16,128]{2,1,0:T(8,128)S(1)}, u32[]{:S(2)}, u32[]{:S(2)}) %all-to-all-start) | async-done | bytes 131104 | tf_op jit(solution)/shard_map/all_to_all | solution.py:584
  (51 shorter events, 14.4 us)
Async XLA Ops:
  0.6 0.9 %copy-start = (f32[5,4096]{1,0:T(8,128)S(1)}, f32[5,4096]{1,0:T(8,128)}, u32[]{:S(2)}) copy-start(f32[5,4096]{1,0:T(8,128)} %g_ref.3) | copy-start | bytes 245764
  0.6 0.9 %copy-start.4 = (s32[4096]{0:T(1024)S(1)}, s32[4096]{0:T(1024)}, u32[]{:S(2)}) copy-start(s32[4096]{0:T(1024)} %param.8) | copy-start | bytes 49156
  0.7 0.9 %copy-start.5 = (f32[5,1024]{1,0:T(8,128)S(1)}, f32[5,1024]{1,0:T(8,128)}, u32[]{:S(2)}) copy-start(f32[5,1024]{1,0:T(8,128)} %prior_ref.1) | copy-start | bytes 61444
  0.7 2.2 %copy-start.1 = (f32[4,4096]{1,0:T(4,128)S(1)}, f32[4,4096]{1,0:T(4,128)}, u32[]{:S(2)}) copy-start(f32[4,4096]{1,0:T(4,128)} %h_ref.3) | copy-start | bytes 196612
  0.7 2.2 %copy-start.2 = (s32[4096]{0:T(1024)S(1)}, s32[4096]{0:T(1024)}, u32[]{:S(2)}) copy-start(s32[4096]{0:T(1024)} %param.9) | copy-start | bytes 49156
  0.7 2.2 %copy-start.3 = (f32[4096]{0:T(1024)S(1)}, f32[4096]{0:T(1024)}, u32[]{:S(2)}) copy-start(f32[4096]{0:T(1024)} %param.13) | copy-start | bytes 49156
  2.8 1.6 %collective-permute-start = (f32[160,128]{1,0:T(8,128)S(1)}, f32[160,128]{1,0:T(8,128)S(1)}, u32[]{:S(2)}, u32[]{:S(2)}) collective-permute-start(f32[160,128]{1,0:T(8,128)S(1)} %get-tuple-element.23), channel_id=1, source_target_pairs={{0,1},{1,0},{2,3},{3,2},{4,5},{5,4},{6,7},{7,6},{8,9},{9,8},{10,11... | collective-permute-start | bytes 245768 | tf_op jit(solution)/shard_map/ppermute | solution.py:510
  4.5 11.1 %collective-permute-start.2 = (f32[192,128]{1,0:T(8,128)S(1)}, f32[192,128]{1,0:T(8,128)S(1)}, u32[]{:S(2)}, u32[]{:S(2)}) collective-permute-start(f32[192,128]{1,0:T(8,128)S(1)} %get-tuple-element.43), channel_id=1, source_target_pairs={{0,7},{1,6},{2,1},{3,0},{4,3},{5,2},{6,5},{7,4},{8,15},{9,14},{10,... | collective-permute-start | bytes 294920 | tf_op jit(solution)/shard_map/ppermute | solution.py:506
  8.8 7.8 %collective-permute-start.1 = (f32[192,128]{1,0:T(8,128)S(1)}, f32[192,128]{1,0:T(8,128)S(1)}, u32[]{:S(2)}, u32[]{:S(2)}) collective-permute-start(f32[192,128]{1,0:T(8,128)S(1)} %get-tuple-element.44.own), channel_id=1, source_target_pairs={{0,3},{1,2},{2,5},{3,4},{4,7},{5,6},{6,1},{7,0},{8,11},{9,10},{10,... | collective-permute-start | bytes 294920 | tf_op jit(solution)/shard_map/ppermute | solution.py:506
  8.8 6.8 %collective-permute-start.3 = (f32[160,128]{1,0:T(8,128)S(1)}, f32[160,128]{1,0:T(8,128)S(1)}, u32[]{:S(2)}, u32[]{:S(2)}) collective-permute-start(f32[160,128]{1,0:T(8,128)S(1)} %add.34), channel_id=1, source_target_pairs={{0,4},{2,6},{4,0},{6,2},{1,5},{3,7},{5,1},{7,3},{8,12},{10,14},{12... | collective-permute-start | bytes 245768 | tf_op jit(solution)/shard_map/ppermute | solution.py:558
  10.3 1.2 %collective-permute-start.4 = (f32[32,128]{1,0:T(8,128)S(1)}, f32[32,128]{1,0:T(8,128)S(1)}, u32[]{:S(2)}, u32[]{:S(2)}) collective-permute-start(f32[32,128]{1,0:T(8,128)S(1)} %get-tuple-element.27), channel_id=1, source_target_pairs={{0,1},{1,0},{2,3},{3,2},{4,5},{5,4},{6,7},{7,6},{8,9},{9,8},{10,11... | collective-permute-start | bytes 49160 | tf_op jit(solution)/shard_map/ppermute | solution.py:510
  17.9 5.9 %collective-permute-start.7 = (f32[72,256]{1,0:T(8,128)S(1)}, f32[72,256]{1,0:T(8,128)S(1)}, u32[]{:S(2)}, u32[]{:S(2)}) collective-permute-start(f32[72,256]{1,0:T(8,128)S(1)} %get-tuple-element.29), channel_id=1, source_target_pairs={{0,16},{8,24},{16,0},{24,8},{1,17},{9,25},{17,1},{25,9},{2,18},{10... | collective-permute-start | bytes 221192 | tf_op jit(solution)/shard_map/ppermute | solution.py:499
  20.9 4.5 %collective-permute-start.6 = (f32[72,256]{1,0:T(8,128)S(1)}, f32[72,256]{1,0:T(8,128)S(1)}, u32[]{:S(2)}, u32[]{:S(2)}) collective-permute-start(f32[72,256]{1,0:T(8,128)S(1)} %get-tuple-element.29), channel_id=1, source_target_pairs={{0,24},{8,0},{16,8},{24,16},{1,25},{9,1},{17,9},{25,17},{2,26},{10... | collective-permute-start | bytes 221192 | tf_op jit(solution)/shard_map/ppermute | solution.py:499
  22.1 5.6 %collective-permute-start.5 = (f32[72,256]{1,0:T(8,128)S(1)}, f32[72,256]{1,0:T(8,128)S(1)}, u32[]{:S(2)}, u32[]{:S(2)}) collective-permute-start(f32[72,256]{1,0:T(8,128)S(1)} %get-tuple-element.29), channel_id=1, source_target_pairs={{0,8},{8,16},{16,24},{24,0},{1,9},{9,17},{17,25},{25,1},{2,10},{10... | collective-permute-start | bytes 221192 | tf_op jit(solution)/shard_map/ppermute | solution.py:499
  27.7 6.3 %collective-permute-start.10 = (f32[72,256]{1,0:T(8,128)S(1)}, f32[72,256]{1,0:T(8,128)S(1)}, u32[]{:S(2)}, u32[]{:S(2)}) collective-permute-start(f32[72,256]{1,0:T(8,128)S(1)} %add_add_fusion.1.own), channel_id=1, source_target_pairs={{0,64},{32,96},{64,0},{96,32},{1,65},{33,97},{65,1},{97,33},{2,66}... | collective-permute-start | bytes 221192 | tf_op jit(solution)/shard_map/ppermute | solution.py:499
  30.9 4.4 %collective-permute-start.9 = (f32[72,256]{1,0:T(8,128)S(1)}, f32[72,256]{1,0:T(8,128)S(1)}, u32[]{:S(2)}, u32[]{:S(2)}) collective-permute-start(f32[72,256]{1,0:T(8,128)S(1)} %add_add_fusion.1.own), channel_id=1, source_target_pairs={{0,96},{32,0},{64,32},{96,64},{1,97},{33,1},{65,33},{97,65},{2,98}... | collective-permute-start | bytes 221192 | tf_op jit(solution)/shard_map/ppermute | solution.py:499
  32.0 5.6 %collective-permute-start.8 = (f32[72,256]{1,0:T(8,128)S(1)}, f32[72,256]{1,0:T(8,128)S(1)}, u32[]{:S(2)}, u32[]{:S(2)}) collective-permute-start(f32[72,256]{1,0:T(8,128)S(1)} %add_add_fusion.1.own), channel_id=1, source_target_pairs={{0,32},{32,64},{64,96},{96,0},{1,33},{33,65},{65,97},{97,1},{2,34}... | collective-permute-start | bytes 221192 | tf_op jit(solution)/shard_map/ppermute | solution.py:499
  38.8 1.3 %collective-permute-start.11 = (f32[56,128]{1,0:T(8,128)S(1)}, f32[56,128]{1,0:T(8,128)S(1)}, u32[]{:S(2)}, u32[]{:S(2)}) collective-permute-start(f32[56,128]{1,0:T(8,128)S(1)} %get-tuple-element.32), channel_id=1, source_target_pairs={{0,1},{1,0},{2,3},{3,2},{4,5},{5,4},{6,7},{7,6},{8,9},{9,8},{10,11... | collective-permute-start | bytes 86024 | tf_op jit(solution)/shard_map/ppermute | solution.py:510
  40.0 5.4 %collective-permute-start.14 = (f32[56,128]{1,0:T(8,128)S(1)}, f32[56,128]{1,0:T(8,128)S(1)}, u32[]{:S(2)}, u32[]{:S(2)}) collective-permute-start(f32[56,128]{1,0:T(8,128)S(1)} %add.38.own), channel_id=1, source_target_pairs={{0,4},{2,6},{4,0},{6,2},{1,5},{3,7},{5,1},{7,3},{8,12},{10,14},{12... | collective-permute-start | bytes 86024 | tf_op jit(solution)/shard_map/ppermute | solution.py:499
  40.5 5.0 %collective-permute-start.13 = (f32[56,128]{1,0:T(8,128)S(1)}, f32[56,128]{1,0:T(8,128)S(1)}, u32[]{:S(2)}, u32[]{:S(2)}) collective-permute-start(f32[56,128]{1,0:T(8,128)S(1)} %add.38.own), channel_id=1, source_target_pairs={{0,6},{2,0},{4,2},{6,4},{1,7},{3,1},{5,3},{7,5},{8,14},{10,8},{12,... | collective-permute-start | bytes 86024 | tf_op jit(solution)/shard_map/ppermute | solution.py:499
  41.7 5.1 %collective-permute-start.12 = (f32[56,128]{1,0:T(8,128)S(1)}, f32[56,128]{1,0:T(8,128)S(1)}, u32[]{:S(2)}, u32[]{:S(2)}) collective-permute-start(f32[56,128]{1,0:T(8,128)S(1)} %add.38.own), channel_id=1, source_target_pairs={{0,2},{2,4},{4,6},{6,0},{1,3},{3,5},{5,7},{7,1},{8,10},{10,12},{12... | collective-permute-start | bytes 86024 | tf_op jit(solution)/shard_map/ppermute | solution.py:499
  47.9 6.0 %collective-permute-start.17 = (f32[72,256]{1,0:T(8,128)S(1)}, f32[72,256]{1,0:T(8,128)S(1)}, u32[]{:S(2)}, u32[]{:S(2)}) collective-permute-start(f32[72,256]{1,0:T(8,128)S(1)} %get-tuple-element.35), channel_id=1, source_target_pairs={{0,16},{8,24},{16,0},{24,8},{1,17},{9,25},{17,1},{25,9},{2,18},{10... | collective-permute-start | bytes 221192 | tf_op jit(solution)/shard_map/ppermute | solution.py:499
  48.4 5.5 %collective-permute-start.16 = (f32[72,256]{1,0:T(8,128)S(1)}, f32[72,256]{1,0:T(8,128)S(1)}, u32[]{:S(2)}, u32[]{:S(2)}) collective-permute-start(f32[72,256]{1,0:T(8,128)S(1)} %get-tuple-element.35), channel_id=1, source_target_pairs={{0,24},{8,0},{16,8},{24,16},{1,25},{9,1},{17,9},{25,17},{2,26},{10... | collective-permute-start | bytes 221192 | tf_op jit(solution)/shard_map/ppermute | solution.py:499
  50.3 5.6 %collective-permute-start.15 = (f32[72,256]{1,0:T(8,128)S(1)}, f32[72,256]{1,0:T(8,128)S(1)}, u32[]{:S(2)}, u32[]{:S(2)}) collective-permute-start(f32[72,256]{1,0:T(8,128)S(1)} %get-tuple-element.35), channel_id=1, source_target_pairs={{0,8},{8,16},{16,24},{24,0},{1,9},{9,17},{17,25},{25,1},{2,10},{10... | collective-permute-start | bytes 221192 | tf_op jit(solution)/shard_map/ppermute | solution.py:499
  55.9 6.1 %collective-permute-start.20 = (f32[72,256]{1,0:T(8,128)S(1)}, f32[72,256]{1,0:T(8,128)S(1)}, u32[]{:S(2)}, u32[]{:S(2)}) collective-permute-start(f32[72,256]{1,0:T(8,128)S(1)} %add_add_fusion.own), channel_id=1, source_target_pairs={{0,64},{32,96},{64,0},{96,32},{1,65},{33,97},{65,1},{97,33},{2,66}... | collective-permute-start | bytes 221192 | tf_op jit(solution)/shard_map/ppermute | solution.py:499
  56.6 5.4 %collective-permute-start.19 = (f32[72,256]{1,0:T(8,128)S(1)}, f32[72,256]{1,0:T(8,128)S(1)}, u32[]{:S(2)}, u32[]{:S(2)}) collective-permute-start(f32[72,256]{1,0:T(8,128)S(1)} %add_add_fusion.own), channel_id=1, source_target_pairs={{0,96},{32,0},{64,32},{96,64},{1,97},{33,1},{65,33},{97,65},{2,98}... | collective-permute-start | bytes 221192 | tf_op jit(solution)/shard_map/ppermute | solution.py:499
  58.6 5.6 %collective-permute-start.18 = (f32[72,256]{1,0:T(8,128)S(1)}, f32[72,256]{1,0:T(8,128)S(1)}, u32[]{:S(2)}, u32[]{:S(2)}) collective-permute-start(f32[72,256]{1,0:T(8,128)S(1)} %add_add_fusion.own), channel_id=1, source_target_pairs={{0,32},{32,64},{64,96},{96,0},{1,33},{33,65},{65,97},{97,1},{2,34}... | collective-permute-start | bytes 221192 | tf_op jit(solution)/shard_map/ppermute | solution.py:499
  65.4 1.3 %collective-permute-start.21 = (f32[56,128]{1,0:T(8,128)S(1)}, f32[56,128]{1,0:T(8,128)S(1)}, u32[]{:S(2)}, u32[]{:S(2)}) collective-permute-start(f32[56,128]{1,0:T(8,128)S(1)} %get-tuple-element.38), channel_id=1, source_target_pairs={{0,1},{1,0},{2,3},{3,2},{4,5},{5,4},{6,7},{7,6},{8,9},{9,8},{10,11... | collective-permute-start | bytes 86024 | tf_op jit(solution)/shard_map/ppermute | solution.py:510
  66.7 5.4 %collective-permute-start.24 = (f32[56,128]{1,0:T(8,128)S(1)}, f32[56,128]{1,0:T(8,128)S(1)}, u32[]{:S(2)}, u32[]{:S(2)}) collective-permute-start(f32[56,128]{1,0:T(8,128)S(1)} %add.42.own), channel_id=1, source_target_pairs={{0,4},{2,6},{4,0},{6,2},{1,5},{3,7},{5,1},{7,3},{8,12},{10,14},{12... | collective-permute-start | bytes 86024 | tf_op jit(solution)/shard_map/ppermute | solution.py:499
  68.1 3.9 %collective-permute-start.23 = (f32[56,128]{1,0:T(8,128)S(1)}, f32[56,128]{1,0:T(8,128)S(1)}, u32[]{:S(2)}, u32[]{:S(2)}) collective-permute-start(f32[56,128]{1,0:T(8,128)S(1)} %add.42.own), channel_id=1, source_target_pairs={{0,6},{2,0},{4,2},{6,4},{1,7},{3,1},{5,3},{7,5},{8,14},{10,8},{12,... | collective-permute-start | bytes 86024 | tf_op jit(solution)/shard_map/ppermute | solution.py:499
  69.0 5.1 %collective-permute-start.22 = (f32[56,128]{1,0:T(8,128)S(1)}, f32[56,128]{1,0:T(8,128)S(1)}, u32[]{:S(2)}, u32[]{:S(2)}) collective-permute-start(f32[56,128]{1,0:T(8,128)S(1)} %add.42.own), channel_id=1, source_target_pairs={{0,2},{2,4},{4,6},{6,0},{1,3},{3,5},{5,7},{7,1},{8,10},{10,12},{12... | collective-permute-start | bytes 86024 | tf_op jit(solution)/shard_map/ppermute | solution.py:499
  76.1 11.5 %all-to-all-start = ((f32[16,16,128]{2,1,0:T(8,128)}), f32[16,16,128]{2,1,0:T(8,128)S(1)}, u32[]{:S(2)}, u32[]{:S(2)}) async-start(f32[16,16,128]{2,1,0:T(8,128)} %get-tuple-element.41), calls=%async_computation | async-start | bytes 262144 | tf_op jit(solution)/shard_map/all_to_all | solution.py:584
  (1 other events, 0.9 us)

commit v7 on v6

--- a/solution.py
+++ b/solution.py
@@ -333,7 +333,7 @@
     knots_ref[...], _ = back(BEFORE, tm_ref[0], (own, one, three, two), work, state)
 
 
-def back_to_owners_kernel(tm_ref, own, one, three, two, _work, _state, blocks_ref, work, state):
+def back_to_owners_kernel(tm_ref, place_ref, own, one, three, two, _work, _state, blocks_ref, own_ref, work, state):
     knots, energy = back(AFTER, tm_ref[0], (own, one, three, two), work, state)
     group = lax.broadcasted_iota(jnp.int32, (8, 128), 1) >> 4
     for half in range(2):
@@ -348,6 +348,7 @@
         for at in range(8):
             blocks_ref[8 * half + at, 0:8] = tiles[at]
             blocks_ref[8 * half + at, 8:16] = energy
+    put_own(place_ref[0], state, own_ref)
 
 
 def assembled(knots):
@@ -417,8 +418,7 @@
 OWN = ((152, 128), f32)
 
 
-def own_kernel(place_ref, state, own_ref):
-    place = place_ref[0]
+def put_own(place, state, own_ref):
     lane_place = lax.broadcasted_iota(jnp.int32, (8, 128), 1) >> 4
     for at, lanes in enumerate((START, MAPPED, RESIDUAL)):
         result = jnp.zeros((8, 128), f32)
@@ -577,10 +577,15 @@
     parts = sky_parts(knots)
     sums, work, state = call(next_kernel, "next", [SUMS, WORK, STATE], tm, *parts, work, state, **kept)
     parts = tm_parts(sums)
-    blocks, work, state = call(
-        back_to_owners_kernel, "back_to_owners", [((16, 16, 128), f32), WORK, STATE], tm, *parts, work, state, **kept
-    )
-    (own,) = call(own_kernel, "own", [OWN], place, state, scalars=1)
+    blocks, own, work, state = call(
+        back_to_owners_kernel,
+        "back_to_owners",
+        [((16, 16, 128), f32), OWN, WORK, STATE],
+        tm, place, *parts, work, state,
+        scalars=2,
+        aliases={6: 2, 7: 3},
+    )
+    blocks, own = lax.optimization_barrier((blocks, own))
     blocks = lax.all_to_all(blocks, SKY, 0, 0, tiled=True)
     return call(
         last_kernel,

time: 88.7 us -> 87.1 us (0.982)
  blocking collectives: 0 us -> 10.6 us
  waiting for transfers between devices: 44.1 us -> 36.3 us
  starting transfers between devices: 31.3 us -> 27.8 us
    all_to_all x0 -> x1, blocking collectives: none -> 10.6 us  [shards(): blocks = lax.all_to_all(blocks, SKY, 0, 0, tiled=True)]
    all_to_all x1 -> x0, waiting for transfers between devices: 7.77 us -> none  [shards(): blocks = lax.all_to_all(blocks, SKY, 0, 0, tiled=True)]
    all_to_all x1 -> x0, starting transfers between devices: 3.51 us -> none  [shards(): blocks = lax.all_to_all(blocks, SKY, 0, 0, tiled=True)]
    pallas_call x11 -> x10, Pallas kernels: 11.2 us -> 10.4 us  [call(): pl.pallas_call(kernel, out_shape=shapes, in_specs=specs, out_specs=[VMEM]...]
  transfers between devices with their start and end apart: 26 -> 25, of which waited for: 20 -> 19; matrix products, arithmetic and copies ran while one was open for 0% -> 0% of each run, Pallas kernels for 2% -> 2%
where the time goes in v7:
time: 87.1 us; the launch traced here: 86.9 us
  waiting for transfers between devices  36.3 us (42%)
  starting transfers between devices  27.8 us (32%)
  blocking collectives  10.6 us (12%)
  Pallas kernels  10.4 us (12%)
  between operations  1.56 us (2%)
    ppermute x18, waiting for transfers between devices, ring_parts(): lax.ppermute(value, axis, [(at, (at + step) % count) for at in range(coun...  28.4 us
    ppermute x18, starting transfers between devices, ring_parts(): lax.ppermute(value, axis, [(at, (at + step) % count) for at in range(coun...  21.6 us
    all_to_all x1, blocking collectives, shards(): blocks = lax.all_to_all(blocks, SKY, 0, 0, tiled=True)  10.6 us
    pallas_call x10, Pallas kernels, call(): pl.pallas_call(kernel, out_shape=shapes, in_specs=specs, out_specs=[VMEM]...  10.4 us
    ppermute x2, starting transfers between devices, crossing(): return lax.ppermute(value, TM, pairs)  4.26 us
    ppermute x1, waiting for transfers between devices, shards(): lax.ppermute(sums, 'tm_0', [(at, (at + 2) % 4) for at in range(4)])  4.07 us
    ppermute x4, waiting for transfers between devices, to_twin(): return lax.ppermute(value, 'tm_1', [(0, 1), (1, 0)])  2.89 us
  transfers between devices with their start and end apart: 25, of which 19 were waited for; matrix products, arithmetic and copies ran while one was open for 0% of the time, Pallas kernels for 2%

profile of v7, /device:TPU:0, one launch (start us, length us, event | category | flops | bytes accessed | tf_op | source)
XLA Modules:
  0.0 86.9 jit_solution(13273623181303041156)
XLA Ops:
  1.5 1.2 %source_sums.1 = (f32[128,4096]{1,0:T(8,128)S(1)}, f32[160,128]{1,0:T(8,128)S(1)}, f32[80,1408]{1,0:T(8,128)S(1)}) custom-call(s32[1]{0:T(128)S(6)} %copy.35.count_ref, s32[1]{0:T(128)} %bitcast.2.first_ref, s32[1,4096]{1,0:T(1,128)S(1)} %bitcast.14, f32[5,4096]{1,0:T(8,128)S(1)} %copy-done, ...), custom_call_target="tpu_custom_call", output_to_operand_aliasing={{2}: (6, {})} | custom-call | tf_op jit(solution)/shard_map/source_sums/pallas_call | solution.py:484
  2.9 1.5 %ghosts.1 = (f32[32,128]{1,0:T(8,128)S(1)}, f32[32,128]{1,0:T(8,128)S(1)}, f32[32,128]{1,0:T(8,128)S(1)}) custom-call(s32[1]{0:T(128)S(6)} %copy.35.count_ref, s32[1]{0:T(128)} %bitcast.tm_ref, s32[32,128]{1,0:T(8,128)S(1)} %bitcast.9, s32[1,4096]{1,0:T(1,128)S(1)} %bitcast.10, s32[1,4096]{1,0:T(1,128)S(1)} %bitcast.15, f32[5,4096]{1,0:T(8,128)S(1)} %copy-done, ...), custom_call_target="tpu_custom_call" | custom-call | tf_op jit(solution)/shard_map/ghosts/pallas_call | solution.py:484
  4.5 4.3 %collective-permute-start.2 = (f32[192,128]{1,0:T(8,128)S(1)}, f32[192,128]{1,0:T(8,128)S(1)}, u32[]{:S(2)}, u32[]{:S(2)}) collective-permute-start(f32[192,128]{1,0:T(8,128)S(1)} %get-tuple-element.47), channel_id=1, source_target_pairs={{0,7},{1,6},{2,1},{3,0},{4,3},{5,2},{6,5},{7,4},{8,15},{9,14},{10,... | collective-permute-start | bytes 294920 | tf_op jit(solution)/shard_map/ppermute | solution.py:506
  8.8 1.5 %collective-permute-start.3 = (f32[160,128]{1,0:T(8,128)S(1)}, f32[160,128]{1,0:T(8,128)S(1)}, u32[]{:S(2)}, u32[]{:S(2)}) collective-permute-start(f32[160,128]{1,0:T(8,128)S(1)} %add.35), channel_id=1, source_target_pairs={{0,4},{2,6},{4,0},{6,2},{1,5},{3,7},{5,1},{7,3},{8,12},{10,14},{12... | collective-permute-start | bytes 245768 | tf_op jit(solution)/shard_map/ppermute | solution.py:558
  11.5 4.1 %collective-permute-done.3.two = f32[160,128]{1,0:T(8,128)S(1)} collective-permute-done((f32[160,128]{1,0:T(8,128)S(1)}, f32[160,128]{1,0:T(8,128)S(1)}, u32[]{:S(2)}, u32[]{:S(2)}) %collective-permute-start.3) | collective-permute-done | bytes 81952 | tf_op jit(solution)/shard_map/ppermute | solution.py:558
  16.6 1.3 %first.1 = (f32[72,256]{1,0:T(8,128)S(1)}, f32[128,4096]{1,0:T(8,128)S(1)}, f32[80,1408]{1,0:T(8,128)S(1)}) custom-call(s32[1]{0:T(128)} %bitcast.tm_ref, f32[192,128]{1,0:T(8,128)S(1)} %get-tuple-element.48.own, f32[192,128]{1,0:T(8,128)S(1)} %collective-permute-done.1.one, ...), custom_call_target="tpu_custom_call", output_to_operand_aliasing={{1}: (6, {}), {2}: (7, {})} | custom-call | tf_op jit(solution)/shard_map/first/pallas_call | solution.py:484
  17.9 3.1 %collective-permute-start.7 = (f32[72,256]{1,0:T(8,128)S(1)}, f32[72,256]{1,0:T(8,128)S(1)}, u32[]{:S(2)}, u32[]{:S(2)}) collective-permute-start(f32[72,256]{1,0:T(8,128)S(1)} %get-tuple-element.31), channel_id=1, source_target_pairs={{0,16},{8,24},{16,0},{24,8},{1,17},{9,25},{17,1},{25,9},{2,18},{10... | collective-permute-start | bytes 221192 | tf_op jit(solution)/shard_map/ppermute | solution.py:499
  23.8 1.7 %collective-permute-done.6 = f32[72,256]{1,0:T(8,128)S(1)} collective-permute-done((f32[72,256]{1,0:T(8,128)S(1)}, f32[72,256]{1,0:T(8,128)S(1)}, u32[]{:S(2)}, u32[]{:S(2)}) %collective-permute-start.6) | collective-permute-done | bytes 73760 | tf_op jit(solution)/shard_map/ppermute | solution.py:499
  25.4 2.2 %collective-permute-done.5 = f32[72,256]{1,0:T(8,128)S(1)} collective-permute-done((f32[72,256]{1,0:T(8,128)S(1)}, f32[72,256]{1,0:T(8,128)S(1)}, u32[]{:S(2)}, u32[]{:S(2)}) %collective-permute-start.5) | collective-permute-done | bytes 73760 | tf_op jit(solution)/shard_map/ppermute | solution.py:499
  27.7 3.3 %collective-permute-start.10 = (f32[72,256]{1,0:T(8,128)S(1)}, f32[72,256]{1,0:T(8,128)S(1)}, u32[]{:S(2)}, u32[]{:S(2)}) collective-permute-start(f32[72,256]{1,0:T(8,128)S(1)} %add_add_fusion.1.own), channel_id=1, source_target_pairs={{0,64},{32,96},{64,0},{96,32},{1,65},{33,97},{65,1},{97,33},{2,66}... | collective-permute-start | bytes 221192 | tf_op jit(solution)/shard_map/ppermute | solution.py:499
  34.0 1.3 %collective-permute-done.9.three = f32[72,256]{1,0:T(8,128)S(1)} collective-permute-done((f32[72,256]{1,0:T(8,128)S(1)}, f32[72,256]{1,0:T(8,128)S(1)}, u32[]{:S(2)}, u32[]{:S(2)}) %collective-permute-start.9) | collective-permute-done | bytes 73760 | tf_op jit(solution)/shard_map/ppermute | solution.py:499
  35.3 2.3 %collective-permute-done.8.one = f32[72,256]{1,0:T(8,128)S(1)} collective-permute-done((f32[72,256]{1,0:T(8,128)S(1)}, f32[72,256]{1,0:T(8,128)S(1)}, u32[]{:S(2)}, u32[]{:S(2)}) %collective-permute-start.8) | collective-permute-done | bytes 73760 | tf_op jit(solution)/shard_map/ppermute | solution.py:499
  37.5 1.2 %start.1 = (f32[56,128]{1,0:T(8,128)S(1)}, f32[128,4096]{1,0:T(8,128)S(1)}, f32[80,1408]{1,0:T(8,128)S(1)}) custom-call(s32[1]{0:T(128)} %bitcast.tm_ref, f32[72,256]{1,0:T(8,128)S(1)} %add_add_fusion.1.own, f32[72,256]{1,0:T(8,128)S(1)} %collective-permute-done.8.one, ...), custom_call_target="tpu_custom_call", output_to_operand_aliasing={{1}: (5, {}), {2}: (6, {})} | custom-call | tf_op jit(solution)/shard_map/start/pallas_call | solution.py:484
  38.9 1.2 %collective-permute-done.11 = f32[56,128]{1,0:T(8,128)S(1)} collective-permute-done((f32[56,128]{1,0:T(8,128)S(1)}, f32[56,128]{1,0:T(8,128)S(1)}, u32[]{:S(2)}, u32[]{:S(2)}) %collective-permute-start.11) | collective-permute-done | bytes 28704 | tf_op jit(solution)/shard_map/ppermute | solution.py:510
  40.5 1.2 %collective-permute-start.13 = (f32[56,128]{1,0:T(8,128)S(1)}, f32[56,128]{1,0:T(8,128)S(1)}, u32[]{:S(2)}, u32[]{:S(2)}) collective-permute-start(f32[56,128]{1,0:T(8,128)S(1)} %add.39.own), channel_id=1, source_target_pairs={{0,6},{2,0},{4,2},{6,4},{1,7},{3,1},{5,3},{7,5},{8,14},{10,8},{12,... | collective-permute-start | bytes 86024 | tf_op jit(solution)/shard_map/ppermute | solution.py:499
  42.5 2.9 %collective-permute-done.14.two = f32[56,128]{1,0:T(8,128)S(1)} collective-permute-done((f32[56,128]{1,0:T(8,128)S(1)}, f32[56,128]{1,0:T(8,128)S(1)}, u32[]{:S(2)}, u32[]{:S(2)}) %collective-permute-start.14) | collective-permute-done | bytes 28704 | tf_op jit(solution)/shard_map/ppermute | solution.py:499
  45.4 1.3 %collective-permute-done.12.one = f32[56,128]{1,0:T(8,128)S(1)} collective-permute-done((f32[56,128]{1,0:T(8,128)S(1)}, f32[56,128]{1,0:T(8,128)S(1)}, u32[]{:S(2)}, u32[]{:S(2)}) %collective-permute-start.12) | collective-permute-done | bytes 28704 | tf_op jit(solution)/shard_map/ppermute | solution.py:499
  46.8 1.2 %back.1 = (f32[72,256]{1,0:T(8,128)S(1)}, f32[128,4096]{1,0:T(8,128)S(1)}, f32[80,1408]{1,0:T(8,128)S(1)}) custom-call(s32[1]{0:T(128)} %bitcast.tm_ref, f32[56,128]{1,0:T(8,128)S(1)} %add.39.own, f32[56,128]{1,0:T(8,128)S(1)} %collective-permute-done.12.one, ...), custom_call_target="tpu_custom_call", output_to_operand_aliasing={{1}: (5, {}), {2}: (6, {})} | custom-call | tf_op jit(solution)/shard_map/back/pallas_call | solution.py:484
  48.4 1.9 %collective-permute-start.16 = (f32[72,256]{1,0:T(8,128)S(1)}, f32[72,256]{1,0:T(8,128)S(1)}, u32[]{:S(2)}, u32[]{:S(2)}) collective-permute-start(f32[72,256]{1,0:T(8,128)S(1)} %get-tuple-element.37), channel_id=1, source_target_pairs={{0,24},{8,0},{16,8},{24,16},{1,25},{9,1},{17,9},{25,17},{2,26},{10... | collective-permute-start | bytes 221192 | tf_op jit(solution)/shard_map/ppermute | solution.py:499
  50.5 3.4 %collective-permute-done.17 = f32[72,256]{1,0:T(8,128)S(1)} collective-permute-done((f32[72,256]{1,0:T(8,128)S(1)}, f32[72,256]{1,0:T(8,128)S(1)}, u32[]{:S(2)}, u32[]{:S(2)}) %collective-permute-start.17) | collective-permute-done | bytes 73760 | tf_op jit(solution)/shard_map/ppermute | solution.py:499
  53.9 2.0 %collective-permute-done.15 = f32[72,256]{1,0:T(8,128)S(1)} collective-permute-done((f32[72,256]{1,0:T(8,128)S(1)}, f32[72,256]{1,0:T(8,128)S(1)}, u32[]{:S(2)}, u32[]{:S(2)}) %collective-permute-start.15) | collective-permute-done | bytes 73760 | tf_op jit(solution)/shard_map/ppermute | solution.py:499
  56.6 2.0 %collective-permute-start.19 = (f32[72,256]{1,0:T(8,128)S(1)}, f32[72,256]{1,0:T(8,128)S(1)}, u32[]{:S(2)}, u32[]{:S(2)}) collective-permute-start(f32[72,256]{1,0:T(8,128)S(1)} %add_add_fusion.own), channel_id=1, source_target_pairs={{0,96},{32,0},{64,32},{96,64},{1,97},{33,1},{65,33},{97,65},{2,98}... | collective-permute-start | bytes 221192 | tf_op jit(solution)/shard_map/ppermute | solution.py:499
  58.7 3.4 %collective-permute-done.20.two = f32[72,256]{1,0:T(8,128)S(1)} collective-permute-done((f32[72,256]{1,0:T(8,128)S(1)}, f32[72,256]{1,0:T(8,128)S(1)}, u32[]{:S(2)}, u32[]{:S(2)}) %collective-permute-start.20) | collective-permute-done | bytes 73760 | tf_op jit(solution)/shard_map/ppermute | solution.py:499
  62.0 2.1 %collective-permute-done.18.one = f32[72,256]{1,0:T(8,128)S(1)} collective-permute-done((f32[72,256]{1,0:T(8,128)S(1)}, f32[72,256]{1,0:T(8,128)S(1)}, u32[]{:S(2)}, u32[]{:S(2)}) %collective-permute-start.18) | collective-permute-done | bytes 73760 | tf_op jit(solution)/shard_map/ppermute | solution.py:499
  64.2 1.3 %next.1 = (f32[56,128]{1,0:T(8,128)S(1)}, f32[128,4096]{1,0:T(8,128)S(1)}, f32[80,1408]{1,0:T(8,128)S(1)}) custom-call(s32[1]{0:T(128)} %bitcast.tm_ref, f32[72,256]{1,0:T(8,128)S(1)} %add_add_fusion.own, f32[72,256]{1,0:T(8,128)S(1)} %collective-permute-done.18.one, ...), custom_call_target="tpu_custom_call", output_to_operand_aliasing={{1}: (5, {}), {2}: (6, {})} | custom-call | tf_op jit(solution)/shard_map/next/pallas_call | solution.py:484
  65.5 1.2 %collective-permute-done.21 = f32[56,128]{1,0:T(8,128)S(1)} collective-permute-done((f32[56,128]{1,0:T(8,128)S(1)}, f32[56,128]{1,0:T(8,128)S(1)}, u32[]{:S(2)}, u32[]{:S(2)}) %collective-permute-start.21) | collective-permute-done | bytes 28704 | tf_op jit(solution)/shard_map/ppermute | solution.py:510
  66.7 1.4 %collective-permute-start.24 = (f32[56,128]{1,0:T(8,128)S(1)}, f32[56,128]{1,0:T(8,128)S(1)}, u32[]{:S(2)}, u32[]{:S(2)}) collective-permute-start(f32[56,128]{1,0:T(8,128)S(1)} %add.43.own), channel_id=1, source_target_pairs={{0,4},{2,6},{4,0},{6,2},{1,5},{3,7},{5,1},{7,3},{8,12},{10,14},{12... | collective-permute-start | bytes 86024 | tf_op jit(solution)/shard_map/ppermute | solution.py:499
  69.0 1.2 %collective-permute-start.22 = (f32[56,128]{1,0:T(8,128)S(1)}, f32[56,128]{1,0:T(8,128)S(1)}, u32[]{:S(2)}, u32[]{:S(2)}) collective-permute-start(f32[56,128]{1,0:T(8,128)S(1)} %add.43.own), channel_id=1, source_target_pairs={{0,2},{2,4},{4,6},{6,0},{1,3},{3,5},{5,7},{7,1},{8,10},{10,12},{12... | collective-permute-start | bytes 86024 | tf_op jit(solution)/shard_map/ppermute | solution.py:499
  70.2 1.9 %collective-permute-done.24.two = f32[56,128]{1,0:T(8,128)S(1)} collective-permute-done((f32[56,128]{1,0:T(8,128)S(1)}, f32[56,128]{1,0:T(8,128)S(1)}, u32[]{:S(2)}, u32[]{:S(2)}) %collective-permute-start.24) | collective-permute-done | bytes 28704 | tf_op jit(solution)/shard_map/ppermute | solution.py:499
  72.1 2.0 %collective-permute-done.22.one = f32[56,128]{1,0:T(8,128)S(1)} collective-permute-done((f32[56,128]{1,0:T(8,128)S(1)}, f32[56,128]{1,0:T(8,128)S(1)}, u32[]{:S(2)}, u32[]{:S(2)}) %collective-permute-start.22) | collective-permute-done | bytes 28704 | tf_op jit(solution)/shard_map/ppermute | solution.py:499
  74.1 1.4 %back_to_owners.1 = (f32[16,16,128]{2,1,0:T(8,128)S(1)}, f32[152,128]{1,0:T(8,128)S(1)}, f32[128,4096]{1,0:T(8,128)S(1)}, f32[80,1408]{1,0:T(8,128)S(1)}) custom-call(s32[1]{0:T(128)} %bitcast.tm_ref, s32[1]{0:T(128)} %bitcast.1.place_ref, f32[56,128]{1,0:T(8,128)S(1)} %add.43.own, ...), custom_call_target="tpu_custom_call", output_to_operand_aliasing={{2}: (6, {}), {3}: (7, {})} | custom-call | tf_op jit(solution)/shard_map/back_to_owners/pallas_call | solution.py:484
  75.5 10.6 %all_to_all.5.blocks_ref = f32[16,16,128]{2,1,0:T(8,128)S(1)} all-to-all(f32[16,16,128]{2,1,0:T(8,128)S(1)} %get-tuple-element.45), channel_id=1, replica_groups=mesh['sky_0'=4,'sky_1'=4,'tm_0'=4,'tm_1'=2] {'sky_0','sky_1'}, dimensions={0} | all-to-all | bytes 262144 | tf_op jit(solution)/shard_map/all_to_all | solution.py:589
  (49 shorter events, 13.1 us)
Async XLA Ops:
  0.6 0.9 %copy-start = (f32[5,4096]{1,0:T(8,128)S(1)}, f32[5,4096]{1,0:T(8,128)}, u32[]{:S(2)}) copy-start(f32[5,4096]{1,0:T(8,128)} %g_ref.3) | copy-start | bytes 245764
  0.6 0.9 %copy-start.4 = (s32[4096]{0:T(1024)S(1)}, s32[4096]{0:T(1024)}, u32[]{:S(2)}) copy-start(s32[4096]{0:T(1024)} %param.8) | copy-start | bytes 49156
  0.7 0.9 %copy-start.5 = (f32[5,1024]{1,0:T(8,128)S(1)}, f32[5,1024]{1,0:T(8,128)}, u32[]{:S(2)}) copy-start(f32[5,1024]{1,0:T(8,128)} %prior_ref.1) | copy-start | bytes 61444
  0.7 0.9 %copy-start.6 = (f32[4096]{0:T(1024)S(1)}, f32[4096]{0:T(1024)}, u32[]{:S(2)}) copy-start(f32[4096]{0:T(1024)} %param.14) | copy-start | bytes 49156
  0.7 2.2 %copy-start.1 = (f32[4,4096]{1,0:T(4,128)S(1)}, f32[4,4096]{1,0:T(4,128)}, u32[]{:S(2)}) copy-start(f32[4,4096]{1,0:T(4,128)} %h_ref.3) | copy-start | bytes 196612
  0.7 2.2 %copy-start.2 = (s32[4096]{0:T(1024)S(1)}, s32[4096]{0:T(1024)}, u32[]{:S(2)}) copy-start(s32[4096]{0:T(1024)} %param.9) | copy-start | bytes 49156
  0.7 2.2 %copy-start.3 = (f32[4096]{0:T(1024)S(1)}, f32[4096]{0:T(1024)}, u32[]{:S(2)}) copy-start(f32[4096]{0:T(1024)} %param.13) | copy-start | bytes 49156
  2.8 1.6 %collective-permute-start = (f32[160,128]{1,0:T(8,128)S(1)}, f32[160,128]{1,0:T(8,128)S(1)}, u32[]{:S(2)}, u32[]{:S(2)}) collective-permute-start(f32[160,128]{1,0:T(8,128)S(1)} %get-tuple-element.25), channel_id=1, source_target_pairs={{0,1},{1,0},{2,3},{3,2},{4,5},{5,4},{6,7},{7,6},{8,9},{9,8},{10,11... | collective-permute-start | bytes 245768 | tf_op jit(solution)/shard_map/ppermute | solution.py:510
  4.5 11.1 %collective-permute-start.2 = (f32[192,128]{1,0:T(8,128)S(1)}, f32[192,128]{1,0:T(8,128)S(1)}, u32[]{:S(2)}, u32[]{:S(2)}) collective-permute-start(f32[192,128]{1,0:T(8,128)S(1)} %get-tuple-element.47), channel_id=1, source_target_pairs={{0,7},{1,6},{2,1},{3,0},{4,3},{5,2},{6,5},{7,4},{8,15},{9,14},{10,... | collective-permute-start | bytes 294920 | tf_op jit(solution)/shard_map/ppermute | solution.py:506
  8.8 7.8 %collective-permute-start.1 = (f32[192,128]{1,0:T(8,128)S(1)}, f32[192,128]{1,0:T(8,128)S(1)}, u32[]{:S(2)}, u32[]{:S(2)}) collective-permute-start(f32[192,128]{1,0:T(8,128)S(1)} %get-tuple-element.48.own), channel_id=1, source_target_pairs={{0,3},{1,2},{2,5},{3,4},{4,7},{5,6},{6,1},{7,0},{8,11},{9,10},{10,... | collective-permute-start | bytes 294920 | tf_op jit(solution)/shard_map/ppermute | solution.py:506
  8.8 6.8 %collective-permute-start.3 = (f32[160,128]{1,0:T(8,128)S(1)}, f32[160,128]{1,0:T(8,128)S(1)}, u32[]{:S(2)}, u32[]{:S(2)}) collective-permute-start(f32[160,128]{1,0:T(8,128)S(1)} %add.35), channel_id=1, source_target_pairs={{0,4},{2,6},{4,0},{6,2},{1,5},{3,7},{5,1},{7,3},{8,12},{10,14},{12... | collective-permute-start | bytes 245768 | tf_op jit(solution)/shard_map/ppermute | solution.py:558
  10.3 1.2 %collective-permute-start.4 = (f32[32,128]{1,0:T(8,128)S(1)}, f32[32,128]{1,0:T(8,128)S(1)}, u32[]{:S(2)}, u32[]{:S(2)}) collective-permute-start(f32[32,128]{1,0:T(8,128)S(1)} %get-tuple-element.29), channel_id=1, source_target_pairs={{0,1},{1,0},{2,3},{3,2},{4,5},{5,4},{6,7},{7,6},{8,9},{9,8},{10,11... | collective-permute-start | bytes 49160 | tf_op jit(solution)/shard_map/ppermute | solution.py:510
  17.9 5.9 %collective-permute-start.7 = (f32[72,256]{1,0:T(8,128)S(1)}, f32[72,256]{1,0:T(8,128)S(1)}, u32[]{:S(2)}, u32[]{:S(2)}) collective-permute-start(f32[72,256]{1,0:T(8,128)S(1)} %get-tuple-element.31), channel_id=1, source_target_pairs={{0,16},{8,24},{16,0},{24,8},{1,17},{9,25},{17,1},{25,9},{2,18},{10... | collective-permute-start | bytes 221192 | tf_op jit(solution)/shard_map/ppermute | solution.py:499
  20.9 4.5 %collective-permute-start.6 = (f32[72,256]{1,0:T(8,128)S(1)}, f32[72,256]{1,0:T(8,128)S(1)}, u32[]{:S(2)}, u32[]{:S(2)}) collective-permute-start(f32[72,256]{1,0:T(8,128)S(1)} %get-tuple-element.31), channel_id=1, source_target_pairs={{0,24},{8,0},{16,8},{24,16},{1,25},{9,1},{17,9},{25,17},{2,26},{10... | collective-permute-start | bytes 221192 | tf_op jit(solution)/shard_map/ppermute | solution.py:499
  22.1 5.6 %collective-permute-start.5 = (f32[72,256]{1,0:T(8,128)S(1)}, f32[72,256]{1,0:T(8,128)S(1)}, u32[]{:S(2)}, u32[]{:S(2)}) collective-permute-start(f32[72,256]{1,0:T(8,128)S(1)} %get-tuple-element.31), channel_id=1, source_target_pairs={{0,8},{8,16},{16,24},{24,0},{1,9},{9,17},{17,25},{25,1},{2,10},{10... | collective-permute-start | bytes 221192 | tf_op jit(solution)/shard_map/ppermute | solution.py:499
  27.7 6.3 %collective-permute-start.10 = (f32[72,256]{1,0:T(8,128)S(1)}, f32[72,256]{1,0:T(8,128)S(1)}, u32[]{:S(2)}, u32[]{:S(2)}) collective-permute-start(f32[72,256]{1,0:T(8,128)S(1)} %add_add_fusion.1.own), channel_id=1, source_target_pairs={{0,64},{32,96},{64,0},{96,32},{1,65},{33,97},{65,1},{97,33},{2,66}... | collective-permute-start | bytes 221192 | tf_op jit(solution)/shard_map/ppermute | solution.py:499
  30.9 4.4 %collective-permute-start.9 = (f32[72,256]{1,0:T(8,128)S(1)}, f32[72,256]{1,0:T(8,128)S(1)}, u32[]{:S(2)}, u32[]{:S(2)}) collective-permute-start(f32[72,256]{1,0:T(8,128)S(1)} %add_add_fusion.1.own), channel_id=1, source_target_pairs={{0,96},{32,0},{64,32},{96,64},{1,97},{33,1},{65,33},{97,65},{2,98}... | collective-permute-start | bytes 221192 | tf_op jit(solution)/shard_map/ppermute | solution.py:499
  32.0 5.6 %collective-permute-start.8 = (f32[72,256]{1,0:T(8,128)S(1)}, f32[72,256]{1,0:T(8,128)S(1)}, u32[]{:S(2)}, u32[]{:S(2)}) collective-permute-start(f32[72,256]{1,0:T(8,128)S(1)} %add_add_fusion.1.own), channel_id=1, source_target_pairs={{0,32},{32,64},{64,96},{96,0},{1,33},{33,65},{65,97},{97,1},{2,34}... | collective-permute-start | bytes 221192 | tf_op jit(solution)/shard_map/ppermute | solution.py:499
  38.8 1.3 %collective-permute-start.11 = (f32[56,128]{1,0:T(8,128)S(1)}, f32[56,128]{1,0:T(8,128)S(1)}, u32[]{:S(2)}, u32[]{:S(2)}) collective-permute-start(f32[56,128]{1,0:T(8,128)S(1)} %get-tuple-element.34), channel_id=1, source_target_pairs={{0,1},{1,0},{2,3},{3,2},{4,5},{5,4},{6,7},{7,6},{8,9},{9,8},{10,11... | collective-permute-start | bytes 86024 | tf_op jit(solution)/shard_map/ppermute | solution.py:510
  40.0 5.4 %collective-permute-start.14 = (f32[56,128]{1,0:T(8,128)S(1)}, f32[56,128]{1,0:T(8,128)S(1)}, u32[]{:S(2)}, u32[]{:S(2)}) collective-permute-start(f32[56,128]{1,0:T(8,128)S(1)} %add.39.own), channel_id=1, source_target_pairs={{0,4},{2,6},{4,0},{6,2},{1,5},{3,7},{5,1},{7,3},{8,12},{10,14},{12... | collective-permute-start | bytes 86024 | tf_op jit(solution)/shard_map/ppermute | solution.py:499
  40.5 5.0 %collective-permute-start.13 = (f32[56,128]{1,0:T(8,128)S(1)}, f32[56,128]{1,0:T(8,128)S(1)}, u32[]{:S(2)}, u32[]{:S(2)}) collective-permute-start(f32[56,128]{1,0:T(8,128)S(1)} %add.39.own), channel_id=1, source_target_pairs={{0,6},{2,0},{4,2},{6,4},{1,7},{3,1},{5,3},{7,5},{8,14},{10,8},{12,... | collective-permute-start | bytes 86024 | tf_op jit(solution)/shard_map/ppermute | solution.py:499
  41.7 5.1 %collective-permute-start.12 = (f32[56,128]{1,0:T(8,128)S(1)}, f32[56,128]{1,0:T(8,128)S(1)}, u32[]{:S(2)}, u32[]{:S(2)}) collective-permute-start(f32[56,128]{1,0:T(8,128)S(1)} %add.39.own), channel_id=1, source_target_pairs={{0,2},{2,4},{4,6},{6,0},{1,3},{3,5},{5,7},{7,1},{8,10},{10,12},{12... | collective-permute-start | bytes 86024 | tf_op jit(solution)/shard_map/ppermute | solution.py:499
  47.9 6.0 %collective-permute-start.17 = (f32[72,256]{1,0:T(8,128)S(1)}, f32[72,256]{1,0:T(8,128)S(1)}, u32[]{:S(2)}, u32[]{:S(2)}) collective-permute-start(f32[72,256]{1,0:T(8,128)S(1)} %get-tuple-element.37), channel_id=1, source_target_pairs={{0,16},{8,24},{16,0},{24,8},{1,17},{9,25},{17,1},{25,9},{2,18},{10... | collective-permute-start | bytes 221192 | tf_op jit(solution)/shard_map/ppermute | solution.py:499
  48.4 5.5 %collective-permute-start.16 = (f32[72,256]{1,0:T(8,128)S(1)}, f32[72,256]{1,0:T(8,128)S(1)}, u32[]{:S(2)}, u32[]{:S(2)}) collective-permute-start(f32[72,256]{1,0:T(8,128)S(1)} %get-tuple-element.37), channel_id=1, source_target_pairs={{0,24},{8,0},{16,8},{24,16},{1,25},{9,1},{17,9},{25,17},{2,26},{10... | collective-permute-start | bytes 221192 | tf_op jit(solution)/shard_map/ppermute | solution.py:499
  50.3 5.6 %collective-permute-start.15 = (f32[72,256]{1,0:T(8,128)S(1)}, f32[72,256]{1,0:T(8,128)S(1)}, u32[]{:S(2)}, u32[]{:S(2)}) collective-permute-start(f32[72,256]{1,0:T(8,128)S(1)} %get-tuple-element.37), channel_id=1, source_target_pairs={{0,8},{8,16},{16,24},{24,0},{1,9},{9,17},{17,25},{25,1},{2,10},{10... | collective-permute-start | bytes 221192 | tf_op jit(solution)/shard_map/ppermute | solution.py:499
  55.9 6.1 %collective-permute-start.20 = (f32[72,256]{1,0:T(8,128)S(1)}, f32[72,256]{1,0:T(8,128)S(1)}, u32[]{:S(2)}, u32[]{:S(2)}) collective-permute-start(f32[72,256]{1,0:T(8,128)S(1)} %add_add_fusion.own), channel_id=1, source_target_pairs={{0,64},{32,96},{64,0},{96,32},{1,65},{33,97},{65,1},{97,33},{2,66}... | collective-permute-start | bytes 221192 | tf_op jit(solution)/shard_map/ppermute | solution.py:499
  56.6 5.4 %collective-permute-start.19 = (f32[72,256]{1,0:T(8,128)S(1)}, f32[72,256]{1,0:T(8,128)S(1)}, u32[]{:S(2)}, u32[]{:S(2)}) collective-permute-start(f32[72,256]{1,0:T(8,128)S(1)} %add_add_fusion.own), channel_id=1, source_target_pairs={{0,96},{32,0},{64,32},{96,64},{1,97},{33,1},{65,33},{97,65},{2,98}... | collective-permute-start | bytes 221192 | tf_op jit(solution)/shard_map/ppermute | solution.py:499
  58.6 5.6 %collective-permute-start.18 = (f32[72,256]{1,0:T(8,128)S(1)}, f32[72,256]{1,0:T(8,128)S(1)}, u32[]{:S(2)}, u32[]{:S(2)}) collective-permute-start(f32[72,256]{1,0:T(8,128)S(1)} %add_add_fusion.own), channel_id=1, source_target_pairs={{0,32},{32,64},{64,96},{96,0},{1,33},{33,65},{65,97},{97,1},{2,34}... | collective-permute-start | bytes 221192 | tf_op jit(solution)/shard_map/ppermute | solution.py:499
  65.4 1.3 %collective-permute-start.21 = (f32[56,128]{1,0:T(8,128)S(1)}, f32[56,128]{1,0:T(8,128)S(1)}, u32[]{:S(2)}, u32[]{:S(2)}) collective-permute-start(f32[56,128]{1,0:T(8,128)S(1)} %get-tuple-element.40), channel_id=1, source_target_pairs={{0,1},{1,0},{2,3},{3,2},{4,5},{5,4},{6,7},{7,6},{8,9},{9,8},{10,11... | collective-permute-start | bytes 86024 | tf_op jit(solution)/shard_map/ppermute | solution.py:510
  66.7 5.4 %collective-permute-start.24 = (f32[56,128]{1,0:T(8,128)S(1)}, f32[56,128]{1,0:T(8,128)S(1)}, u32[]{:S(2)}, u32[]{:S(2)}) collective-permute-start(f32[56,128]{1,0:T(8,128)S(1)} %add.43.own), channel_id=1, source_target_pairs={{0,4},{2,6},{4,0},{6,2},{1,5},{3,7},{5,1},{7,3},{8,12},{10,14},{12... | collective-permute-start | bytes 86024 | tf_op jit(solution)/shard_map/ppermute | solution.py:499
  68.1 3.9 %collective-permute-start.23 = (f32[56,128]{1,0:T(8,128)S(1)}, f32[56,128]{1,0:T(8,128)S(1)}, u32[]{:S(2)}, u32[]{:S(2)}) collective-permute-start(f32[56,128]{1,0:T(8,128)S(1)} %add.43.own), channel_id=1, source_target_pairs={{0,6},{2,0},{4,2},{6,4},{1,7},{3,1},{5,3},{7,5},{8,14},{10,8},{12,... | collective-permute-start | bytes 86024 | tf_op jit(solution)/shard_map/ppermute | solution.py:499
  69.0 5.1 %collective-permute-start.22 = (f32[56,128]{1,0:T(8,128)S(1)}, f32[56,128]{1,0:T(8,128)S(1)}, u32[]{:S(2)}, u32[]{:S(2)}) collective-permute-start(f32[56,128]{1,0:T(8,128)S(1)} %add.43.own), channel_id=1, source_target_pairs={{0,2},{2,4},{4,6},{6,0},{1,3},{3,5},{5,7},{7,1},{8,10},{10,12},{12... | collective-permute-start | bytes 86024 | tf_op jit(solution)/shard_map/ppermute | solution.py:499
